TPU v7x, 32 devices: a whole 2x2x4 slice. The times are simulated.
32 devices in a mesh: dp: 4 (over y, x), fsdp: 8 (over z, core).
Axes of the slice: x: 2, y: 2, z: 4, core: 2. Of those that a mesh axis runs over, the one named last changes fastest.
Arguments:
- features: bfloat16 [1152, 49, 2048], P(('dp', 'fsdp')), may hold values from -16 to 16
- grid_size: int32 [1152], P(('dp', 'fsdp')), may hold values from 2 to 7, as said below
- w_reduce: bfloat16 [2, 2048, 512], P(None, 'fsdp'), may hold values from -0.125 to 0.125
- w_spatial: bfloat16 [2, 4608, 512], P(None, 'fsdp'), may hold values from -0.09375 to 0.09375
- w_expand: bfloat16 [2, 512, 2048], P(None, 'fsdp'), may hold values from -0.25 to 0.25
- gain_mid: float32 [2, 2, 512], replicated, may hold values from 0.25 to 1.75
- bias_mid: float32 [2, 2, 512], replicated, may hold values from -2.5 to 2.5
- gain_out: float32 [2, 2048], replicated, may hold values from 0.25 to 1.75
- bias_out: float32 [2, 2048], replicated, may hold values from -2.5 to 2.5
- head_a: bfloat16 [2048, 1000], P('fsdp'), may hold values from -0.5 to 0.5
- head_b: bfloat16 [2048, 365], P('fsdp'), may hold values from -0.5 to 0.5
- head_c: bfloat16 [2048, 40], P('fsdp'), may hold values from -0.5 to 0.5
- label_a: int32 [1152], P(('dp', 'fsdp')), may hold values from 0 to 999
- label_b: int32 [1152], P(('dp', 'fsdp')), may hold values from 0 to 364
- label_c: int32 [1152], P(('dp', 'fsdp')), may hold values from 0 to 39
- drop_bits: int32 [1152, 2048], P(('dp', 'fsdp')), may hold values from 0 to 32767
Outputs:
- trunk_out: bfloat16 [1152, 49, 2048], P(('dp', 'fsdp'))
- grad_features: float32 [1152, 49, 2048], P(('dp', 'fsdp'))
- grad_w_reduce: float32 [2, 2048, 512], P(None, 'fsdp')
- grad_w_spatial: float32 [2, 4608, 512], P(None, 'fsdp')
- grad_w_expand: float32 [2, 512, 2048], P(None, 'fsdp')
- grad_gain_mid: float32 [2, 2, 512], replicated
- grad_bias_mid: float32 [2, 2, 512], replicated
- grad_gain_out: float32 [2, 2048], replicated
- grad_bias_out: float32 [2, 2048], replicated
- grad_head_a: float32 [2048, 1000], P('fsdp')
- grad_head_b: float32 [2048, 365], P('fsdp')
- grad_head_c: float32 [2048, 40], P('fsdp')
Inputs may be any that keep to these rules, and one draw needn't show every extreme that they name: `grid_size`: each image's grid side is 7 or 2, the same for the 4 images of an aligned group; both sides occur in every draw.
All inputs are finite; a program needn't handle non-finite values.
Results may differ from a plain program's by a relative error of at most 0.017.
Values may be sent and summed in bfloat16 or wider, within the bound.
No kernel may reach another device: no remote copies, remote signals or barrier semaphores. Data moves between devices by JAX's collectives and lax.ppermute only.
A program may use at most 448 MiB of HBM per device.

v0:
```python
import jax
import jax.numpy as jnp
from jax import lax
from jax.sharding import PartitionSpec as P

SIDE = 7


norm_eps = 1e-05
abs_floor = 0.05
drop_width = 0.1
loss_scale = 256.0


def pixel_masks(grid_size):
    cells = jnp.arange(SIDE * SIDE, dtype=jnp.int32)
    grid_rows = cells // SIDE
    grid_cols = cells % SIDE
    bound = grid_size[:, None]
    inside = (grid_rows[None, :] < bound) & (grid_cols[None, :] < bound)
    return jnp.where(inside, 1.0, 0.0).astype(jnp.float32)


def matmul(left, right):
    return jnp.dot(left, right, preferred_element_type=jnp.float32)


def matmul_t(left, right):
    return lax.dot_general(
        left, right, (((1,), (1,)), ((), ())), preferred_element_type=jnp.float32
    )


def contract_rows(left, right):
    return lax.dot_general(
        left, right, (((0,), (0,)), ((), ())), preferred_element_type=jnp.float32
    )


def patches(values):
    images = values.shape[0] // (SIDE * SIDE)
    channels = values.shape[1]
    grid = values.reshape(images, SIDE, SIDE, channels)
    padded = jnp.pad(grid, ((0, 0), (1, 1), (1, 1), (0, 0)))
    taps = [
        padded[:, row_off : row_off + SIDE, col_off : col_off + SIDE, :]
        for row_off in range(3)
        for col_off in range(3)
    ]
    return jnp.concatenate(taps, axis=-1).reshape(images * SIDE * SIDE, 9 * channels)


def fold_patches(grads, channels):
    images = grads.shape[0] // (SIDE * SIDE)
    taps = grads.reshape(images, SIDE, SIDE, 9, channels)
    summed = jnp.zeros((images, SIDE + 2, SIDE + 2, channels), jnp.float32)
    for row_off in range(3):
        for col_off in range(3):
            summed = summed + jnp.pad(
                taps[:, :, :, 3 * row_off + col_off, :],
                ((0, 0), (row_off, 2 - row_off), (col_off, 2 - col_off), (0, 0)),
            )
    return summed[:, 1 : SIDE + 1, 1 : SIDE + 1, :].reshape(images * SIDE * SIDE, channels)


def silu_slope(values):
    sigma = jax.nn.sigmoid(values)
    return sigma * (1.0 + values * (1.0 - sigma))


def norm_forward(hidden, pixel_rows, local_count, gain, shift):
    summed, squares, live_count = lax.psum(
        (
            jnp.sum(hidden * pixel_rows, axis=0),
            jnp.sum(pixel_rows * hidden * hidden, axis=0),
            local_count,
        ),
        ("dp", "fsdp"),
    )
    center = summed / live_count
    spread = squares / live_count - center * center
    scale = lax.rsqrt(spread + norm_eps)
    normed = (hidden - center) * scale
    return (normed, scale, live_count, normed * gain + shift)


def norm_backward(upstream, normed, scale, live_count, gain, pixel_rows):
    sum_up, sum_cross = lax.psum(
        (jnp.sum(pixel_rows * upstream, axis=0), jnp.sum(pixel_rows * upstream * normed, axis=0)),
        ("dp", "fsdp"),
    )
    grad_hidden = (
        pixel_rows
        * scale
        * gain
        * (upstream - sum_up / live_count - normed * sum_cross / live_count)
    )
    return (grad_hidden.astype(jnp.bfloat16), sum_cross, sum_up)


def block_forward(
    inputs, pixel_rows, local_count, weights, gain_pair, bias_pair, gain_last, bias_last
):
    w_one, w_two, w_three = weights
    hidden_one = matmul(inputs, w_one)
    normed_one, scale_one, live_count, pre_one = norm_forward(
        hidden_one, pixel_rows, local_count, gain_pair[0], bias_pair[0]
    )
    act_one = (pixel_rows * jax.nn.silu(pre_one)).astype(jnp.bfloat16)
    hidden_two = matmul(patches(act_one), w_two)
    normed_two, scale_two, live_count, pre_two = norm_forward(
        hidden_two, pixel_rows, local_count, gain_pair[1], bias_pair[1]
    )
    act_two = (pixel_rows * jax.nn.silu(pre_two)).astype(jnp.bfloat16)
    hidden_three = matmul(act_two, w_three)
    normed_three, scale_three, live_count, pre_three = norm_forward(
        hidden_three, pixel_rows, local_count, gain_last, bias_last
    )
    pre_out = pre_three + inputs.astype(jnp.float32)
    outputs = (pixel_rows * jax.nn.silu(pre_out)).astype(jnp.bfloat16)
    kept = (
        inputs,
        act_one,
        act_two,
        pre_one,
        pre_two,
        pre_out,
        normed_one,
        normed_two,
        normed_three,
        scale_one,
        scale_two,
        scale_three,
        live_count,
    )
    return (outputs, kept)


def block_backward(grad_out, kept, weights, gain_pair, gain_last, pixel_rows):
    (
        inputs,
        act_one,
        act_two,
        pre_one,
        pre_two,
        pre_out,
        normed_one,
        normed_two,
        normed_three,
        scale_one,
        scale_two,
        scale_three,
        live_count,
    ) = kept
    w_one, w_two, w_three = weights
    grad_pre = grad_out * pixel_rows * silu_slope(pre_out)
    grad_three, gain_three, shift_three = norm_backward(
        grad_pre, normed_three, scale_three, live_count, gain_last, pixel_rows
    )
    wgrad_three = contract_rows(act_two, grad_three)
    back_two = matmul_t(grad_three, w_three)
    grad_inner = back_two * pixel_rows * silu_slope(pre_two)
    grad_two, gain_two, shift_two = norm_backward(
        grad_inner, normed_two, scale_two, live_count, gain_pair[1], pixel_rows
    )
    wgrad_two = contract_rows(patches(act_one), grad_two)
    back_one = fold_patches(matmul_t(grad_two, w_two), act_one.shape[1])
    grad_first = back_one * pixel_rows * silu_slope(pre_one)
    grad_one, gain_one, shift_one = norm_backward(
        grad_first, normed_one, scale_one, live_count, gain_pair[0], pixel_rows
    )
    wgrad_one = contract_rows(inputs, grad_one)
    grad_in = matmul_t(grad_one, w_one) + grad_pre
    shards = (
        lax.psum_scatter(wgrad_one, "fsdp", scatter_dimension=0, tiled=True),
        lax.psum_scatter(wgrad_two, "fsdp", scatter_dimension=0, tiled=True),
        lax.psum_scatter(wgrad_three, "fsdp", scatter_dimension=0, tiled=True),
    )
    return (
        grad_in,
        shards,
        jnp.stack([gain_one, gain_two]),
        jnp.stack([shift_one, shift_two]),
        gain_three,
        shift_three,
    )


def grad_drop(task_grads, drop_bits):
    summed = task_grads[0] + task_grads[1] + task_grads[2]
    magnitude = sum([jnp.sqrt(single * single + abs_floor * abs_floor) for single in task_grads])
    purity = 0.5 * (1.0 + summed / magnitude)
    level = (drop_bits.astype(jnp.float32) + 0.5) / 32768.0
    keep_share = jax.nn.sigmoid((purity - level) / drop_width)
    return 0.5 * summed + (keep_share - 0.5) * magnitude


def on_device(
    features,
    grid_size,
    w_reduce,
    w_spatial,
    w_expand,
    gain_mid,
    bias_mid,
    gain_out,
    bias_out,
    head_a,
    head_b,
    head_c,
    label_a,
    label_b,
    label_c,
    drop_bits,
):
    pixel_mask = pixel_masks(grid_size)
    pixel_area = (grid_size * grid_size).astype(jnp.float32)
    local_count = jnp.sum(pixel_area)
    pixel_rows = pixel_mask.reshape(-1, 1)
    channels = features.shape[2]
    inputs = (features * pixel_mask[:, :, None].astype(jnp.bfloat16)).reshape(-1, channels)
    blocks = w_reduce.shape[0]
    current = inputs
    saved = []
    gathered = []
    for block_index in range(blocks):
        weights = (
            lax.all_gather(w_reduce[block_index], "fsdp", axis=0, tiled=True),
            lax.all_gather(w_spatial[block_index], "fsdp", axis=0, tiled=True),
            lax.all_gather(w_expand[block_index], "fsdp", axis=0, tiled=True),
        )
        current, kept = block_forward(
            current,
            pixel_rows,
            local_count,
            weights,
            gain_mid[block_index],
            bias_mid[block_index],
            gain_out[block_index],
            bias_out[block_index],
        )
        saved.append(kept)
        gathered.append(weights)
    trunk_grid = current.reshape(-1, SIDE * SIDE, channels)
    heads = (
        lax.all_gather(head_a, "fsdp", axis=0, tiled=True),
        lax.all_gather(head_b, "fsdp", axis=0, tiled=True),
        lax.all_gather(head_c, "fsdp", axis=0, tiled=True),
    )
    pooled_raw = (
        jnp.sum(trunk_grid.astype(jnp.float32) * pixel_mask[:, :, None], axis=1)
        / pixel_area[:, None]
    )
    pooled = pooled_raw.astype(jnp.bfloat16)
    task_grads = []
    head_terms = []
    for weight, labels in ((heads[0], label_a), (heads[1], label_b), (heads[2], label_c)):
        logits = matmul(pooled, weight)
        classes = jnp.arange(weight.shape[1], dtype=jnp.int32)
        targets = jnp.where(classes[None, :] == labels[:, None], 1.0, 0.0)
        probs = jax.nn.softmax(logits, axis=1)
        grad_logits = (loss_scale * (probs - targets)).astype(jnp.bfloat16)
        head_terms.append(contract_rows(pooled, grad_logits))
        task_grads.append(matmul_t(grad_logits, weight) / pixel_area[:, None])
    merged = grad_drop(task_grads, drop_bits)
    grad_out = (pixel_mask[:, :, None] * merged[:, None, :]).reshape(-1, channels)
    head_shards = (
        lax.psum_scatter(head_terms[0], "fsdp", scatter_dimension=0, tiled=True),
        lax.psum_scatter(head_terms[1], "fsdp", scatter_dimension=0, tiled=True),
        lax.psum_scatter(head_terms[2], "fsdp", scatter_dimension=0, tiled=True),
    )
    reduce_parts = []
    spatial_parts = []
    expand_parts = []
    gain_parts = []
    bias_parts = []
    gain_last_parts = []
    bias_last_parts = []
    for block_index in reversed(range(blocks)):
        weights = (
            lax.all_gather(w_reduce[block_index], "fsdp", axis=0, tiled=True),
            lax.all_gather(w_spatial[block_index], "fsdp", axis=0, tiled=True),
            lax.all_gather(w_expand[block_index], "fsdp", axis=0, tiled=True),
        )
        grad_out, shards, gain_pair, bias_pair, gain_last, bias_last = block_backward(
            grad_out,
            saved[block_index],
            weights,
            gain_mid[block_index],
            gain_out[block_index],
            pixel_rows,
        )
        reduce_parts.insert(0, shards[0])
        spatial_parts.insert(0, shards[1])
        expand_parts.insert(0, shards[2])
        gain_parts.insert(0, gain_pair)
        bias_parts.insert(0, bias_pair)
        gain_last_parts.insert(0, gain_last)
        bias_last_parts.insert(0, bias_last)
    totals = (
        lax.psum(jnp.stack(reduce_parts).astype(jnp.bfloat16), "dp").astype(jnp.float32),
        lax.psum(jnp.stack(spatial_parts).astype(jnp.bfloat16), "dp").astype(jnp.float32),
        lax.psum(jnp.stack(expand_parts).astype(jnp.bfloat16), "dp").astype(jnp.float32),
        lax.psum(head_shards[0].astype(jnp.bfloat16), "dp").astype(jnp.float32),
        lax.psum(head_shards[1].astype(jnp.bfloat16), "dp").astype(jnp.float32),
        lax.psum(head_shards[2].astype(jnp.bfloat16), "dp").astype(jnp.float32),
    )
    grad_features = grad_out.reshape(-1, SIDE * SIDE, channels) * pixel_mask[:, :, None]
    return (
        trunk_grid,
        grad_features,
        totals[0] / loss_scale,
        totals[1] / loss_scale,
        totals[2] / loss_scale,
        jnp.stack(gain_parts) / loss_scale,
        jnp.stack(bias_parts) / loss_scale,
        jnp.stack(gain_last_parts) / loss_scale,
        jnp.stack(bias_last_parts) / loss_scale,
        totals[3] / loss_scale,
        totals[4] / loss_scale,
        totals[5] / loss_scale,
    )


def solution(mesh):
    in_specs = (
        P(("dp", "fsdp"), None, None),
        P(("dp", "fsdp")),
        P(None, "fsdp", None),
        P(None, "fsdp", None),
        P(None, "fsdp", None),
        P(),
        P(),
        P(),
        P(),
        P("fsdp", None),
        P("fsdp", None),
        P("fsdp", None),
        P(("dp", "fsdp")),
        P(("dp", "fsdp")),
        P(("dp", "fsdp")),
        P(("dp", "fsdp"), None),
    )
    out_specs = (
        P(("dp", "fsdp"), None, None),
        P(("dp", "fsdp"), None, None),
        P(None, "fsdp", None),
        P(None, "fsdp", None),
        P(None, "fsdp", None),
        P(),
        P(),
        P(),
        P(),
        P("fsdp", None),
        P("fsdp", None),
        P("fsdp", None),
    )
    return jax.shard_map(
        on_device, mesh=mesh, in_specs=in_specs, out_specs=out_specs, check_vma=False
    )
```

profile of v0, /device:TPU:0, one launch (start us, length us, event | category | flops | bytes accessed | tf_op | source)
XLA Modules:
  0.0 1843.8 jit_solution(9966195940612426294)
XLA Ops:
  19.8 17.3 all_gather.41
  57.4 9.7 multiply_reduce_fusion.10
  67.1 42.5 %all-reduce.31 = (f32[512]{0:T(512)S(1)}, f32[]{:T(128)}, f32[512]{0:T(512)S(1)}) all-reduce(f32[512]{0:T(512)S(1)} %get-tuple-element.167, f32[]{:T(128)} %fusion.30, f32[512]{0:T(512)S(1)} %get-tuple-element.166), channel_id=1, replica_groups=mesh['dp'=4,'fsdp'=8] {'dp','fsdp'}, use_global_device_ids=true, to_apply=%region_5.6 | all-reduce | flops 1025 | bytes 8200 | tf_op jit(solution)/shard_map/psum | solution.py:72
  115.2 12.3 pad_slice_fusion.8
  172.3 15.0 multiply_reduce_fusion.9
  187.4 41.6 %all-reduce.30 = (f32[512]{0:T(512)S(1)}, f32[512]{0:T(512)S(1)}) all-reduce(f32[512]{0:T(512)S(1)} %get-tuple-element.165, f32[512]{0:T(512)S(1)} %get-tuple-element.164), channel_id=1, replica_groups=mesh['dp'=4,'fsdp'=8] {'dp','fsdp'}, use_global_device_ids=true, to_apply=%region_9.10 | all-reduce | flops 1024 | bytes 8192 | tf_op jit(solution)/shard_map/psum | solution.py:72
  229.7 10.4 multiply_reduce_fusion.1
  240.2 41.3 %all-reduce.29 = (f32[2048]{0:T(1024)S(1)}, f32[2048]{0:T(1024)S(1)}) all-reduce(f32[2048]{0:T(1024)S(1)} %get-tuple-element.151, f32[2048]{0:T(1024)S(1)} %get-tuple-element.150), channel_id=1, replica_groups=mesh['dp'=4,'fsdp'=8] {'dp','fsdp'}, use_global_device_ids=true, to_apply=%region_13.14 | all-reduce | flops 4096 | bytes 32768 | tf_op jit(solution)/shard_map/psum | solution.py:72
  282.2 12.9 multiply_convert_fusion.3
  295.2 9.8 multiply_reduce_fusion.8
  304.9 39.2 %all-reduce.28 = (f32[512]{0:T(512)S(1)}, f32[512]{0:T(512)S(1)}) all-reduce(f32[512]{0:T(512)S(1)} %get-tuple-element.163, f32[512]{0:T(512)S(1)} %get-tuple-element.162), channel_id=1, replica_groups=mesh['dp'=4,'fsdp'=8] {'dp','fsdp'}, use_global_device_ids=true, to_apply=%region_17.18 | all-reduce | flops 1024 | bytes 8192 | tf_op jit(solution)/shard_map/psum | solution.py:72
  349.8 12.3 pad_slice_fusion
  406.9 14.9 multiply_reduce_fusion.7
  421.8 41.3 %all-reduce.27 = (f32[512]{0:T(512)S(1)}, f32[512]{0:T(512)S(1)}) all-reduce(f32[512]{0:T(512)S(1)} %get-tuple-element.161, f32[512]{0:T(512)S(1)} %get-tuple-element.160), channel_id=1, replica_groups=mesh['dp'=4,'fsdp'=8] {'dp','fsdp'}, use_global_device_ids=true, to_apply=%region_21.22 | all-reduce | flops 1024 | bytes 8192 | tf_op jit(solution)/shard_map/psum | solution.py:72
  463.8 10.3 multiply_reduce_fusion
  474.2 39.2 %all-reduce.26 = (f32[2048]{0:T(1024)S(1)}, f32[2048]{0:T(1024)S(1)}) all-reduce(f32[2048]{0:T(1024)S(1)} %get-tuple-element.149, f32[2048]{0:T(1024)S(1)} %get-tuple-element.148), channel_id=1, replica_groups=mesh['dp'=4,'fsdp'=8] {'dp','fsdp'}, use_global_device_ids=true, to_apply=%region_25.26 | all-reduce | flops 4096 | bytes 32768 | tf_op jit(solution)/shard_map/psum | solution.py:72
  514.1 12.8 multiply_convert_fusion.2
  561.0 11.9 mul.758
  572.9 20.3 %multiply_reduce_fusion.6 = (f32[2048]{0:T(1024)S(1)}, f32[2048]{0:T(1024)S(1)}, f32[1764,2048]{1,0:T(8,128)}) fusion(f32[1764]{0:T(1024)S(1)} %get-tuple-element.246, f32[2048]{0:T(1024)S(1)} %get-tuple-element.248, f32[1764,2048]{1,0:T(8,128)} %get-tuple-element.274, f32[2048]{0:T(1024)S(1)} %get-tuple-element.247, ...), kind=kLoop, calls=%fused_computation.22 | loop fusion | flops 72249344 | bytes 50640672 | tf_op jit(solution)/shard_map/reduce_sum | solution.py:89
  593.2 41.3 %all-reduce.25 = (f32[2048]{0:T(1024)S(1)}, f32[2048]{0:T(1024)S(1)}) all-reduce(f32[2048]{0:T(1024)S(1)} %get-tuple-element.147, f32[2048]{0:T(1024)S(1)} %get-tuple-element.146), channel_id=1, replica_groups=mesh['dp'=4,'fsdp'=8] {'dp','fsdp'}, use_global_device_ids=true, to_apply=%region_36.37 | all-reduce | flops 4096 | bytes 32768 | tf_op jit(solution)/shard_map/psum | solution.py:88
  635.3 12.4 multiply_convert_fusion.1
  655.5 39.3 %all-reduce.24 = (f32[512]{0:T(512)S(1)}, f32[512]{0:T(512)S(1)}) all-reduce(f32[512]{0:T(512)S(1)} %get-tuple-element.159, f32[512]{0:T(512)S(1)} %get-tuple-element.158), channel_id=1, replica_groups=mesh['dp'=4,'fsdp'=8] {'dp','fsdp'}, use_global_device_ids=true, to_apply=%region_40.41 | all-reduce | flops 1024 | bytes 8192 | tf_op jit(solution)/shard_map/psum | solution.py:88
  695.5 20.6 %fusion.2 = f32[1764,4608]{1,0:T(8,128)} fusion(bf16[1,4608,512]{2,1,0:T(8,128)(2,1)} %all-gather.27.cloned.1.call-done, f32[1764,512]{1,0:T(8,128)} %get-tuple-element.281, f32[1764,512]{1,0:T(8,128)} %get-tuple-element.273, f32[]{:T(128)} %get-tuple-element.191, f32[512]{0:T(512)S(1)} %get-tuple-element.176, f32[512]{0:T(512)S(1)} %broadcast_divide_fusion.7, ...), kind=kOutput, calls=%fused_computation.51 | convolution fusion | flops 8332627968 | bytes 44475284 | tf_op jit(solution)/shard_map/dot_general | solution.py:29
  716.2 40.2 %reshape.295 = f32[36,7,7,9,512]{4,3,2,1,0:T(8,128)} reshape(f32[1764,4608]{1,0:T(8,128)} %fusion.2) | data formatting | bytes 65028096 | tf_op jit(solution)/shard_map/reshape | solution.py:55
  756.3 89.2 %fusion.37 = (f32[36,7,7,1,512]{4,3,2,1,0:T(1,128)}, f32[36,7,7,1,512]{4,3,2,1,0:T(1,128)S(1)}, f32[36,7,7,1,512]{4,3,2,1,0:T(1,128)}, f32[36,7,7,1,512]{4,3,2,1...) fusion(f32[36,7,7,9,512]{4,3,2,1,0:T(8,128)} %reshape.295), kind=kLoop, calls=%fused_computation.237 | loop fusion | bytes 65028096 | tf_op jit(solution)/shard_map/slice | solution.py:60
  900.4 41.1 %all-reduce.23 = (f32[512]{0:T(512)S(1)}, f32[512]{0:T(512)S(1)}) all-reduce(f32[512]{0:T(512)S(1)} %get-tuple-element.157, f32[512]{0:T(512)S(1)} %get-tuple-element.156), channel_id=1, replica_groups=mesh['dp'=4,'fsdp'=8] {'dp','fsdp'}, use_global_device_ids=true, to_apply=%region_44.45 | all-reduce | flops 1024 | bytes 8192 | tf_op jit(solution)/shard_map/psum | solution.py:88
  942.3 11.0 fusion.35
  958.1 22.7 %multiply_reduce_fusion.5 = (f32[2048]{0:T(1024)S(1)}, f32[2048]{0:T(1024)S(1)}, f32[1764,2048]{1,0:T(8,128)}) fusion(f32[1764]{0:T(1024)S(1)} %get-tuple-element.246, f32[2048]{0:T(1024)S(1)} %copy-done.52, f32[1764,2048]{1,0:T(8,128)} %get-tuple-element.271, f32[2048]{0:T(1024)S(1)} %copy-done.50, bf16[1764,2048]{1,0:T(8,128)(2,1)} %reshape.291, ...), kind=kOutput, calls=%fused_computation.21 | convolution fusion | flops 3771625472 | bytes 54537104 | tf_op jit(solution)/shard_map/dot_general | solution.py:29
  980.9 40.2 %all-reduce.22 = (f32[2048]{0:T(1024)S(1)}, f32[2048]{0:T(1024)S(1)}) all-reduce(f32[2048]{0:T(1024)S(1)} %get-tuple-element.145, f32[2048]{0:T(1024)S(1)} %get-tuple-element.144), channel_id=1, replica_groups=mesh['dp'=4,'fsdp'=8] {'dp','fsdp'}, use_global_device_ids=true, to_apply=%region_48.49 | all-reduce | flops 4096 | bytes 32768 | tf_op jit(solution)/shard_map/psum | solution.py:88
  1021.8 12.1 multiply_convert_fusion
  1043.6 12.3 multiply_reduce_fusion.16
  1055.9 42.2 %all-reduce.21 = (f32[512]{0:T(512)S(1)}, f32[512]{0:T(512)S(1)}) all-reduce(f32[512]{0:T(512)S(1)} %get-tuple-element.155, f32[512]{0:T(512)S(1)} %get-tuple-element.154), channel_id=1, replica_groups=mesh['dp'=4,'fsdp'=8] {'dp','fsdp'}, use_global_device_ids=true, to_apply=%region_52.53 | all-reduce | flops 1024 | bytes 8192 | tf_op jit(solution)/shard_map/psum | solution.py:88
  1098.7 20.6 %fusion.6 = f32[1764,4608]{1,0:T(8,128)} fusion(bf16[1,4608,512]{2,1,0:T(8,128)(2,1)} %all-gather.21.cloned.1.call-done, f32[1764,512]{1,0:T(8,128)} %get-tuple-element.283, f32[1764,512]{1,0:T(8,128)} %get-tuple-element.270, f32[512]{0:T(512)S(1)} %get-tuple-element.170, f32[512]{0:T(512)S(1)} %broadcast_divide_fusion.5, f32[]{:T(128)} %get-tuple-element.191, ...), kind=kOutput, calls=%fused_computation.55 | convolution fusion | flops 8332627968 | bytes 44475284 | tf_op jit(solution)/shard_map/dot_general | solution.py:29
  1119.4 40.2 %reshape.297 = f32[36,7,7,9,512]{4,3,2,1,0:T(8,128)} reshape(f32[1764,4608]{1,0:T(8,128)} %fusion.6) | data formatting | bytes 65028096 | tf_op jit(solution)/shard_map/reshape | solution.py:55
  1168.8 90.5 %fusion.36 = (f32[36,7,7,1,512]{4,3,2,1,0:T(1,128)}, f32[36,7,7,1,512]{4,3,2,1,0:T(1,128)S(1)}, f32[36,7,7,1,512]{4,3,2,1,0:T(1,128)}, f32[36,7,7,1,512]{4,3,2,1...) fusion(f32[36,7,7,9,512]{4,3,2,1,0:T(8,128)} %reshape.297), kind=kLoop, calls=%fused_computation.236 | loop fusion | bytes 65028096 | tf_op jit(solution)/shard_map/slice | solution.py:60
  1314.7 40.0 %all-reduce.20 = (f32[512]{0:T(512)S(1)}, f32[512]{0:T(512)S(1)}) all-reduce(f32[512]{0:T(512)S(1)} %get-tuple-element.153, f32[512]{0:T(512)S(1)} %get-tuple-element.152), channel_id=1, replica_groups=mesh['dp'=4,'fsdp'=8] {'dp','fsdp'}, use_global_device_ids=true, to_apply=%region_56.57 | all-reduce | flops 1024 | bytes 8192 | tf_op jit(solution)/shard_map/psum | solution.py:88
  1360.0 9.2 fusion.50
  1375.6 18.6 %fusion.48 = f32[4608,512]{1,0:T(8,128)} fusion(bf16[1764,4608]{1,0:T(8,128)(2,1)} %constant_dynamic-update-slice_fusion.9, f32[1764,512]{1,0:T(8,128)} %get-tuple-element.281, f32[1764,512]{1,0:T(8,128)} %get-tuple-element.273, f32[]{:T(128)} %get-tuple-element.191, f32[512]{0:T(512)S(1)} %copy-done.117, f32[512]{0:T(512)S(1)} %copy-done.115, ...), kind=kOutput, calls=%fused_computation.248 | convolution fusion | flops 8332627968 | bytes 32936852 | tf_op jit(solution)/shard_map/dot_general | solution.py:35
  1394.3 18.4 fusion.49
  1422.3 85.5 %reduce-scatter.22.cloned.1.call-done = f32[256,1000]{0,1:T(8,128)} async-done(((f32[2048,1000]{0,1:T(8,128)}), f32[256,1000]{0,1:T(8,128)}) %reduce-scatter.22.cloned.1.call-update) | async-done | bytes 1024016 | tf_op jit(solution)/shard_map/reduce_scatter | solution.py:268
  1509.9 98.6 %reduce-scatter.16.cloned.1.call-done = f32[576,512]{1,0:T(8,128)} async-done(((f32[4608,512]{1,0:T(8,128)}), f32[576,512]{1,0:T(8,128)}) %reduce-scatter.16.cloned.1.call-update) | async-done | bytes 1179664 | tf_op jit(solution)/shard_map/reduce_scatter | solution.py:176
  1609.8 98.7 %reduce-scatter.14.cloned.1.call-done = f32[576,512]{1,0:T(8,128)} async-done(((f32[4608,512]{1,0:T(8,128)}), f32[576,512]{1,0:T(8,128)}) %reduce-scatter.14.cloned.1.call-update) | async-done | bytes 1179664 | tf_op jit(solution)/shard_map/reduce_scatter | solution.py:176
  1711.0 11.3 convolution_add_fusion
  1722.4 10.8 copy.324
  1733.1 11.4 reshape.299
  1752.0 11.3 copy.325
  1766.6 16.7 psum.262
  1783.9 44.0 %all-reduce.35.cloned.1.call-done = (bf16[2,256,512]{2,1,0:T(8,128)(2,1)}, bf16[2,576,512]{2,1,0:T(8,128)(2,1)}, bf16[2,64,2048]{2,1,0:T(8,128)(2,1)}, bf16[256,1000]{0,1:T(8,128)(2,1)}, bf16[256,365]{0,1:T(8,128)(2,1)}) async-done(((bf16[2,256,512]{2,1,0:T(8,128)(2,1)}, bf16[2,576,512]{2,1,0:T(8,128)(2,1)}, bf16[2,64,2048]{2,1,0:T(8,128)(2,1)}, bf16[256,1000]{0,1:T(8,128)(2,1)}, ...) | async-done | bytes 2927120 | tf_op jit(solution)/shard_map/psum | solution.py:301
  (466 shorter events, 362.4 us)
Async XLA Ops:
  7.2 50.2 %all-gather.19.cloned.1.call-start = ((), (), s32[]{:S(2)}) async-start(), calls=%async_computation.20 | async-start | bytes 2359296 | tf_op jit(solution)/shard_map/all_gather | solution.py:228
  9.3 163.1 %all-gather.21.cloned.1.call-start = ((), (), s32[]{:S(2)}) async-start(), calls=%async_computation.21 | async-start | bytes 5308416 | tf_op jit(solution)/shard_map/all_gather | solution.py:229
  11.7 218.0 %all-gather.23.cloned.1.call-start = ((), (), s32[]{:S(2)}) async-start(), calls=%async_computation.22 | async-start | bytes 2359296 | tf_op jit(solution)/shard_map/all_gather | solution.py:230
  12.6 282.6 %all-gather.25.cloned.1.call-start = ((), (), s32[]{:S(2)}) async-start(), calls=%async_computation.23 | async-start | bytes 2359296 | tf_op jit(solution)/shard_map/all_gather | solution.py:228
  13.1 393.8 %all-gather.27.cloned.1.call-start = ((), (), s32[]{:S(2)}) async-start(), calls=%async_computation.24 | async-start | bytes 5308416 | tf_op jit(solution)/shard_map/all_gather | solution.py:229
  13.7 450.1 %all-gather.29.cloned.1.call-start = ((), (), s32[]{:S(2)}) async-start(), calls=%async_computation.25 | async-start | bytes 2359296 | tf_op jit(solution)/shard_map/all_gather | solution.py:230
  14.3 527.6 %all-gather.17.cloned.1.call-start = ((), (), s32[]{:S(2)}) async-start(), calls=%async_computation.10 | async-start | bytes 1695744 | tf_op jit(solution)/shard_map/all_gather | solution.py:247
  15.1 531.8 %all-gather.15.cloned.1.call-start = ((), (), s32[]{:S(2)}) async-start(), calls=%async_computation.9 | async-start | bytes 4608000 | tf_op jit(solution)/shard_map/all_gather | solution.py:246
  15.8 1398.7 %reduce-scatter.24.cloned.1.call-start = ((), (), s32[]{:S(2)}) async-start(), calls=%async_computation.18 | async-start | bytes 3391488 | tf_op jit(solution)/shard_map/reduce_scatter | solution.py:269
  17.8 145.8 %copy-start.62 = (f32[1,1,512]{2,1,0:T(1,128)}, f32[1,1,512]{2,1,0:T(1,128)S(1)}, u32[]{:S(2)}) copy-start(f32[1,1,512]{2,1,0:T(1,128)S(1)} %get-tuple-element.251) | copy-start | bytes 6148
  17.8 211.9 %copy-start.118 = (f32[1,1,512]{2,1,0:T(1,128)}, f32[1,1,512]{2,1,0:T(1,128)S(1)}, u32[]{:S(2)}) copy-start(f32[1,1,512]{2,1,0:T(1,128)S(1)} %get-tuple-element.250) | copy-start | bytes 6148
  17.8 380.2 %copy-start.64 = (f32[1,1,512]{2,1,0:T(1,128)}, f32[1,1,512]{2,1,0:T(1,128)S(1)}, u32[]{:S(2)}) copy-start(f32[1,1,512]{2,1,0:T(1,128)S(1)} %get-tuple-element.252) | copy-start | bytes 6148
  17.8 924.4 %copy-start.120 = (f32[1,1,512]{2,1,0:T(1,128)}, f32[1,1,512]{2,1,0:T(1,128)S(1)}, u32[]{:S(2)}) copy-start(f32[1,1,512]{2,1,0:T(1,128)S(1)} %get-tuple-element.249) | copy-start | bytes 6148
  17.8 145.8 %copy-start.66 = (f32[1,1,512]{2,1,0:T(1,128)}, f32[1,1,512]{2,1,0:T(1,128)S(1)}, u32[]{:S(2)}) copy-start(f32[1,1,512]{2,1,0:T(1,128)S(1)} %get-tuple-element.255) | copy-start | bytes 6148
  17.8 211.9 %copy-start.122 = (f32[1,1,512]{2,1,0:T(1,128)}, f32[1,1,512]{2,1,0:T(1,128)S(1)}, u32[]{:S(2)}) copy-start(f32[1,1,512]{2,1,0:T(1,128)S(1)} %get-tuple-element.254) | copy-start | bytes 6148
  17.8 380.2 %copy-start.68 = (f32[1,1,512]{2,1,0:T(1,128)}, f32[1,1,512]{2,1,0:T(1,128)S(1)}, u32[]{:S(2)}) copy-start(f32[1,1,512]{2,1,0:T(1,128)S(1)} %get-tuple-element.256) | copy-start | bytes 6148
  18.5 263.7 %copy-start.47 = (f32[1,2048]{1,0:T(1,128)}, f32[1,2048]{1,0:T(1,128)S(1)}, u32[]{:S(2)}) copy-start(f32[1,2048]{1,0:T(1,128)S(1)} %get-tuple-element.242) | copy-start | bytes 24580
  19.1 263.1 %copy-start.70 = (f32[1,2048]{1,0:T(1,128)}, f32[1,2048]{1,0:T(1,128)S(1)}, u32[]{:S(2)}) copy-start(f32[1,2048]{1,0:T(1,128)S(1)} %get-tuple-element.244) | copy-start | bytes 24580
  110.3 53.3 %copy-start.54 = (f32[512]{0:T(512)}, f32[512]{0:T(512)S(1)}, u32[]{:S(2)}) copy-start(f32[512]{0:T(512)S(1)} %get-tuple-element.265) | copy-start | bytes 6148
  110.3 53.3 %copy-start.56 = (f32[512]{0:T(512)}, f32[512]{0:T(512)S(1)}, u32[]{:S(2)}) copy-start(f32[512]{0:T(512)S(1)} %get-tuple-element.266) | copy-start | bytes 6148
  344.8 53.2 %copy-start.58 = (f32[512]{0:T(512)}, f32[512]{0:T(512)S(1)}, u32[]{:S(2)}) copy-start(f32[512]{0:T(512)S(1)} %get-tuple-element.261) | copy-start | bytes 6148
  344.8 53.2 %copy-start.60 = (f32[512]{0:T(512)}, f32[512]{0:T(512)S(1)}, u32[]{:S(2)}) copy-start(f32[512]{0:T(512)S(1)} %get-tuple-element.262) | copy-start | bytes 6148
  463.8 478.5 %copy-start.109 = (f32[512]{0:T(512)}, f32[512]{0:T(512)S(1)}, u32[]{:S(2)}) copy-start(f32[512]{0:T(512)S(1)} %get-tuple-element.259) | copy-start | bytes 6148
  463.8 478.5 %copy-start.111 = (f32[512]{0:T(512)}, f32[512]{0:T(512)S(1)}, u32[]{:S(2)}) copy-start(f32[512]{0:T(512)S(1)} %get-tuple-element.260) | copy-start | bytes 6148
  463.8 50.3 %copy-start.46 = (f32[1,2048]{1,0:T(1,128)S(1)}, f32[1,2048]{1,0:T(1,128)}, u32[]{:S(2)}) copy-start(f32[1,2048]{1,0:T(1,128)} %get-tuple-element.241) | copy-start | bytes 24580
  463.8 50.3 %copy-start.53 = (f32[1,2048]{1,0:T(1,128)S(1)}, f32[1,2048]{1,0:T(1,128)}, u32[]{:S(2)}) copy-start(f32[1,2048]{1,0:T(1,128)} %get-tuple-element.243) | copy-start | bytes 24580
  546.6 869.6 %reduce-scatter.20.cloned.1.call-start = ((), (), s32[]{:S(2)}) async-start(), calls=%async_computation.16 | async-start | bytes 4718592 | tf_op jit(solution)/shard_map/reduce_scatter | solution.py:177
  634.5 13.1 copy-start.72
  634.5 13.1 copy-start.76
  694.8 21.3 %copy-start.90 = (f32[512]{0:T(512)}, f32[512]{0:T(512)S(1)}, u32[]{:S(2)}) copy-start(f32[512]{0:T(512)S(1)} %get-tuple-element.177) | copy-start | bytes 6148
  694.8 21.3 %copy-start.116 = (f32[512]{0:T(512)}, f32[512]{0:T(512)S(1)}, u32[]{:S(2)}) copy-start(f32[512]{0:T(512)S(1)} %get-tuple-element.176) | copy-start | bytes 6148
  695.5 20.7 %copy-start.114 = (f32[512]{0:T(512)}, f32[512]{0:T(512)S(1)}, u32[]{:S(2)}) copy-start(f32[512]{0:T(512)S(1)} %broadcast_divide_fusion.7) | copy-start | bytes 6148
  953.3 464.1 %reduce-scatter.18.cloned.1.call-start = ((), (), s32[]{:S(2)}) async-start(), calls=%async_computation.15 | async-start | bytes 4718592 | tf_op jit(solution)/shard_map/reduce_scatter | solution.py:177
  1021.8 15.2 copy-start.106
  1021.8 15.2 copy-start.108
  1021.8 15.2 copy-start.119
  1021.8 15.2 copy-start.123
  1021.8 15.2 copy-start.130
  1043.5 375.7 %reduce-scatter.12.cloned.1.call-start = ((), (), s32[]{:S(2)}) async-start(), calls=%async_computation.12 | async-start | bytes 4718592 | tf_op jit(solution)/shard_map/reduce_scatter | solution.py:175
  1098.0 21.3 %copy-start.94 = (f32[512]{0:T(512)}, f32[512]{0:T(512)S(1)}, u32[]{:S(2)}) copy-start(f32[512]{0:T(512)S(1)} %get-tuple-element.171) | copy-start | bytes 6148
  1168.7 251.6 %reduce-scatter.10.cloned.1.call-start = ((), (), s32[]{:S(2)}) async-start(), calls=%async_computation.11 | async-start | bytes 4718592 | tf_op jit(solution)/shard_map/reduce_scatter | solution.py:175
  1369.3 138.6 %reduce-scatter.22.cloned.1.call-start = ((), (), s32[]{:S(2)}) async-start(), calls=%async_computation.17 | async-start | bytes 9216000 | tf_op jit(solution)/shard_map/reduce_scatter | solution.py:268
  1374.8 233.6 %reduce-scatter.16.cloned.1.call-start = ((), (), s32[]{:S(2)}) async-start(), calls=%async_computation.14 | async-start | bytes 10616832 | tf_op jit(solution)/shard_map/reduce_scatter | solution.py:176
  1394.2 314.3 %reduce-scatter.14.cloned.1.call-start = ((), (), s32[]{:S(2)}) async-start(), calls=%async_computation.13 | async-start | bytes 10616832 | tf_op jit(solution)/shard_map/reduce_scatter | solution.py:176
  1412.7 353.1 %reduce-scatter.26.cloned.1.call-start = ((), (), s32[]{:S(2)}) async-start(), calls=%async_computation.19 | async-start | bytes 368640 | tf_op jit(solution)/shard_map/reduce_scatter | solution.py:270
  1414.5 413.5 %all-reduce.35.cloned.1.call-start = ((), (), s32[]{:S(2)}) async-start(), calls=%async_computation.26 | async-start | bytes 5857280 | tf_op jit(solution)/shard_map/psum | solution.py:301
  1751.9 13.3 copy-start.73
  1752.0 13.3 copy-start.75
  (102 other events, 565.3 us)
Sparse Core Ops, SparseCore 0:
  10.2 33.1 all-gather.18
  45.6 52.0 all-gather.20
  99.8 27.7 all-gather.22
  129.1 28.6 all-gather.24
  159.8 51.5 all-gather.26
  213.4 27.8 all-gather.28
  243.0 26.7 all-gather.16
  271.4 47.6 all-gather.14
  546.7 40.1 reduce-scatter.23
  953.4 49.2 reduce-scatter.19
  1043.7 51.4 reduce-scatter.17
  1168.9 49.9 reduce-scatter.11
  1369.4 50.1 reduce-scatter.9
  1421.9 85.8 reduce-scatter.21
  1510.6 97.8 reduce-scatter.15
  1610.6 97.8 reduce-scatter.13
  1711.2 28.8 reduce-scatter.25
  1745.2 82.7 all-reduce.34
where the time goes:
time: 1860 us; the launch traced here: 1840 us
  local copies, waits for them, and re-layouts  536 us (29%)
  blocking collectives  523 us (28%)
  waiting for transfers between devices  330 us (18%)
  matrix products  255 us (14%)
  other arithmetic  183 us (10%)
    psum x6, blocking collectives, norm_forward(): lax.psum((jnp.sum(hidden * pixel_rows, axis=0), jnp.sum(pixel_rows * hidd...  245 us
    psum x6, blocking collectives, norm_backward(): lax.psum((jnp.sum(pixel_rows * upstream, axis=0), jnp.sum(pixel_rows * up...  244 us
    slice x20, local copies, waits for them, and re-layouts, fold_patches(): taps[:, :, :, 3 * row_off + col_off, :]  221 us
    reduce_scatter x2, waiting for transfers between devices, block_backward(): lax.psum_scatter(wgrad_two, 'fsdp', scatter_dimension=0, tiled=True)  197 us
    dot_general x9, matrix products, matmul_t(): lax.dot_general(left, right, (((1,), (1,)), ((), ())), preferred_element_...  97.6 us
    reduce_scatter x1, waiting for transfers between devices, on_device(): lax.psum_scatter(head_terms[0], 'fsdp', scatter_dimension=0, tiled=True)  85.5 us
    dot_general x9, matrix products, contract_rows(): lax.dot_general(left, right, (((0,), (0,)), ((), ())), preferred_element_...  80.9 us
    reshape x2, local copies, waits for them, and re-layouts, fold_patches(): taps = grads.reshape(images, SIDE, SIDE, 9, channels)  80.3 us
  transfers between devices with their start and end apart: 18, of which 4 were waited for; matrix products, arithmetic and copies ran while one was open for 51% of the time, Pallas kernels for 0%

commit v1 on v0

v1 whole, which is shorter than its diff:
```python
import functools

import jax
import jax.numpy as jnp
from jax import lax
from jax.experimental import pallas as pl
from jax.experimental.pallas import tpu as pltpu
from jax.sharding import PartitionSpec as P

SIDE = 7
TAPS = 3
EPS = 1e-05
FLOOR = 0.05
WIDTH = 0.1
SCALE = 256.0
BF = jnp.bfloat16
F32 = jnp.float32
VMEM_LIMIT = 56 * 1024 * 1024
AXES = ("dp", "fsdp")


def nn(left, right):
    return jnp.dot(left, right, preferred_element_type=F32)


def nt(left, right):
    return lax.dot_general(left, right, (((1,), (1,)), ((), ())), preferred_element_type=F32)


def tn(left, right):
    return lax.dot_general(left, right, (((0,), (0,)), ((), ())), preferred_element_type=F32)


def sigmoid(v):
    return 0.5 * jnp.tanh(0.5 * v) + 0.5


def slope(v):
    s = sigmoid(v)
    return s * (1.0 + v * (1.0 - s))


def rowsum(v):
    return jnp.sum(v, axis=0, keepdims=True)


def params(n_grid):
    return pltpu.CompilerParams(
        dimension_semantics=("arbitrary",) * n_grid, vmem_limit_bytes=VMEM_LIMIT
    )


def whole(shape):
    zeros = (0,) * len(shape)
    return pl.BlockSpec(shape, lambda *g: zeros)


def tile(rows, cols):
    return pl.BlockSpec((rows, cols), lambda j: (j, 0))


def sds(shape, dtype):
    return jax.ShapeDtypeStruct(shape, dtype)


def cost(flops, nbytes, trans=0):
    return pl.CostEstimate(flops=int(flops), bytes_accessed=int(nbytes), transcendentals=int(trans))


def forward_consts(tot, inv, gb):
    mu = tot[0:1, :] * inv
    var = jnp.maximum(tot[1:2, :] * inv - mu * mu, 0.0)
    rstd = lax.rsqrt(var + EPS)
    a = rstd * gb[0:1, :]
    return mu, rstd, a, gb[1:2, :] - mu * a


def backward_consts(mu, rstd, a, btot, inv):
    ex = btot[1:2, :] * rstd * inv
    c1 = -a * rstd * ex
    c0 = -a * btot[0:1, :] * inv - c1 * mu
    return c1, c0


def add_stats(st, first, top, low, cols=slice(None)):
    @pl.when(first)
    def _():
        st[0:1, cols] = top
        st[1:2, cols] = low

    @pl.when(jnp.logical_not(first))
    def _():
        st[0:1, cols] += top
        st[1:2, cols] += low


class Shape:
    def __init__(self, images):
        self.images = images
        self.main = images // 16 * 16
        self.rest = images - self.main
        self.top = SIDE * self.main
        self.low = (SIDE + 1) * self.rest
        self.rows = self.top + self.low
        self.total = SIDE * self.rows
        self.padded = self.main + 16


def prep_kernel(sh, f, mask, x, scr):
    channels = x.shape[1]
    scr[...] = jnp.zeros_like(scr)
    for s in range(SIDE):
        x[s * sh.main : (s + 1) * sh.main, :] = (
            f[s, 0 : sh.main, :].astype(F32) * mask[s * sh.main : (s + 1) * sh.main, :]
        ).astype(BF)
        scr[s * sh.rest : (s + 1) * sh.rest, :] = f[s, sh.main : sh.images, :].astype(F32)
    x[sh.top : sh.rows, :] = jnp.where(mask[sh.top : sh.rows, :] > 0.0, scr[...], 0.0).astype(BF)


def prep(sh, features, mask):
    channels = features.shape[2]
    return pl.pallas_call(
        functools.partial(prep_kernel, sh),
        grid=(SIDE,),
        in_specs=[
            pl.BlockSpec((SIDE, sh.images, channels), lambda j: (j, 0, 0)),
            tile(sh.rows, 1),
        ],
        out_specs=tile(sh.rows, channels),
        out_shape=sds((sh.total, channels), BF),
        scratch_shapes=[pltpu.VMEM((sh.low, channels), F32)],
        compiler_params=params(1),
        name="prep",
    )(features, mask)


def reduce_kernel(x, w, h, st):
    acc = nn(x[...], w[...])
    h[...] = acc
    add_stats(st, pl.program_id(0) == 0, rowsum(acc), rowsum(acc * acc))


def reduce_conv(sh, x, w):
    c, m = w.shape
    return pl.pallas_call(
        reduce_kernel,
        grid=(SIDE,),
        in_specs=[tile(sh.rows, c), whole((c, m))],
        out_specs=[tile(sh.rows, m), whole((2, m))],
        out_shape=[sds((sh.total, m), F32), sds((2, m), F32)],
        compiler_params=params(1),
        cost_estimate=cost(2 * sh.total * c * m, 2 * sh.total * c + 4 * sh.total * m),
        name="reduce_conv",
    )(x, w)


def shifted(sh, v, scr):
    m = v.shape[1]
    gap = jnp.zeros((sh.main, m), F32)
    scr[8 : 8 + sh.low, :] = v[sh.top :, :]
    before = jnp.concatenate([gap, v[: sh.top - sh.main, :], scr[8 - sh.rest : 8 - sh.rest + sh.low, :]], axis=0)
    after = jnp.concatenate([v[sh.main : sh.top, :], gap, scr[8 + sh.rest : 8 + sh.rest + sh.low, :]], axis=0)
    return before, v, after


def put_shifted(sh, v, scr, pat, row):
    m = v.shape[1]
    at = pl.ds(pl.multiple_of(row * sh.rows, sh.rows), sh.rows)
    for k, part in enumerate(shifted(sh, v, scr)):
        pat[at, k * m : (k + 1) * m] = part.astype(BF)


def spatial_kernel(sh, inv, h1, tot, gb, mask, mask_out, w, act, h2, st, pat, scr):
    j = pl.program_id(0)
    m = h1.shape[1]

    @pl.when(j == 0)
    def _():
        pat[...] = jnp.zeros_like(pat)
        scr[...] = jnp.zeros_like(scr)

    mu, rstd, a, b = forward_consts(tot, inv[0, 0], gb)
    acc = None
    for k in range(2):
        at = pl.ds(pl.multiple_of((j + k) * sh.rows, sh.rows), sh.rows)
        part = nn(pat[at, :], w[k * TAPS * m : (k + 1) * TAPS * m, :])
        acc = part if acc is None else acc + part
    live = jnp.where(j < SIDE, mask[...], 0.0)
    v = h1[...] * a + b
    y = live * (v * sigmoid(v))

    @pl.when(j < SIDE)
    def _():
        act[...] = y.astype(BF)

    put_shifted(sh, y, scr, pat, j + 2)
    at = pl.ds(pl.multiple_of((j + 2) * sh.rows, sh.rows), sh.rows)
    acc = acc + nn(pat[at, :], w[2 * TAPS * m :, :])
    h2[...] = acc
    got = jnp.where(j > 0, mask_out[...], 0.0) * acc
    add_stats(st, j == 0, rowsum(got), rowsum(got * acc))


def spatial_conv(sh, h1, tot, inv, gb, mask, w):
    m = h1.shape[1]
    into = lambda j: (jnp.minimum(j, SIDE - 1), 0)
    outof = lambda j: (jnp.maximum(j - 1, 0), 0)
    return pl.pallas_call(
        functools.partial(spatial_kernel, sh),
        grid=(SIDE + 1,),
        in_specs=[
            pl.BlockSpec(memory_space=pltpu.SMEM),
            pl.BlockSpec((sh.rows, m), into),
            whole((2, m)),
            whole((2, m)),
            pl.BlockSpec((sh.rows, 1), into),
            pl.BlockSpec((sh.rows, 1), outof),
            whole(w.shape),
        ],
        out_specs=[
            pl.BlockSpec((sh.rows, m), into),
            pl.BlockSpec((sh.rows, m), outof),
            whole((2, m)),
        ],
        out_shape=[sds((sh.total, m), BF), sds((sh.total, m), F32), sds((2, m), F32)],
        scratch_shapes=[
            pltpu.VMEM(((SIDE + 3) * sh.rows, TAPS * m), BF),
            pltpu.VMEM((sh.low + 16, m), F32),
        ],
        compiler_params=params(1),
        cost_estimate=cost(2 * sh.total * w.size, 2 * w.size + 10 * sh.total * m),
        name="spatial_conv",
    )(inv, h1, tot, gb, mask, mask, w)


def expand_kernel(inv, h2, tot, gb, mask, w, act, h3, st):
    first = pl.program_id(0) == 0
    mu, rstd, a, b = forward_consts(tot, inv[0, 0], gb)
    v = h2[...] * a + b
    y = (mask[...] * (v * sigmoid(v))).astype(BF)
    act[...] = y
    step = 512
    for c in range(0, w.shape[1], step):
        cols = slice(c, c + step)
        acc = nn(y, w[:, cols])
        h3[:, cols] = acc.astype(BF)
        add_stats(st, first, rowsum(acc), rowsum(acc * acc), cols)


def expand_conv(sh, h2, tot, inv, gb, mask, w):
    m, c = w.shape
    return pl.pallas_call(
        expand_kernel,
        grid=(SIDE,),
        in_specs=[
            pl.BlockSpec(memory_space=pltpu.SMEM),
            tile(sh.rows, m),
            whole((2, m)),
            whole((2, m)),
            tile(sh.rows, 1),
            whole((m, c)),
        ],
        out_specs=[tile(sh.rows, m), tile(sh.rows, c), whole((2, c))],
        out_shape=[sds((sh.total, m), BF), sds((sh.total, c), BF), sds((2, c), F32)],
        compiler_params=params(1),
        cost_estimate=cost(2 * sh.total * c * m, 2 * sh.total * c + 6 * sh.total * m),
        name="expand_conv",
    )(inv, h2, tot, gb, mask, w)


def join_kernel(inv, h3, x, tot, gb, mask, w, y, h1, st):
    mu, rstd, a, b = forward_consts(tot, inv[0, 0], gb)
    step = 512
    acc = None
    for c in range(0, x.shape[1], step):
        cols = slice(c, c + step)
        v = h3[:, cols].astype(F32) * a[:, cols] + b[:, cols] + x[:, cols].astype(F32)
        out = (mask[...] * (v * sigmoid(v))).astype(BF)
        y[:, cols] = out
        part = nn(out, w[cols, :])
        acc = part if acc is None else acc + part
    h1[...] = acc
    add_stats(st, pl.program_id(0) == 0, rowsum(acc), rowsum(acc * acc))


def join(sh, h3, x, tot, inv, gb, mask, w):
    c, m = w.shape
    return pl.pallas_call(
        join_kernel,
        grid=(SIDE,),
        in_specs=[
            pl.BlockSpec(memory_space=pltpu.SMEM),
            tile(sh.rows, c),
            tile(sh.rows, c),
            whole((2, c)),
            whole((2, c)),
            tile(sh.rows, 1),
            whole((c, m)),
        ],
        out_specs=[tile(sh.rows, c), tile(sh.rows, m), whole((2, m))],
        out_shape=[sds((sh.total, c), BF), sds((sh.total, m), F32), sds((2, m), F32)],
        compiler_params=params(1),
        cost_estimate=cost(2 * sh.total * c * m, 6 * sh.total * c + 4 * sh.total * m),
        name="join",
    )(inv, h3, x, tot, gb, mask, w)


def last_kernel(sh, inv, h3, x, tot, gb, mask, area, pick, trunk, pooled, sums, scr):
    j = pl.program_id(0)
    mu, rstd, a, b = forward_consts(tot, inv[0, 0], gb)
    step = 512
    for c in range(0, x.shape[1], step):
        cols = slice(c, c + step)
        v = h3[:, cols].astype(F32) * a[:, cols] + b[:, cols] + x[:, cols].astype(F32)
        out = mask[...] * (v * sigmoid(v))
        low = out.astype(BF)
        scr[:, cols] = out[sh.top :, :]
        for s in range(SIDE):
            trunk[s, 0 : sh.main, cols] = low[s * sh.main : (s + 1) * sh.main, :]
            trunk[s, sh.main : sh.images, cols] = scr[s * sh.rest : (s + 1) * sh.rest, cols].astype(BF)
        part = nn(pick[...], low)

        @pl.when(j == 0)
        def _():
            sums[:, cols] = part

        @pl.when(j > 0)
        def _():
            sums[:, cols] += part

    @pl.when(j == SIDE - 1)
    def _():
        pooled[...] = (sums[...] / area[...]).astype(BF)


def last_join(sh, h3, x, tot, inv, gb, mask, area, pick):
    c = x.shape[1]
    return pl.pallas_call(
        functools.partial(last_kernel, sh),
        grid=(SIDE,),
        in_specs=[
            pl.BlockSpec(memory_space=pltpu.SMEM),
            tile(sh.rows, c),
            tile(sh.rows, c),
            whole((2, c)),
            whole((2, c)),
            tile(sh.rows, 1),
            whole((sh.padded, 1)),
            whole((sh.padded, sh.rows)),
        ],
        out_specs=[
            pl.BlockSpec((SIDE, sh.images, c), lambda j: (j, 0, 0)),
            whole((sh.padded, c)),
        ],
        out_shape=[sds((SIDE * SIDE, sh.images, c), BF), sds((sh.padded, c), BF)],
        scratch_shapes=[pltpu.VMEM((sh.padded, c), F32), pltpu.VMEM((sh.low, c), F32)],
        compiler_params=params(1),
        cost_estimate=cost(2 * sh.padded * sh.total * c, 6 * sh.total * c),
        name="last_join",
    )(inv, h3, x, tot, gb, mask, area, pick)


def heads_kernel(sizes, offsets, pooled, labels, area, bits, w, merged, out):
    rows = pooled.shape[0]
    out[...] = jnp.zeros_like(out)
    summed = None
    at = 0
    for t, (classes, place) in enumerate(zip(sizes, offsets)):
        span = -(-classes // 16) * 16
        wt = w[at : at + span, :]
        at += span
        logits = nt(pooled[...], wt)
        index = lax.broadcasted_iota(jnp.int32, (rows, span), 1)
        inside = index < classes
        logits = jnp.where(inside, logits, -1e30)
        top = jnp.max(logits, axis=1, keepdims=True)
        ex = jnp.where(inside, jnp.exp(logits - top), 0.0)
        probs = ex / jnp.sum(ex, axis=1, keepdims=True)
        targets = jnp.where(index == labels[:, t : t + 1], 1.0, 0.0)
        grad = (SCALE * (probs - targets)).astype(BF)
        out[:, place : place + span] = grad
        single = nn(grad, wt) / area[...]
        size = jnp.sqrt(single * single + FLOOR * FLOOR)
        summed = single if summed is None else summed + single
        magnitude = size if t == 0 else magnitude + size
    purity = 0.5 * (1.0 + summed / magnitude)
    level = (bits[...].astype(F32) + 0.5) / 32768.0
    keep = sigmoid((purity - level) / WIDTH)
    merged[...] = 0.5 * summed + (keep - 0.5) * magnitude


def heads(pooled, labels, area, bits, w, sizes, offsets, span):
    rows, c = pooled.shape
    return pl.pallas_call(
        functools.partial(heads_kernel, sizes, offsets),
        out_shape=[sds((rows, c), F32), sds((rows, span), BF)],
        compiler_params=pltpu.CompilerParams(vmem_limit_bytes=VMEM_LIMIT),
        cost_estimate=cost(4 * rows * c * span, 2 * w.size),
        name="heads",
    )(pooled, labels, area, bits, w)


def top_grad_kernel(sh, inv, merged, h3, x, tot, gb, mask, e3, st, scr):
    j = pl.program_id(0)
    mu, rstd, a, b = forward_consts(tot, inv[0, 0], gb)

    @pl.when(j == 0)
    def _():
        for s in range(SIDE + 1):
            scr[s * sh.rest : (s + 1) * sh.rest, :] = merged[sh.main : sh.images, :]

    step = 256
    for c in range(0, x.shape[1], step):
        cols = slice(c, c + step)
        h = h3[:, cols].astype(F32)
        v = h * a[:, cols] + b[:, cols] + x[:, cols].astype(F32)
        up = jnp.concatenate([merged[0 : sh.main, cols]] * SIDE + [scr[:, cols]], axis=0)
        e = mask[...] * up * slope(v)
        e3[:, cols] = e.astype(BF)
        add_stats(st, j == 0, rowsum(e), rowsum(e * (h - mu[:, cols])), cols)


def top_grad(sh, merged, h3, x, tot, inv, gb, mask):
    c = x.shape[1]
    return pl.pallas_call(
        functools.partial(top_grad_kernel, sh),
        grid=(SIDE,),
        in_specs=[
            pl.BlockSpec(memory_space=pltpu.SMEM),
            whole(merged.shape),
            tile(sh.rows, c),
            tile(sh.rows, c),
            whole((2, c)),
            whole((2, c)),
            tile(sh.rows, 1),
        ],
        out_specs=[tile(sh.rows, c), whole((2, c))],
        out_shape=[sds((sh.total, c), BF), sds((2, c), F32)],
        scratch_shapes=[pltpu.VMEM((sh.low, c), F32)],
        compiler_params=params(1),
        cost_estimate=cost(20 * sh.total * c, 6 * sh.total * c),
        name="top_grad",
    )(inv, merged, h3, x, tot, gb, mask)


def expand_back_kernel(inv, e3, h3, tot3, gb3, btot3, mask, w, h2, tot2, gb2, g3, e2, st):
    mu, rstd, a, b = forward_consts(tot3, inv[0, 0], gb3)
    c1, c0 = backward_consts(mu, rstd, a, btot3, inv[0, 0])
    step = 512
    acc = None
    for c in range(0, e3.shape[1], step):
        cols = slice(c, c + step)
        g = a[:, cols] * e3[:, cols].astype(F32) + c1[:, cols] * h3[:, cols].astype(F32) + c0[:, cols]
        g = (mask[...] * g).astype(BF)
        g3[:, cols] = g
        part = nt(g, w[:, cols])
        acc = part if acc is None else acc + part
    mu, rstd, a, b = forward_consts(tot2, inv[0, 0], gb2)
    h = h2[...]
    e = mask[...] * acc * slope(h * a + b)
    e2[...] = e
    add_stats(st, pl.program_id(0) == 0, rowsum(e), rowsum(e * (h - mu)))


def expand_back(sh, e3, h3, tot3, gb3, btot3, inv, mask, w, h2, tot2, gb2):
    m, c = w.shape
    return pl.pallas_call(
        expand_back_kernel,
        grid=(SIDE,),
        in_specs=[
            pl.BlockSpec(memory_space=pltpu.SMEM),
            tile(sh.rows, c),
            tile(sh.rows, c),
            whole((2, c)),
            whole((2, c)),
            whole((2, c)),
            tile(sh.rows, 1),
            whole((m, c)),
            tile(sh.rows, m),
            whole((2, m)),
            whole((2, m)),
        ],
        out_specs=[tile(sh.rows, c), tile(sh.rows, m), whole((2, m))],
        out_shape=[sds((sh.total, c), BF), sds((sh.total, m), F32), sds((2, m), F32)],
        compiler_params=params(1),
        cost_estimate=cost(2 * sh.total * c * m, 6 * sh.total * c + 8 * sh.total * m),
        name="expand_back",
    )(inv, e3, h3, tot3, gb3, btot3, mask, w, h2, tot2, gb2)


def spatial_back_kernel(
    sh, inv, e2, h2, tot2, gb2, btot2, mask, mask_out, w, h1, tot1, gb1, g2, e1, st, pat, scr
):
    j = pl.program_id(0)
    m = e2.shape[1]

    @pl.when(j == 0)
    def _():
        pat[...] = jnp.zeros_like(pat)
        scr[...] = jnp.zeros_like(scr)

    def taps(k):
        at = pl.ds(pl.multiple_of((j + k) * sh.rows, sh.rows), sh.rows)
        total = None
        for l in range(TAPS):
            tap = TAPS * (2 - k) + (2 - l)
            part = nt(pat[at, l * m : (l + 1) * m], w[tap * m : (tap + 1) * m, :])
            total = part if total is None else total + part
        return total

    acc = taps(0) + taps(1)
    mu, rstd, a, b = forward_consts(tot2, inv[0, 0], gb2)
    c1, c0 = backward_consts(mu, rstd, a, btot2, inv[0, 0])
    live = jnp.where(j < SIDE, mask[...], 0.0)
    g = live * (a * e2[...] + c1 * h2[...] + c0)

    @pl.when(j < SIDE)
    def _():
        g2[...] = g.astype(BF)

    put_shifted(sh, g, scr, pat, j + 2)
    acc = acc + taps(2)
    mu, rstd, a, b = forward_consts(tot1, inv[0, 0], gb1)
    h = h1[...]
    e = jnp.where(j > 0, mask_out[...], 0.0) * acc * slope(h * a + b)
    e1[...] = e
    add_stats(st, j == 0, rowsum(e), rowsum(e * (h - mu)))


def spatial_back(sh, e2, h2, tot2, gb2, btot2, inv, mask, w, h1, tot1, gb1):
    m = e2.shape[1]
    into = lambda j: (jnp.minimum(j, SIDE - 1), 0)
    outof = lambda j: (jnp.maximum(j - 1, 0), 0)
    return pl.pallas_call(
        functools.partial(spatial_back_kernel, sh),
        grid=(SIDE + 1,),
        in_specs=[
            pl.BlockSpec(memory_space=pltpu.SMEM),
            pl.BlockSpec((sh.rows, m), into),
            pl.BlockSpec((sh.rows, m), into),
            whole((2, m)),
            whole((2, m)),
            whole((2, m)),
            pl.BlockSpec((sh.rows, 1), into),
            pl.BlockSpec((sh.rows, 1), outof),
            whole(w.shape),
            pl.BlockSpec((sh.rows, m), outof),
            whole((2, m)),
            whole((2, m)),
        ],
        out_specs=[
            pl.BlockSpec((sh.rows, m), into),
            pl.BlockSpec((sh.rows, m), outof),
            whole((2, m)),
        ],
        out_shape=[sds((sh.total, m), BF), sds((sh.total, m), F32), sds((2, m), F32)],
        scratch_shapes=[
            pltpu.VMEM(((SIDE + 3) * sh.rows, TAPS * m), BF),
            pltpu.VMEM((sh.low + 16, m), F32),
        ],
        compiler_params=params(1),
        cost_estimate=cost(2 * sh.total * w.size, 2 * w.size + 18 * sh.total * m),
        name="spatial_back",
    )(inv, e2, h2, tot2, gb2, btot2, mask, mask, w, h1, tot1, gb1)


def reduce_back_kernel(
    inv, e1, h1, tot1, gb1, btot1, mask, w, e3, h3, x, tot3, gb3, g1, down, st
):
    mu, rstd, a, b = forward_consts(tot1, inv[0, 0], gb1)
    c1, c0 = backward_consts(mu, rstd, a, btot1, inv[0, 0])
    g = (mask[...] * (a * e1[...] + c1 * h1[...] + c0)).astype(BF)
    g1[...] = g
    mu, rstd, a, b = forward_consts(tot3, inv[0, 0], gb3)
    first = pl.program_id(0) == 0
    step = 256
    for c in range(0, x.shape[1], step):
        cols = slice(c, c + step)
        up = nt(g, w[cols, :]) + e3[:, cols].astype(F32)
        h = h3[:, cols].astype(F32)
        v = h * a[:, cols] + b[:, cols] + x[:, cols].astype(F32)
        e = mask[...] * up * slope(v)
        down[:, cols] = e.astype(BF)
        add_stats(st, first, rowsum(e), rowsum(e * (h - mu[:, cols])), cols)


def reduce_back(sh, e1, h1, tot1, gb1, btot1, inv, mask, w, e3, h3, x, tot3, gb3):
    c, m = w.shape
    return pl.pallas_call(
        reduce_back_kernel,
        grid=(SIDE,),
        in_specs=[
            pl.BlockSpec(memory_space=pltpu.SMEM),
            tile(sh.rows, m),
            tile(sh.rows, m),
            whole((2, m)),
            whole((2, m)),
            whole((2, m)),
            tile(sh.rows, 1),
            whole((c, m)),
            tile(sh.rows, c),
            tile(sh.rows, c),
            tile(sh.rows, c),
            whole((2, c)),
            whole((2, c)),
        ],
        out_specs=[tile(sh.rows, m), tile(sh.rows, c), whole((2, c))],
        out_shape=[sds((sh.total, m), BF), sds((sh.total, c), BF), sds((2, c), F32)],
        compiler_params=params(1),
        cost_estimate=cost(2 * sh.total * c * m, 8 * sh.total * c + 10 * sh.total * m),
        name="reduce_back",
    )(inv, e1, h1, tot1, gb1, btot1, mask, w, e3, h3, x, tot3, gb3)


def features_back_kernel(sh, inv, e1, h1, tot1, gb1, btot1, mask, w, e3, g1, out, scr):
    mu, rstd, a, b = forward_consts(tot1, inv[0, 0], gb1)
    c1, c0 = backward_consts(mu, rstd, a, btot1, inv[0, 0])
    g = (mask[...] * (a * e1[...] + c1 * h1[...] + c0)).astype(BF)
    g1[...] = g
    step = 512
    for c in range(0, w.shape[0], step):
        cols = slice(c, c + step)
        up = mask[...] * (nt(g, w[cols, :]) + e3[:, cols].astype(F32))
        scr[:, cols] = up[sh.top :, :]
        for s in range(SIDE):
            out[s, 0 : sh.main, cols] = up[s * sh.main : (s + 1) * sh.main, :]
            out[s, sh.main : sh.images, cols] = scr[s * sh.rest : (s + 1) * sh.rest, cols]


def features_back(sh, e1, h1, tot1, gb1, btot1, inv, mask, w, e3):
    c, m = w.shape
    return pl.pallas_call(
        functools.partial(features_back_kernel, sh),
        grid=(SIDE,),
        in_specs=[
            pl.BlockSpec(memory_space=pltpu.SMEM),
            tile(sh.rows, m),
            tile(sh.rows, m),
            whole((2, m)),
            whole((2, m)),
            whole((2, m)),
            tile(sh.rows, 1),
            whole((c, m)),
            tile(sh.rows, c),
        ],
        out_specs=[tile(sh.rows, m), pl.BlockSpec((SIDE, sh.images, c), lambda j: (j, 0, 0))],
        out_shape=[sds((sh.total, m), BF), sds((SIDE * SIDE, sh.images, c), F32)],
        scratch_shapes=[pltpu.VMEM((sh.low, c), F32)],
        compiler_params=params(1),
        cost_estimate=cost(2 * sh.total * c * m, 6 * sh.total * c + 10 * sh.total * m),
        name="features_back",
    )(inv, e1, h1, tot1, gb1, btot1, mask, w, e3)


def wgrad_kernel(left, right, out):
    out[...] = tn(left[...], right[...]).astype(BF)


def wgrad(left, right, step):
    rows, a = left.shape
    b = right.shape[1]
    by_left = a >= b
    if by_left:
        specs = [pl.BlockSpec((rows, step), lambda j: (0, j)), whole((rows, b))]
        out_spec = pl.BlockSpec((step, b), lambda j: (j, 0))
    else:
        specs = [whole((rows, a)), pl.BlockSpec((rows, step), lambda j: (0, j))]
        out_spec = pl.BlockSpec((a, step), lambda j: (0, j))
    return pl.pallas_call(
        wgrad_kernel,
        grid=(max(a, b) // step,),
        in_specs=specs,
        out_specs=out_spec,
        out_shape=sds((a, b), BF),
        compiler_params=params(1),
        cost_estimate=cost(2 * rows * a * b, 2 * (rows * (a + b) + a * b)),
        name="wgrad",
    )(left, right)


def spatial_wgrad_kernel(sh, act, g, out, pat, scr):
    j = pl.program_id(0)
    m = act.shape[1]

    @pl.when(j == 0)
    def _():
        scr[...] = jnp.zeros_like(scr)
        pat[0 : sh.rows, :] = jnp.zeros((sh.rows, TAPS * m), BF)
        pat[(SIDE + 1) * sh.rows :, :] = jnp.zeros((sh.rows, TAPS * m), BF)
        for r in range(SIDE):
            put_shifted(sh, act[r * sh.rows : (r + 1) * sh.rows, :].astype(F32), scr, pat, r + 1)

    for k in range(TAPS):

        @pl.when(j == k)
        def _(k=k):
            rows = slice(k * sh.rows, (k + SIDE) * sh.rows)
            for l in range(TAPS):
                out[l * m : (l + 1) * m, :] = tn(pat[rows, l * m : (l + 1) * m], g[...]).astype(BF)


def spatial_wgrad(sh, act, g):
    m = act.shape[1]
    return pl.pallas_call(
        functools.partial(spatial_wgrad_kernel, sh),
        grid=(TAPS,),
        in_specs=[whole(act.shape), whole(g.shape)],
        out_specs=pl.BlockSpec((TAPS * m, m), lambda j: (j, 0)),
        out_shape=sds((TAPS * TAPS * m, m), BF),
        scratch_shapes=[
            pltpu.VMEM(((SIDE + 2) * sh.rows, TAPS * m), BF),
            pltpu.VMEM((sh.low + 16, m), F32),
        ],
        compiler_params=params(1),
        cost_estimate=cost(18 * sh.total * m * m, 4 * sh.total * m + 18 * m * m),
        name="spatial_wgrad",
    )(act, g)


def total_of(v, devices):
    flat = v.reshape(8, -1)
    spread = jnp.broadcast_to(flat[None], (devices,) + flat.shape)
    got = lax.all_to_all(spread, AXES, 0, 0, tiled=True)
    return jnp.sum(got, axis=0).reshape(v.shape)


def on_device(
    devices,
    owners,
    features,
    grid_size,
    w_reduce,
    w_spatial,
    w_expand,
    gain_mid,
    bias_mid,
    gain_out,
    bias_out,
    head_a,
    head_b,
    head_c,
    label_a,
    label_b,
    label_c,
    drop_bits,
):
    images, _, channels = features.shape
    inner = w_reduce.shape[2]
    blocks = w_reduce.shape[0]
    sh = Shape(images)

    gather = functools.partial(lax.all_gather, axis_name="fsdp", axis=0, tiled=True)
    weights = [
        (gather(w_reduce[b]), gather(w_spatial[b]), gather(w_expand[b])) for b in range(blocks)
    ]
    sizes = [head.shape[1] for head in (head_a, head_b, head_c)]
    spans = [-(-size // 16) * 16 for size in sizes]
    lanes = [-(-size // 128) * 128 for size in sizes]
    offsets = [0, lanes[0], lanes[0] + lanes[1]]
    head_t = jnp.concatenate(
        [
            jnp.pad(head.T, ((0, span - size), (0, 0)))
            for head, size, span in zip((head_a, head_b, head_c), sizes, spans)
        ],
        axis=0,
    )
    head_all = lax.all_gather(head_t, "fsdp", axis=1, tiled=True)

    steps = jnp.arange(SIDE + 1, dtype=jnp.int32)
    bound = grid_size
    row_ok = steps[:SIDE, None, None] < bound[None, None, :]
    col_ok = steps[None, :, None] < bound[None, None, :]
    alive = (row_ok & col_ok).astype(F32)
    mask = jnp.concatenate(
        [
            alive[:, :SIDE, : sh.main].reshape(SIDE, sh.top),
            alive[:, :, sh.main :].reshape(SIDE, sh.low),
        ],
        axis=1,
    ).reshape(sh.total, 1)
    pixel_area = (grid_size * grid_size).astype(F32)
    area = jnp.pad(pixel_area, (0, sh.padded - images), constant_values=1.0)[:, None]
    row = jnp.arange(sh.rows, dtype=jnp.int32)
    owner = jnp.where(row < sh.top, row % sh.main, sh.main + (row - sh.top) % sh.rest)
    pick = (owner[None, :] == jnp.arange(sh.padded, dtype=jnp.int32)[:, None]).astype(BF)
    labels = jnp.pad(jnp.stack([label_a, label_b, label_c], axis=1), ((0, sh.padded - images), (0, 0)))
    bits = jnp.pad(drop_bits, ((0, sh.padded - images), (0, 0)))
    gb_mid = jnp.stack([gain_mid, bias_mid], axis=2)
    gb_out = jnp.stack([gain_out, bias_out], axis=1)

    x = prep(sh, jnp.transpose(features, (1, 0, 2)), mask)
    saved = []
    h1, part = reduce_conv(sh, x, weights[0][0])
    count = jnp.broadcast_to(jnp.sum(pixel_area), (2, inner))
    both = total_of(jnp.concatenate([part, count], axis=0), devices)
    tot1, live_count = both[:2], both[2, 0]
    inv = (1.0 / live_count).reshape(1, 1)
    for b in range(blocks):
        w1, w2, w3 = weights[b]
        act1, h2, part = spatial_conv(sh, h1, tot1, inv, gb_mid[b, 0], mask, w2)
        tot2 = total_of(part, devices)
        act2, h3, part = expand_conv(sh, h2, tot2, inv, gb_mid[b, 1], mask, w3)
        tot3 = total_of(part, devices)
        saved.append((x, h1, tot1, act1, h2, tot2, act2, h3, tot3))
        if b + 1 < blocks:
            x, h1, part = join(sh, h3, x, tot3, inv, gb_out[b], mask, weights[b + 1][0])
            tot1 = total_of(part, devices)
    trunk, pooled = last_join(sh, h3, x, tot3, inv, gb_out[-1], mask, area, pick)
    merged, grad_logits = heads(
        pooled, labels, area, bits, head_all, sizes, offsets, sum(lanes)
    )

    mine = lax.all_to_all(
        pooled.reshape(sh.padded, owners, channels // owners).transpose(1, 0, 2),
        "fsdp",
        0,
        0,
        tiled=True,
    ).reshape(owners * sh.padded, channels // owners)
    all_logits = gather(grad_logits)
    head_grad = tn(all_logits, mine).astype(BF)

    e3, part = top_grad(sh, merged, h3, x, tot3, inv, gb_out[-1], mask)
    btot3 = total_of(part, devices)
    scatter = functools.partial(lax.psum_scatter, axis_name="fsdp", scatter_dimension=0, tiled=True)
    reduce_grads, spatial_grads, expand_grads = [], [], []
    sums_mid, sums_out = [], []
    for b in reversed(range(blocks)):
        w1, w2, w3 = weights[b]
        x, h1, tot1, act1, h2, tot2, act2, h3, tot3 = saved[b]
        g3, e2, part = expand_back(
            sh, e3, h3, tot3, gb_out[b], btot3, inv, mask, w3, h2, tot2, gb_mid[b, 1]
        )
        btot2 = total_of(part, devices)
        expand_grads.insert(0, scatter(wgrad(act2, g3, inner)))
        g2, e1, part = spatial_back(
            sh, e2, h2, tot2, gb_mid[b, 1], btot2, inv, mask, w2, h1, tot1, gb_mid[b, 0]
        )
        btot1 = total_of(part, devices)
        spatial_grads.insert(0, scatter(spatial_wgrad(sh, act1, g2)))
        sums_out.insert(0, (btot3, tot3))
        sums_mid.insert(0, ((btot1, tot1), (btot2, tot2)))
        if b > 0:
            xp, _, _, _, _, _, _, h3p, tot3p = saved[b - 1]
            g1, e3, part = reduce_back(
                sh, e1, h1, tot1, gb_mid[b, 0], btot1, inv, mask, w1, e3, h3p, xp, tot3p, gb_out[b - 1]
            )
            btot3 = total_of(part, devices)
        else:
            g1, grad_features = features_back(
                sh, e1, h1, tot1, gb_mid[b, 0], btot1, inv, mask, w1, e3
            )
        reduce_grads.insert(0, scatter(wgrad(x, g1, inner)))

    reduced = lax.psum(
        (jnp.stack(reduce_grads), jnp.stack(spatial_grads), jnp.stack(expand_grads), head_grad), "dp"
    )
    finals = [v.astype(F32) / SCALE for v in reduced]
    at = [(place, size) for place, size in zip(offsets, sizes)]

    def gains(pair):
        btot, tot = pair
        mu = tot[0] / live_count
        var = jnp.maximum(tot[1] / live_count - mu * mu, 0.0)
        return btot[1] * lax.rsqrt(var + EPS) / SCALE

    return (
        jnp.transpose(trunk, (1, 0, 2)),
        jnp.transpose(grad_features, (1, 0, 2)),
        finals[0],
        finals[1],
        finals[2],
        jnp.stack([jnp.stack([gains(p) for p in pairs]) for pairs in sums_mid]),
        jnp.stack([jnp.stack([p[0][0] / SCALE for p in pairs]) for pairs in sums_mid]),
        jnp.stack([gains(p) for p in sums_out]),
        jnp.stack([p[0][0] / SCALE for p in sums_out]),
    ) + tuple(finals[3][place : place + size].T for place, size in at)


def solution(mesh):
    split = P(AXES)
    rows = P(None, "fsdp", None)
    head = P("fsdp", None)
    in_specs = (
        P(AXES, None, None), split, rows, rows, rows, P(), P(), P(), P(),
        head, head, head, split, split, split, P(AXES, None),
    )
    out_specs = (
        P(AXES, None, None), P(AXES, None, None), rows, rows, rows, P(), P(), P(), P(), head, head, head,
    )
    body = functools.partial(on_device, mesh.size, mesh.shape["fsdp"])
    return jax.shard_map(body, mesh=mesh, in_specs=in_specs, out_specs=out_specs, check_vma=False)
```

time: 1860 us -> 859 us (0.46)
  local copies, waits for them, and re-layouts: 536 us -> 30.5 us
  blocking collectives: 523 us -> 138 us
  Pallas kernels: 0 us -> 303 us
  matrix products: 255 us -> 2.76 us
  other arithmetic: 183 us -> 20.7 us
    psum x13 -> x0, blocking collectives: 506 us -> none  [the longest x6 245 us: norm_forward(): lax.psum((jnp.sum(hidden * pixel_rows, axis=0), jnp.sum(pixel_rows * hidd...]
    pallas_call x0 -> x22, Pallas kernels: none -> 303 us  [the longest x2 36.8 us: spatial_back(): pl.pallas_call(functools.partial(spatial_back_kernel, sh), grid=(SIDE + 1...]
    slice x31 -> x8, local copies, waits for them, and re-layouts: 260 us -> 5.07 us  [the longest x1 1.94 us: on_device(): w_reduce[b]]
    dot_general x27 -> x1, matrix products: 255 us -> 2.76 us  [tn(): lax.dot_general(left, right, (((0,), (0,)), ((), ())), preferred_element_...]
    reduce_scatter x9 -> x6, waiting for transfers between devices: 283 us -> 102 us  [the longest x2 102 us: on_device(): spatial_grads.insert(0, scatter(spatial_wgrad(sh, act1, g2)))]
    all_to_all x0 -> x10, blocking collectives: none -> 138 us  [the longest x9 127 us: total_of(): got = lax.all_to_all(spread, AXES, 0, 0, tiled=True)]
    reshape x9 -> x15, local copies, waits for them, and re-layouts: 122 us -> 6.87 us  [the longest x12 6.7 us: total_of(): return jnp.sum(got, axis=0).reshape(v.shape)]
    all_gather x8, waiting for transfers between devices: 0.1 us -> 72.5 us  [the longest x2 44.2 us: on_device(): gather(w_spatial[b])]
  transfers between devices with their start and end apart: 18 -> 18, of which waited for: 4 -> 12; matrix products, arithmetic and copies ran while one was open for 51% -> 5% of each run, Pallas kernels for 0% -> 35%
where the time goes in v1:
time: 859 us; the launch traced here: 848 us
  waiting for transfers between devices  325 us (38%)
  Pallas kernels  303 us (35%)
  blocking collectives  138 us (16%)
  local copies, waits for them, and re-layouts  30.5 us (4%)
  other arithmetic  20.7 us (2%)
  between operations  15.4 us (2%)
  starting transfers between devices  12.5 us (1%)
    all_to_all x9, blocking collectives, total_of(): got = lax.all_to_all(spread, AXES, 0, 0, tiled=True)  127 us
    reduce_scatter x2, waiting for transfers between devices, on_device(): spatial_grads.insert(0, scatter(spatial_wgrad(sh, act1, g2)))  102 us
    psum x1, waiting for transfers between devices, on_device(): lax.psum((jnp.stack(reduce_grads), jnp.stack(spatial_grads), jnp.stack(ex...  80.5 us
    all_to_all x3, waiting for transfers between devices, total_of(): got = lax.all_to_all(spread, AXES, 0, 0, tiled=True)  67.8 us
    all_gather x2, waiting for transfers between devices, on_device(): gather(w_spatial[b])  44.2 us
    pallas_call x2, Pallas kernels, spatial_back(): pl.pallas_call(functools.partial(spatial_back_kernel, sh), grid=(SIDE + 1...  36.8 us
    pallas_call x2, Pallas kernels, spatial_conv(): pl.pallas_call(functools.partial(spatial_kernel, sh), grid=(SIDE + 1,), i...  33 us
    pallas_call x4, Pallas kernels, wgrad(): pl.pallas_call(wgrad_kernel, grid=(max(a, b) // step,), in_specs=specs, o...  32.7 us
  transfers between devices with their start and end apart: 18, of which 12 were waited for; matrix products, arithmetic and copies ran while one was open for 5% of the time, Pallas kernels for 35%

profile of v1, /device:TPU:0, one launch (start us, length us, event | category | flops | bytes accessed | tf_op | source)
XLA Modules:
  0.0 848.3 jit_solution(15199096946116053843)
XLA Ops:
  7.2 1.9 fusion.36
  15.8 9.6 %prep.1.x.left = bf16[1792,2048]{1,0:T(8,128)(2,1)} custom-call(bf16[49,36,2048]{2,1,0:T(8,128)(2,1)} %bitcast.117, f32[1792,1]{1,0:T(8,128)} %bitcast.97), custom_call_target="tpu_custom_call" | custom-call | tf_op jit(solution)/shard_map/prep/pallas_call | solution.py:122
  26.0 16.1 %all-gather.19.cloned.1.call-done = bf16[1,2048,512]{2,1,0:T(8,128)(2,1)} async-done(((bf16[1,256,512]{2,1,0:T(8,128)(2,1)}), bf16[1,2048,512]{2,1,0:T(8,128)(2,1)}) %all-gather.19.cloned.1.call-update) | async-done | bytes 2097168 | tf_op jit(solution)/shard_map/all_gather | solution.py:754
  42.0 10.0 %reduce_conv.1 = (f32[1792,512]{1,0:T(8,128)}, f32[2,512]{1,0:T(2,128)}) custom-call(bf16[1792,2048]{1,0:T(8,128)(2,1)} %prep.1.x.left, bf16[2048,512]{1,0:T(8,128)(2,1)} %bitcast.122), custom_call_target="tpu_custom_call" | custom-call | flops 3758096384 | bytes 11010048 | tf_op jit(solution)/shard_map/reduce_conv/pallas_call | solution.py:145
  54.1 4.0 all-to-all-start
  58.8 18.0 %all-to-all-done = f32[32,8,256]{2,1,0:T(8,128)S(1)} async-done(((f32[32,8,256]{2,1,0:T(8,128)}), f32[32,8,256]{2,1,0:T(8,128)S(1)}, u32[]{:S(2)}, u32[]{:S(2)}) %all-to-all-start) | async-done | bytes 262176 | tf_op jit(solution)/shard_map/all_to_all | solution.py:723
  78.9 22.1 %all-gather.21.cloned.1.call-done = bf16[1,4608,512]{2,1,0:T(8,128)(2,1)} async-done(((bf16[1,576,512]{2,1,0:T(8,128)(2,1)}), bf16[1,4608,512]{2,1,0:T(8,128)(2,1)}) %all-gather.21.cloned.1.call-update) | async-done | bytes 4718608 | tf_op jit(solution)/shard_map/all_gather | solution.py:754
  101.0 16.5 %spatial_conv.2 = (bf16[1792,512]{1,0:T(8,128)(2,1)}, f32[1792,512]{1,0:T(8,128)}, f32[2,512]{1,0:T(2,128)}) custom-call(f32[1,1]{1,0:T(1,128)} %bitcast.5.inv, f32[1792,512]{1,0:T(8,128)} %get-tuple-element.53.h1, f32[2,512]{1,0:T(2,128)} %slice.179.tot.tot1, f32[2,512]{1,0:T(2,128)} %get-tuple-element.109.gb.gb1, f32[1792,1]{1,0:T(8,128)} %bitcast.98, ...), custom_call_target="tpu_custom_call" | custom-call | flops 8455716864 | bytes 13893632 | tf_op jit(solution)/shard_map/spatial_conv/pallas_call | solution.py:208
  118.2 14.8 %all_to_all.65 = f32[32,8,128]{2,1,0:T(8,128)S(1)} all-to-all(f32[32,8,128]{2,1,0:T(8,128)S(1)} %broadcast_in_dim.97), channel_id=1, replica_groups=mesh['dp'=4,'fsdp'=8] {'dp','fsdp'}, dimensions={0} | all-to-all | bytes 262144 | tf_op jit(solution)/shard_map/all_to_all | solution.py:723
  134.3 13.2 %expand_conv.2 = (bf16[1792,512]{1,0:T(8,128)(2,1)}, bf16[1792,2048]{1,0:T(8,128)(2,1)}, f32[2,2048]{1,0:T(2,128)}) custom-call(f32[1,1]{1,0:T(1,128)} %bitcast.5.inv, f32[1792,512]{1,0:T(8,128)} %get-tuple-element.54.h2, f32[2,512]{1,0:T(2,128)} %reshape.630.tot.tot2, f32[2,512]{1,0:T(2,128)} %get-tuple-element.110.gb.gb2, f32[1792,1]{1,0:T(8,128)} %bitcast.100, ...), custom_call_target="tpu_custom_call" | custom-call | flops 3758096384 | bytes 12845056 | tf_op jit(solution)/shard_map/expand_conv/pallas_call | solution.py:252
  149.1 3.4 all-to-all-start.2
  153.2 23.1 %all-to-all-done.2 = f32[32,8,512]{2,1,0:T(8,128)S(1)} async-done(((f32[32,8,512]{2,1,0:T(8,128)}), f32[32,8,512]{2,1,0:T(8,128)S(1)}, u32[]{:S(2)}, u32[]{:S(2)}) %all-to-all-start.2) | async-done | bytes 524320 | tf_op jit(solution)/shard_map/all_to_all | solution.py:723
  177.0 16.2 %join.1 = (bf16[1792,2048]{1,0:T(8,128)(2,1)}, f32[1792,512]{1,0:T(8,128)}, f32[2,512]{1,0:T(2,128)}) custom-call(f32[1,1]{1,0:T(1,128)} %bitcast.5.inv, bf16[1792,2048]{1,0:T(8,128)(2,1)} %get-tuple-element.56.h3, bf16[1792,2048]{1,0:T(8,128)(2,1)} %prep.1.x.left, f32[2,2048]{1,0:T(2,128)} %reshape.631.tot.tot3, f32[2,2048]{1,0:T(2,128)} %get-tuple-element.103.gb.gb3, ...), custom_call_target="tpu_custom_call" | custom-call | flops 3758096384 | bytes 25690112 | tf_op jit(solution)/shard_map/join/pallas_call | solution.py:288
  193.9 12.9 %all_to_all.66 = f32[32,8,128]{2,1,0:T(8,128)S(1)} all-to-all(f32[32,8,128]{2,1,0:T(8,128)S(1)} %broadcast_in_dim.101), channel_id=1, replica_groups=mesh['dp'=4,'fsdp'=8] {'dp','fsdp'}, dimensions={0} | all-to-all | bytes 262144 | tf_op jit(solution)/shard_map/all_to_all | solution.py:723
  207.4 22.1 %all-gather.27.cloned.1.call-done = bf16[1,4608,512]{2,1,0:T(8,128)(2,1)} async-done(((bf16[1,576,512]{2,1,0:T(8,128)(2,1)}), bf16[1,4608,512]{2,1,0:T(8,128)(2,1)}) %all-gather.27.cloned.1.call-update) | async-done | bytes 4718608 | tf_op jit(solution)/shard_map/all_gather | solution.py:754
  229.4 16.5 %spatial_conv.3 = (bf16[1792,512]{1,0:T(8,128)(2,1)}, f32[1792,512]{1,0:T(8,128)}, f32[2,512]{1,0:T(2,128)}) custom-call(f32[1,1]{1,0:T(1,128)} %bitcast.5.inv, f32[1792,512]{1,0:T(8,128)} %get-tuple-element.58.h1, f32[2,512]{1,0:T(2,128)} %reshape.632.tot.tot1, f32[2,512]{1,0:T(2,128)} %get-tuple-element.111.gb.gb1, f32[1792,1]{1,0:T(8,128)} %bitcast.102, ...), custom_call_target="tpu_custom_call" | custom-call | flops 8455716864 | bytes 13893632 | tf_op jit(solution)/shard_map/spatial_conv/pallas_call | solution.py:208
  246.7 14.4 %all_to_all.67 = f32[32,8,128]{2,1,0:T(8,128)S(1)} all-to-all(f32[32,8,128]{2,1,0:T(8,128)S(1)} %broadcast_in_dim.103), channel_id=1, replica_groups=mesh['dp'=4,'fsdp'=8] {'dp','fsdp'}, dimensions={0} | all-to-all | bytes 262144 | tf_op jit(solution)/shard_map/all_to_all | solution.py:723
  262.1 13.3 %expand_conv.3 = (bf16[1792,512]{1,0:T(8,128)(2,1)}, bf16[1792,2048]{1,0:T(8,128)(2,1)}, f32[2,2048]{1,0:T(2,128)}) custom-call(f32[1,1]{1,0:T(1,128)} %bitcast.5.inv, f32[1792,512]{1,0:T(8,128)} %get-tuple-element.60.h2, f32[2,512]{1,0:T(2,128)} %reshape.633.tot.tot2, f32[2,512]{1,0:T(2,128)} %get-tuple-element.108.gb.gb2, f32[1792,1]{1,0:T(8,128)} %bitcast.104, ...), custom_call_target="tpu_custom_call" | custom-call | flops 3758096384 | bytes 12845056 | tf_op jit(solution)/shard_map/expand_conv/pallas_call | solution.py:252
  277.1 3.4 all-to-all-start.5
  283.9 26.7 %all-to-all-done.5 = f32[32,8,512]{2,1,0:T(8,128)S(1)} async-done(((f32[32,8,512]{2,1,0:T(8,128)}), f32[32,8,512]{2,1,0:T(8,128)S(1)}, u32[]{:S(2)}, u32[]{:S(2)}) %all-to-all-start.5) | async-done | bytes 524320 | tf_op jit(solution)/shard_map/all_to_all | solution.py:723
  311.2 14.9 %last_join.1 = (bf16[49,36,2048]{2,1,0:T(8,128)(2,1)}, bf16[48,2048]{1,0:T(8,128)(2,1)}) custom-call(f32[1,1]{1,0:T(1,128)} %bitcast.5.inv, bf16[1792,2048]{1,0:T(8,128)(2,1)} %get-tuple-element.62.h3, bf16[1792,2048]{1,0:T(8,128)(2,1)} %get-tuple-element.63.x.left, f32[2,2048]{1,0:T(2,128)} %reshape.634.tot.tot3, f32[2,2048]{1,0:T(2,128)} %get-tuple-element.102.gb.gb3, ...), custom_call_target="tpu_custom_call" | custom-call | flops 352321536 | bytes 22020096 | tf_op jit(solution)/shard_map/last_join/pallas_call | solution.py:338
  326.1 11.2 %all-gather.15.cloned.1.call-done.w = bf16[1424,2048]{1,0:T(8,128)(2,1)} async-done(((bf16[1424,256]{1,0:T(8,128)(2,1)}), bf16[1424,2048]{1,0:T(8,128)(2,1)}) %all-gather.15.cloned.1.call-update) | async-done | bytes 5832720 | tf_op jit(solution)/shard_map/all_gather | solution.py:767
  337.3 7.9 heads.1
  345.3 15.3 %top_grad.1 = (bf16[1792,2048]{1,0:T(8,128)(2,1)}, f32[2,2048]{1,0:T(2,128)}) custom-call(f32[1,1]{1,0:T(1,128)} %bitcast.5.inv, f32[48,2048]{1,0:T(8,128)} %get-tuple-element.67.merged, bf16[1792,2048]{1,0:T(8,128)(2,1)} %get-tuple-element.62.h3, bf16[1792,2048]{1,0:T(8,128)(2,1)} %get-tuple-element.63.x.left, f32[2,2048]{1,0:T(2,128)} %reshape.634.tot.tot3, ...), custom_call_target="tpu_custom_call" | custom-call | flops 73400320 | bytes 22020096 | tf_op jit(solution)/shard_map/top_grad/pallas_call | solution.py:425
  361.4 21.0 %all_to_all.68 = f32[32,8,512]{2,1,0:T(8,128)S(1)} all-to-all(f32[32,8,512]{2,1,0:T(8,128)S(1)} %broadcast_in_dim.108), channel_id=1, replica_groups=mesh['dp'=4,'fsdp'=8] {'dp','fsdp'}, dimensions={0} | all-to-all | bytes 1048576 | tf_op jit(solution)/shard_map/all_to_all | solution.py:723
  383.1 15.9 %expand_back.2 = (bf16[1792,2048]{1,0:T(8,128)(2,1)}, f32[1792,512]{1,0:T(8,128)}, f32[2,512]{1,0:T(2,128)}) custom-call(f32[1,1]{1,0:T(1,128)} %bitcast.5.inv, bf16[1792,2048]{1,0:T(8,128)(2,1)} %get-tuple-element.68.e3, bf16[1792,2048]{1,0:T(8,128)(2,1)} %get-tuple-element.62.h3, f32[2,2048]{1,0:T(2,128)} %reshape.634.tot.tot3, ...), custom_call_target="tpu_custom_call" | custom-call | flops 3758096384 | bytes 29360128 | tf_op jit(solution)/shard_map/expand_back/pallas_call | solution.py:467
  399.1 8.2 wgrad.7
  408.0 11.2 %all_to_all.69 = f32[32,8,128]{2,1,0:T(8,128)S(1)} all-to-all(f32[32,8,128]{2,1,0:T(8,128)S(1)} %broadcast_in_dim.110), channel_id=1, replica_groups=mesh['dp'=4,'fsdp'=8] {'dp','fsdp'}, dimensions={0} | all-to-all | bytes 262144 | tf_op jit(solution)/shard_map/all_to_all | solution.py:723
  419.8 18.4 %spatial_back.2 = (bf16[1792,512]{1,0:T(8,128)(2,1)}, f32[1792,512]{1,0:T(8,128)}, f32[2,512]{1,0:T(2,128)}) custom-call(f32[1,1]{1,0:T(1,128)} %bitcast.5.inv, f32[1792,512]{1,0:T(8,128)} %get-tuple-element.70.e2, f32[1792,512]{1,0:T(8,128)} %get-tuple-element.60.h2, f32[2,512]{1,0:T(2,128)} %reshape.633.tot.tot2, f32[2,512]{1,0:T(2,128)} %get-tuple-element.108.gb.gb2, ...), custom_call_target="tpu_custom_call" | custom-call | flops 8455716864 | bytes 21233664 | tf_op jit(solution)/shard_map/spatial_back/pallas_call | solution.py:534
  438.9 11.1 %all_to_all.70 = f32[32,8,128]{2,1,0:T(8,128)S(1)} all-to-all(f32[32,8,128]{2,1,0:T(8,128)S(1)} %broadcast_in_dim.112), channel_id=1, replica_groups=mesh['dp'=4,'fsdp'=8] {'dp','fsdp'}, dimensions={0} | all-to-all | bytes 262144 | tf_op jit(solution)/shard_map/all_to_all | solution.py:723
  450.7 26.4 %reduce_back.1 = (bf16[1792,512]{1,0:T(8,128)(2,1)}, bf16[1792,2048]{1,0:T(8,128)(2,1)}, f32[2,2048]{1,0:T(2,128)}) custom-call(f32[1,1]{1,0:T(1,128)} %bitcast.5.inv, f32[1792,512]{1,0:T(8,128)} %get-tuple-element.72.e1, f32[1792,512]{1,0:T(8,128)} %get-tuple-element.58.h1, f32[2,512]{1,0:T(2,128)} %reshape.632.tot.tot1, ...), custom_call_target="tpu_custom_call" | custom-call | flops 3758096384 | bytes 38535168 | tf_op jit(solution)/shard_map/reduce_back/pallas_call | solution.py:589
  477.9 18.1 %all_to_all.71 = f32[32,8,512]{2,1,0:T(8,128)S(1)} all-to-all(f32[32,8,512]{2,1,0:T(8,128)S(1)} %broadcast_in_dim.114), channel_id=1, replica_groups=mesh['dp'=4,'fsdp'=8] {'dp','fsdp'}, dimensions={0} | all-to-all | bytes 1048576 | tf_op jit(solution)/shard_map/all_to_all | solution.py:723
  496.7 16.1 %expand_back.3 = (bf16[1792,2048]{1,0:T(8,128)(2,1)}, f32[1792,512]{1,0:T(8,128)}, f32[2,512]{1,0:T(2,128)}) custom-call(f32[1,1]{1,0:T(1,128)} %bitcast.5.inv, bf16[1792,2048]{1,0:T(8,128)(2,1)} %get-tuple-element.74.e3, bf16[1792,2048]{1,0:T(8,128)(2,1)} %get-tuple-element.56.h3, f32[2,2048]{1,0:T(2,128)} %reshape.631.tot.tot3, ...), custom_call_target="tpu_custom_call" | custom-call | flops 3758096384 | bytes 29360128 | tf_op jit(solution)/shard_map/expand_back/pallas_call | solution.py:467
  512.7 8.2 wgrad.6
  521.0 8.1 wgrad.5
  529.8 11.1 %all_to_all.72 = f32[32,8,128]{2,1,0:T(8,128)S(1)} all-to-all(f32[32,8,128]{2,1,0:T(8,128)S(1)} %broadcast_in_dim.116), channel_id=1, replica_groups=mesh['dp'=4,'fsdp'=8] {'dp','fsdp'}, dimensions={0} | all-to-all | bytes 262144 | tf_op jit(solution)/shard_map/all_to_all | solution.py:723
  541.6 18.4 %spatial_back.3 = (bf16[1792,512]{1,0:T(8,128)(2,1)}, f32[1792,512]{1,0:T(8,128)}, f32[2,512]{1,0:T(2,128)}) custom-call(f32[1,1]{1,0:T(1,128)} %bitcast.5.inv, f32[1792,512]{1,0:T(8,128)} %get-tuple-element.76.e2, f32[1792,512]{1,0:T(8,128)} %get-tuple-element.54.h2, f32[2,512]{1,0:T(2,128)} %reshape.630.tot.tot2, f32[2,512]{1,0:T(2,128)} %get-tuple-element.110.gb.gb2, ...), custom_call_target="tpu_custom_call" | custom-call | flops 8455716864 | bytes 21233664 | tf_op jit(solution)/shard_map/spatial_back/pallas_call | solution.py:534
  560.7 12.6 %all_to_all.73 = f32[32,8,128]{2,1,0:T(8,128)S(1)} all-to-all(f32[32,8,128]{2,1,0:T(8,128)S(1)} %broadcast_in_dim.118), channel_id=1, replica_groups=mesh['dp'=4,'fsdp'=8] {'dp','fsdp'}, dimensions={0} | all-to-all | bytes 262144 | tf_op jit(solution)/shard_map/all_to_all | solution.py:723
  574.0 17.1 %features_back.1 = (bf16[1792,512]{1,0:T(8,128)(2,1)}, f32[49,36,2048]{2,1,0:T(8,128)}) custom-call(f32[1,1]{1,0:T(1,128)} %bitcast.5.inv, f32[1792,512]{1,0:T(8,128)} %get-tuple-element.78.e1, f32[1792,512]{1,0:T(8,128)} %get-tuple-element.53.h1, f32[2,512]{1,0:T(2,128)} %slice.179.tot.tot1, f32[2,512]{1,0:T(2,128)} %get-tuple-element.109.gb.gb1, ...), custom_call_target="tpu_custom_call" | custom-call | flops 3758096384 | bytes 31195136 | tf_op jit(solution)/shard_map/features_back/pallas_call | solution.py:632
  591.1 8.2 wgrad.4
  599.5 12.5 %spatial_wgrad.3 = bf16[4608,512]{1,0:T(8,128)(2,1)} custom-call(bf16[1792,512]{1,0:T(8,128)(2,1)} %get-tuple-element.85.act, bf16[1792,512]{1,0:T(8,128)(2,1)} %get-tuple-element.86.g), custom_call_target="tpu_custom_call" | custom-call | flops 8455716864 | bytes 8388608 | tf_op jit(solution)/shard_map/spatial_wgrad/pallas_call | solution.py:704
  612.3 12.6 %spatial_wgrad.2 = bf16[4608,512]{1,0:T(8,128)(2,1)} custom-call(bf16[1792,512]{1,0:T(8,128)(2,1)} %get-tuple-element.83.act, bf16[1792,512]{1,0:T(8,128)(2,1)} %get-tuple-element.84.g), custom_call_target="tpu_custom_call" | custom-call | flops 8455716864 | bytes 8388608 | tf_op jit(solution)/shard_map/spatial_wgrad/pallas_call | solution.py:704
  625.8 10.7 %all_to_all.74 = bf16[8,48,256]{2,1,0:T(8,128)(2,1)S(1)} all-to-all(bf16[8,48,256]{2,1,0:T(8,128)(2,1)S(1)} %bitcast.125), channel_id=1, replica_groups=mesh['dp'=4,'fsdp'=8] {'fsdp'}, dimensions={0} | all-to-all | bytes 393216 | tf_op jit(solution)/shard_map/all_to_all | solution.py:813
  636.6 2.8 convolution_convert_fusion
  643.1 46.9 %reduce-scatter.13.cloned.1.call-done = bf16[576,512]{1,0:T(8,128)(2,1)} async-done(((bf16[4608,512]{1,0:T(8,128)(2,1)}), bf16[576,512]{1,0:T(8,128)(2,1)}) %reduce-scatter.13.cloned.1.call-update) | async-done | bytes 589840 | tf_op jit(solution)/shard_map/reduce_scatter | solution.py:840
  689.9 55.5 %reduce-scatter.11.cloned.1.call-done = bf16[576,512]{1,0:T(8,128)(2,1)} async-done(((bf16[4608,512]{1,0:T(8,128)(2,1)}), bf16[576,512]{1,0:T(8,128)(2,1)}) %reduce-scatter.11.cloned.1.call-update) | async-done | bytes 589840 | tf_op jit(solution)/shard_map/reduce_scatter | solution.py:840
  745.5 2.4 pad_maximum_fusion
  753.3 80.5 %all-reduce.10.cloned.1.call-done = (bf16[2,256,512]{2,1,0:T(8,128)(2,1)}, bf16[2,576,512]{2,1,0:T(8,128)(2,1)}, bf16[2,64,2048]{2,1,0:T(8,128)(2,1)}, bf16[1536,256]{1,0:T(8,128)(2,1)}) async-done(((bf16[2,256,512]{2,1,0:T(8,128)(2,1)}, bf16[2,576,512]{2,1,0:T(8,128)(2,1)}, bf16[2,64,2048]{2,1,0:T(8,128)(2,1)}, bf16[1536,256]{1,0:T(8,128)(2,1)}), (bf16[2,256,512]{2,1,0:T(8,128)(2,1)}, ...) | async-done | bytes 3014672 | tf_op jit(solution)/shard_map/psum | solution.py:855
  (189 shorter events, 51.3 us)
Async XLA Ops:
  7.2 2.1 copy-start.1
  7.2 34.9 %all-gather.19.cloned.1.call-start = ((), (), s32[]{:S(2)}) async-start(), calls=%async_computation.27 | async-start | bytes 2359296 | tf_op jit(solution)/shard_map/all_gather | solution.py:754
  9.2 1.3 copy-start.5
  9.2 91.8 %all-gather.21.cloned.1.call-start = ((), (), s32[]{:S(2)}) async-start(), calls=%async_computation.28 | async-start | bytes 5308416 | tf_op jit(solution)/shard_map/all_gather | solution.py:754
  10.3 2.7 copy-start.6
  10.3 2.7 copy-start.8
  10.3 2.7 copy-start.9
  10.4 123.9 %all-gather.23.cloned.1.call-start = ((), (), s32[]{:S(2)}) async-start(), calls=%async_computation.29 | async-start | bytes 2359296 | tf_op jit(solution)/shard_map/all_gather | solution.py:754
  11.3 2.8 copy-start.16
  11.3 165.7 %all-gather.25.cloned.1.call-start = ((), (), s32[]{:S(2)}) async-start(), calls=%async_computation.30 | async-start | bytes 2359296 | tf_op jit(solution)/shard_map/all_gather | solution.py:754
  11.9 217.6 %all-gather.27.cloned.1.call-start = ((), (), s32[]{:S(2)}) async-start(), calls=%async_computation.31 | async-start | bytes 5308416 | tf_op jit(solution)/shard_map/all_gather | solution.py:754
  12.5 249.7 %all-gather.29.cloned.1.call-start = ((), (), s32[]{:S(2)}) async-start(), calls=%async_computation.32 | async-start | bytes 2359296 | tf_op jit(solution)/shard_map/all_gather | solution.py:754
  13.0 324.3 %all-gather.15.cloned.1.call-start = ((), (), s32[]{:S(2)}) async-start(), calls=%async_computation.19 | async-start | bytes 6561792 | tf_op jit(solution)/shard_map/all_gather | solution.py:767
  42.0 16.1 %copy-start.12 = (f32[2,2,512]{2,1,0:T(2,128)S(1)}, f32[2,2,512]{2,1,0:T(2,128)}, u32[]{:S(2)}) copy-start(f32[2,2,512]{2,1,0:T(2,128)} %param.22) | copy-start | bytes 24580
  42.0 16.2 %copy-start.13 = (f32[2,2,512]{2,1,0:T(2,128)S(1)}, f32[2,2,512]{2,1,0:T(2,128)}, u32[]{:S(2)}) copy-start(f32[2,2,512]{2,1,0:T(2,128)} %param.21) | copy-start | bytes 24580
  54.1 22.7 %all-to-all-start = ((f32[32,8,256]{2,1,0:T(8,128)}), f32[32,8,256]{2,1,0:T(8,128)S(1)}, u32[]{:S(2)}, u32[]{:S(2)}) async-start(f32[32,8,256]{2,1,0:T(8,128)} %broadcast_in_dim.95), calls=%async_computation | async-start | bytes 524288 | tf_op jit(solution)/shard_map/all_to_all | solution.py:723
  134.3 18.2 %copy-start.10 = (f32[2,2048]{1,0:T(2,128)S(1)}, f32[2,2048]{1,0:T(2,128)}, u32[]{:S(2)}) copy-start(f32[2,2048]{1,0:T(2,128)} %param.24) | copy-start | bytes 49156
  134.3 18.3 %copy-start.11 = (f32[2,2048]{1,0:T(2,128)S(1)}, f32[2,2048]{1,0:T(2,128)}, u32[]{:S(2)}) copy-start(f32[2,2048]{1,0:T(2,128)} %param.23) | copy-start | bytes 49156
  149.1 27.2 %all-to-all-start.2 = ((f32[32,8,512]{2,1,0:T(8,128)}), f32[32,8,512]{2,1,0:T(8,128)S(1)}, u32[]{:S(2)}, u32[]{:S(2)}) async-start(f32[32,8,512]{2,1,0:T(8,128)} %broadcast_in_dim.99), calls=%async_computation.2 | async-start | bytes 1048576 | tf_op jit(solution)/shard_map/all_to_all | solution.py:723
  262.1 19.6 %copy-start.17 = (s32[36]{0:T(128)S(1)}, s32[36]{0:T(128)}, u32[]{:S(2)}) copy-start(s32[36]{0:T(128)} %param.30) | copy-start | bytes 436
  262.1 19.6 %copy-start.18 = (s32[36]{0:T(128)S(1)}, s32[36]{0:T(128)}, u32[]{:S(2)}) copy-start(s32[36]{0:T(128)} %param.29) | copy-start | bytes 436
  262.1 19.6 %copy-start.19 = (s32[36]{0:T(128)S(1)}, s32[36]{0:T(128)}, u32[]{:S(2)}) copy-start(s32[36]{0:T(128)} %param.28) | copy-start | bytes 436
  275.4 7.0 copy-start.7
  277.1 33.5 %all-to-all-start.5 = ((f32[32,8,512]{2,1,0:T(8,128)}), f32[32,8,512]{2,1,0:T(8,128)S(1)}, u32[]{:S(2)}, u32[]{:S(2)}) async-start(f32[32,8,512]{2,1,0:T(8,128)} %broadcast_in_dim.105), calls=%async_computation.5 | async-start | bytes 1048576 | tf_op jit(solution)/shard_map/all_to_all | solution.py:723
  280.5 356.1 %all-gather.17.cloned.1.call-start = ((), (), s32[]{:S(2)}) async-start(), calls=%async_computation.26 | async-start | bytes 1327104 | tf_op jit(solution)/shard_map/all_gather | solution.py:820
  345.2 294.1 %reduce-scatter.17.cloned.1.call-start = ((), (), s32[]{:S(2)}) async-start(), calls=%async_computation.25 | async-start | bytes 2359296 | tf_op jit(solution)/shard_map/reduce_scatter | solution.py:835
  407.3 0.7 copy-start.15
  407.3 232.1 %reduce-scatter.15.cloned.1.call-start = ((), (), s32[]{:S(2)}) async-start(), calls=%async_computation.24 | async-start | bytes 2359296 | tf_op jit(solution)/shard_map/reduce_scatter | solution.py:835
  520.9 120.3 %reduce-scatter.9.cloned.1.call-start = ((), (), s32[]{:S(2)}) async-start(), calls=%async_computation.21 | async-start | bytes 2359296 | tf_op jit(solution)/shard_map/reduce_scatter | solution.py:853
  529.1 0.7 copy-start.14
  529.1 112.1 %reduce-scatter.7.cloned.1.call-start = ((), (), s32[]{:S(2)}) async-start(), calls=%async_computation.20 | async-start | bytes 2359296 | tf_op jit(solution)/shard_map/reduce_scatter | solution.py:853
  599.3 90.7 %reduce-scatter.13.cloned.1.call-start = ((), (), s32[]{:S(2)}) async-start(), calls=%async_computation.23 | async-start | bytes 5308416 | tf_op jit(solution)/shard_map/reduce_scatter | solution.py:840
  612.0 133.4 %reduce-scatter.11.cloned.1.call-start = ((), (), s32[]{:S(2)}) async-start(), calls=%async_computation.22 | async-start | bytes 5308416 | tf_op jit(solution)/shard_map/reduce_scatter | solution.py:840
  624.9 0.9 copy-start.2
  624.9 208.9 %all-reduce.10.cloned.1.call-start = ((), (), s32[]{:S(2)}) async-start(), calls=%async_computation.33 | async-start | bytes 6029312 | tf_op jit(solution)/shard_map/psum | solution.py:855
  835.1 2.4 copy-start.4
  835.1 3.5 copy-start
  838.6 1.7 copy-start.3
Sparse Core Ops, SparseCore 0:
  10.2 31.7 all-gather.18
  44.3 56.6 all-gather.20
  103.1 31.1 all-gather.22
  136.3 37.0 all-gather.24
  175.5 53.9 all-gather.26
  230.9 31.1 all-gather.28
  264.3 73.0 all-gather.14
  345.3 22.9 all-gather.16
  407.4 35.3 reduce-scatter.16
  521.0 35.0 reduce-scatter.14
  559.0 36.2 reduce-scatter.8
  599.4 33.6 reduce-scatter.6
  635.4 54.4 reduce-scatter.12
  692.1 53.3 reduce-scatter.10
  749.9 83.8 all-reduce.9

commit v2 on v1

--- a/solution.py
+++ b/solution.py
@@ -35,9 +35,13 @@
     return 0.5 * jnp.tanh(0.5 * v) + 0.5
 
 
-def slope(v):
-    s = sigmoid(v)
-    return s * (1.0 + v * (1.0 - s))
+def silu_half(u):
+    return u * jnp.tanh(u) + u
+
+
+def slope_twice(u):
+    t = jnp.tanh(u)
+    return (1.0 + t) * (1.0 + u * (1.0 - t))
 
 
 def rowsum(v):
@@ -76,22 +80,22 @@
 
 
 def backward_consts(mu, rstd, a, btot, inv):
-    ex = btot[1:2, :] * rstd * inv
+    ex = (btot[1:2, :] - mu * btot[0:1, :]) * rstd * inv
     c1 = -a * rstd * ex
     c0 = -a * btot[0:1, :] * inv - c1 * mu
     return c1, c0
 
 
-def add_stats(st, first, top, low, cols=slice(None)):
-    @pl.when(first)
+def clear_at_first(*refs):
+    @pl.when(pl.program_id(0) == 0)
     def _():
-        st[0:1, cols] = top
-        st[1:2, cols] = low
-
-    @pl.when(jnp.logical_not(first))
-    def _():
-        st[0:1, cols] += top
-        st[1:2, cols] += low
+        for ref in refs:
+            ref[...] = jnp.zeros_like(ref)
+
+
+def add_stats(st, top, low, cols=slice(None)):
+    st[0:1, cols] += top
+    st[1:2, cols] += low
 
 
 class Shape:
@@ -135,9 +139,10 @@
 
 
 def reduce_kernel(x, w, h, st):
+    clear_at_first(st)
     acc = nn(x[...], w[...])
     h[...] = acc
-    add_stats(st, pl.program_id(0) == 0, rowsum(acc), rowsum(acc * acc))
+    add_stats(st, rowsum(acc), rowsum(acc * acc))
 
 
 def reduce_conv(sh, x, w):
@@ -174,31 +179,21 @@
     j = pl.program_id(0)
     m = h1.shape[1]
 
-    @pl.when(j == 0)
-    def _():
-        pat[...] = jnp.zeros_like(pat)
-        scr[...] = jnp.zeros_like(scr)
-
+    clear_at_first(pat, scr, st)
     mu, rstd, a, b = forward_consts(tot, inv[0, 0], gb)
     acc = None
     for k in range(2):
         at = pl.ds(pl.multiple_of((j + k) * sh.rows, sh.rows), sh.rows)
         part = nn(pat[at, :], w[k * TAPS * m : (k + 1) * TAPS * m, :])
         acc = part if acc is None else acc + part
-    live = jnp.where(j < SIDE, mask[...], 0.0)
-    v = h1[...] * a + b
-    y = live * (v * sigmoid(v))
-
-    @pl.when(j < SIDE)
-    def _():
-        act[...] = y.astype(BF)
-
-    put_shifted(sh, y, scr, pat, j + 2)
+    y = mask[...] * silu_half(h1[...] * (0.5 * a) + 0.5 * b)
+    act[...] = y.astype(BF)
+    put_shifted(sh, jnp.where(j < SIDE, y, 0.0), scr, pat, j + 2)
     at = pl.ds(pl.multiple_of((j + 2) * sh.rows, sh.rows), sh.rows)
     acc = acc + nn(pat[at, :], w[2 * TAPS * m :, :])
     h2[...] = acc
     got = jnp.where(j > 0, mask_out[...], 0.0) * acc
-    add_stats(st, j == 0, rowsum(got), rowsum(got * acc))
+    add_stats(st, rowsum(got), rowsum(got * acc))
 
 
 def spatial_conv(sh, h1, tot, inv, gb, mask, w):
@@ -234,17 +229,16 @@
 
 
 def expand_kernel(inv, h2, tot, gb, mask, w, act, h3, st):
-    first = pl.program_id(0) == 0
+    clear_at_first(st)
     mu, rstd, a, b = forward_consts(tot, inv[0, 0], gb)
-    v = h2[...] * a + b
-    y = (mask[...] * (v * sigmoid(v))).astype(BF)
+    y = (mask[...] * silu_half(h2[...] * (0.5 * a) + 0.5 * b)).astype(BF)
     act[...] = y
     step = 512
     for c in range(0, w.shape[1], step):
         cols = slice(c, c + step)
         acc = nn(y, w[:, cols])
         h3[:, cols] = acc.astype(BF)
-        add_stats(st, first, rowsum(acc), rowsum(acc * acc), cols)
+        add_stats(st, rowsum(acc), rowsum(acc * acc), cols)
 
 
 def expand_conv(sh, h2, tot, inv, gb, mask, w):
@@ -269,18 +263,19 @@
 
 
 def join_kernel(inv, h3, x, tot, gb, mask, w, y, h1, st):
+    clear_at_first(st)
     mu, rstd, a, b = forward_consts(tot, inv[0, 0], gb)
     step = 512
     acc = None
     for c in range(0, x.shape[1], step):
         cols = slice(c, c + step)
         v = h3[:, cols].astype(F32) * a[:, cols] + b[:, cols] + x[:, cols].astype(F32)
-        out = (mask[...] * (v * sigmoid(v))).astype(BF)
+        out = (mask[...] * silu_half(0.5 * v)).astype(BF)
         y[:, cols] = out
         part = nn(out, w[cols, :])
         acc = part if acc is None else acc + part
     h1[...] = acc
-    add_stats(st, pl.program_id(0) == 0, rowsum(acc), rowsum(acc * acc))
+    add_stats(st, rowsum(acc), rowsum(acc * acc))
 
 
 def join(sh, h3, x, tot, inv, gb, mask, w):
@@ -307,26 +302,19 @@
 
 def last_kernel(sh, inv, h3, x, tot, gb, mask, area, pick, trunk, pooled, sums, scr):
     j = pl.program_id(0)
+    clear_at_first(sums)
     mu, rstd, a, b = forward_consts(tot, inv[0, 0], gb)
     step = 512
     for c in range(0, x.shape[1], step):
         cols = slice(c, c + step)
         v = h3[:, cols].astype(F32) * a[:, cols] + b[:, cols] + x[:, cols].astype(F32)
-        out = mask[...] * (v * sigmoid(v))
+        out = mask[...] * silu_half(0.5 * v)
         low = out.astype(BF)
         scr[:, cols] = out[sh.top :, :]
         for s in range(SIDE):
             trunk[s, 0 : sh.main, cols] = low[s * sh.main : (s + 1) * sh.main, :]
             trunk[s, sh.main : sh.images, cols] = scr[s * sh.rest : (s + 1) * sh.rest, cols].astype(BF)
-        part = nn(pick[...], low)
-
-        @pl.when(j == 0)
-        def _():
-            sums[:, cols] = part
-
-        @pl.when(j > 0)
-        def _():
-            sums[:, cols] += part
+        sums[:, cols] += nn(pick[...], low)
 
     @pl.when(j == SIDE - 1)
     def _():
@@ -402,22 +390,24 @@
 
 def top_grad_kernel(sh, inv, merged, h3, x, tot, gb, mask, e3, st, scr):
     j = pl.program_id(0)
-    mu, rstd, a, b = forward_consts(tot, inv[0, 0], gb)
+    clear_at_first(st)
 
     @pl.when(j == 0)
     def _():
         for s in range(SIDE + 1):
             scr[s * sh.rest : (s + 1) * sh.rest, :] = merged[sh.main : sh.images, :]
 
+    half = 0.5 * mask[...]
+    mu, rstd, a, b = forward_consts(tot, inv[0, 0], gb)
     step = 256
     for c in range(0, x.shape[1], step):
         cols = slice(c, c + step)
         h = h3[:, cols].astype(F32)
         v = h * a[:, cols] + b[:, cols] + x[:, cols].astype(F32)
         up = jnp.concatenate([merged[0 : sh.main, cols]] * SIDE + [scr[:, cols]], axis=0)
-        e = mask[...] * up * slope(v)
+        e = half * up * slope_twice(0.5 * v)
         e3[:, cols] = e.astype(BF)
-        add_stats(st, j == 0, rowsum(e), rowsum(e * (h - mu[:, cols])), cols)
+        add_stats(st, rowsum(e), rowsum(e * h), cols)
 
 
 def top_grad(sh, merged, h3, x, tot, inv, gb, mask):
@@ -444,6 +434,7 @@
 
 
 def expand_back_kernel(inv, e3, h3, tot3, gb3, btot3, mask, w, h2, tot2, gb2, g3, e2, st):
+    clear_at_first(st)
     mu, rstd, a, b = forward_consts(tot3, inv[0, 0], gb3)
     c1, c0 = backward_consts(mu, rstd, a, btot3, inv[0, 0])
     step = 512
@@ -457,9 +448,9 @@
         acc = part if acc is None else acc + part
     mu, rstd, a, b = forward_consts(tot2, inv[0, 0], gb2)
     h = h2[...]
-    e = mask[...] * acc * slope(h * a + b)
+    e = acc * (0.5 * slope_twice(h * (0.5 * a) + 0.5 * b))
     e2[...] = e
-    add_stats(st, pl.program_id(0) == 0, rowsum(e), rowsum(e * (h - mu)))
+    add_stats(st, rowsum(e), rowsum(e * h))
 
 
 def expand_back(sh, e3, h3, tot3, gb3, btot3, inv, mask, w, h2, tot2, gb2):
@@ -494,10 +485,7 @@
     j = pl.program_id(0)
     m = e2.shape[1]
 
-    @pl.when(j == 0)
-    def _():
-        pat[...] = jnp.zeros_like(pat)
-        scr[...] = jnp.zeros_like(scr)
+    clear_at_first(pat, scr, st)
 
     def taps(k):
         at = pl.ds(pl.multiple_of((j + k) * sh.rows, sh.rows), sh.rows)
@@ -511,20 +499,15 @@
     acc = taps(0) + taps(1)
     mu, rstd, a, b = forward_consts(tot2, inv[0, 0], gb2)
     c1, c0 = backward_consts(mu, rstd, a, btot2, inv[0, 0])
-    live = jnp.where(j < SIDE, mask[...], 0.0)
-    g = live * (a * e2[...] + c1 * h2[...] + c0)
-
-    @pl.when(j < SIDE)
-    def _():
-        g2[...] = g.astype(BF)
-
-    put_shifted(sh, g, scr, pat, j + 2)
+    g = mask[...] * (a * e2[...] + c1 * h2[...] + c0)
+    g2[...] = g.astype(BF)
+    put_shifted(sh, jnp.where(j < SIDE, g, 0.0), scr, pat, j + 2)
     acc = acc + taps(2)
     mu, rstd, a, b = forward_consts(tot1, inv[0, 0], gb1)
     h = h1[...]
-    e = jnp.where(j > 0, mask_out[...], 0.0) * acc * slope(h * a + b)
+    e = jnp.where(j > 0, 0.5 * mask_out[...], 0.0) * acc * slope_twice(h * (0.5 * a) + 0.5 * b)
     e1[...] = e
-    add_stats(st, j == 0, rowsum(e), rowsum(e * (h - mu)))
+    add_stats(st, rowsum(e), rowsum(e * h))
 
 
 def spatial_back(sh, e2, h2, tot2, gb2, btot2, inv, mask, w, h1, tot1, gb1):
@@ -567,21 +550,21 @@
 def reduce_back_kernel(
     inv, e1, h1, tot1, gb1, btot1, mask, w, e3, h3, x, tot3, gb3, g1, down, st
 ):
+    clear_at_first(st)
     mu, rstd, a, b = forward_consts(tot1, inv[0, 0], gb1)
     c1, c0 = backward_consts(mu, rstd, a, btot1, inv[0, 0])
     g = (mask[...] * (a * e1[...] + c1 * h1[...] + c0)).astype(BF)
     g1[...] = g
     mu, rstd, a, b = forward_consts(tot3, inv[0, 0], gb3)
-    first = pl.program_id(0) == 0
     step = 256
     for c in range(0, x.shape[1], step):
         cols = slice(c, c + step)
         up = nt(g, w[cols, :]) + e3[:, cols].astype(F32)
         h = h3[:, cols].astype(F32)
         v = h * a[:, cols] + b[:, cols] + x[:, cols].astype(F32)
-        e = mask[...] * up * slope(v)
+        e = up * (0.5 * slope_twice(0.5 * v))
         down[:, cols] = e.astype(BF)
-        add_stats(st, first, rowsum(e), rowsum(e * (h - mu[:, cols])), cols)
+        add_stats(st, rowsum(e), rowsum(e * h), cols)
 
 
 def reduce_back(sh, e1, h1, tot1, gb1, btot1, inv, mask, w, e3, h3, x, tot3, gb3):
@@ -612,15 +595,14 @@
     )(inv, e1, h1, tot1, gb1, btot1, mask, w, e3, h3, x, tot3, gb3)
 
 
-def features_back_kernel(sh, inv, e1, h1, tot1, gb1, btot1, mask, w, e3, g1, out, scr):
+def features_back_kernel(sh, inv, e1, h1, tot1, gb1, btot1, mask, w, e3, out, scr):
     mu, rstd, a, b = forward_consts(tot1, inv[0, 0], gb1)
     c1, c0 = backward_consts(mu, rstd, a, btot1, inv[0, 0])
     g = (mask[...] * (a * e1[...] + c1 * h1[...] + c0)).astype(BF)
-    g1[...] = g
     step = 512
     for c in range(0, w.shape[0], step):
         cols = slice(c, c + step)
-        up = mask[...] * (nt(g, w[cols, :]) + e3[:, cols].astype(F32))
+        up = nt(g, w[cols, :]) + e3[:, cols].astype(F32)
         scr[:, cols] = up[sh.top :, :]
         for s in range(SIDE):
             out[s, 0 : sh.main, cols] = up[s * sh.main : (s + 1) * sh.main, :]
@@ -643,8 +625,8 @@
             whole((c, m)),
             tile(sh.rows, c),
         ],
-        out_specs=[tile(sh.rows, m), pl.BlockSpec((SIDE, sh.images, c), lambda j: (j, 0, 0))],
-        out_shape=[sds((sh.total, m), BF), sds((SIDE * SIDE, sh.images, c), F32)],
+        out_specs=pl.BlockSpec((SIDE, sh.images, c), lambda j: (j, 0, 0)),
+        out_shape=sds((SIDE * SIDE, sh.images, c), F32),
         scratch_shapes=[pltpu.VMEM((sh.low, c), F32)],
         compiler_params=params(1),
         cost_estimate=cost(2 * sh.total * c * m, 6 * sh.total * c + 10 * sh.total * m),
@@ -678,6 +660,44 @@
     )(left, right)
 
 
+def reduce_wgrad_kernel(inv, e1, h1, tot1, gb1, btot1, mask, x, out, acc):
+    clear_at_first(acc)
+    mu, rstd, a, b = forward_consts(tot1, inv[0, 0], gb1)
+    c1, c0 = backward_consts(mu, rstd, a, btot1, inv[0, 0])
+    g = (mask[...] * (a * e1[...] + c1 * h1[...] + c0)).astype(BF)
+    step = 512
+    for c in range(0, x.shape[1], step):
+        acc[c : c + step, :] += tn(x[:, c : c + step], g)
+
+    @pl.when(pl.program_id(0) == SIDE - 1)
+    def _():
+        out[...] = acc[...].astype(BF)
+
+
+def reduce_wgrad(sh, e1, h1, tot1, gb1, btot1, inv, mask, x):
+    c, m = x.shape[1], e1.shape[1]
+    return pl.pallas_call(
+        reduce_wgrad_kernel,
+        grid=(SIDE,),
+        in_specs=[
+            pl.BlockSpec(memory_space=pltpu.SMEM),
+            tile(sh.rows, m),
+            tile(sh.rows, m),
+            whole((2, m)),
+            whole((2, m)),
+            whole((2, m)),
+            tile(sh.rows, 1),
+            tile(sh.rows, c),
+        ],
+        out_specs=whole((c, m)),
+        out_shape=sds((c, m), BF),
+        scratch_shapes=[pltpu.VMEM((c, m), F32)],
+        compiler_params=params(1),
+        cost_estimate=cost(2 * sh.total * c * m, 2 * sh.total * c + 8 * sh.total * m),
+        name="reduce_wgrad",
+    )(inv, e1, h1, tot1, gb1, btot1, mask, x)
+
+
 def spatial_wgrad_kernel(sh, act, g, out, pat, scr):
     j = pl.program_id(0)
     m = act.shape[1]
@@ -717,15 +737,97 @@
     )(act, g)
 
 
-def total_of(v, devices):
+def assemble_kernel(place, own, mate, out, sem):
+    dps, chips, rows, width = own.shape
+    copies = []
+    for e, src in enumerate((own, mate)):
+        for j in range(dps):
+            for k in range(chips):
+                owner = place[0, 1] ^ (2 * k + e)
+                row = pl.multiple_of(owner * rows, rows)
+                col = pl.multiple_of((place[0, 0] ^ j) * width, width)
+                copies.append(
+                    pltpu.make_async_copy(
+                        src.at[j, k],
+                        out.at[pl.ds(row, rows), pl.ds(col, width)],
+                        sem.at[len(copies)],
+                    )
+                )
+    for copy in copies:
+        copy.start()
+    for copy in copies:
+        copy.wait()
+
+
+def assemble(place, own, mate):
+    dps, chips, rows, width = own.shape
+    anywhere = pl.BlockSpec(memory_space=pl.ANY)
+    return pl.pallas_call(
+        assemble_kernel,
+        in_specs=[pl.BlockSpec(memory_space=pltpu.SMEM), anywhere, anywhere],
+        out_specs=pl.BlockSpec(memory_space=pltpu.VMEM),
+        out_shape=sds((2 * chips * rows, dps * width), BF),
+        scratch_shapes=[pltpu.SemaphoreType.DMA((2 * dps * chips,))],
+        compiler_params=pltpu.CompilerParams(vmem_limit_bytes=VMEM_LIMIT),
+        cost_estimate=cost(0, 8 * own.size),
+        name="assemble",
+    )(place, own, mate)
+
+
+def flips(v, axis, size, unit):
+    return [v] + [
+        lax.ppermute(v, axis, [(i, i ^ (unit * k)) for i in range(size)]) for k in range(1, size // unit)
+    ]
+
+
+def others(v, axis, size, unit):
+    turns = size // unit
+    ways = [
+        [(i, (i // unit + d) % turns * unit + i % unit) for i in range(size)]
+        for d in range(1, turns)
+    ]
+    return sum([lax.ppermute(v, axis, way) for way in ways], v)
+
+
+def total_of(v, sizes):
+    dp, fsdp = sizes
     flat = v.reshape(8, -1)
+    if flat.size > 2048:
+        flat = flat + lax.ppermute(flat, "fsdp", [(i, i ^ 1) for i in range(fsdp)])
+        flat = others(flat, "fsdp", fsdp, 2)
+        return others(flat, "dp", dp, 1).reshape(v.shape)
+    devices = dp * fsdp
     spread = jnp.broadcast_to(flat[None], (devices,) + flat.shape)
     got = lax.all_to_all(spread, AXES, 0, 0, tiled=True)
     return jnp.sum(got, axis=0).reshape(v.shape)
 
 
+def copies_sum(arrays, dp):
+    flat = [v.reshape(-1, 512) for v in arrays]
+    flat = jnp.concatenate(flat, axis=0) if len(flat) > 1 else flat[0]
+    cut = flat.shape[0] // 32 * 16
+    halves = [flat[:cut], flat[cut:]]
+    bits = [1 << k for k in range(dp.bit_length() - 1)]
+    for turn in range(len(bits)):
+        for h in range(2):
+            bit = (bits, bits[::-1])[h][turn]
+            got = lax.ppermute(halves[h], "dp", [(i, i ^ bit) for i in range(dp)])
+            halves[h] = (halves[h].astype(F32) + got.astype(F32)).astype(BF)
+    return halves
+
+
+def copies_out(halves, arrays):
+    flat = jnp.concatenate(halves, axis=0).astype(F32) / SCALE
+    out, at = [], 0
+    for v in arrays:
+        rows = v.size // 512
+        out.append(flat[at : at + rows].reshape(v.shape))
+        at += rows
+    return out
+
+
 def on_device(
-    devices,
+    dp,
     owners,
     features,
     grid_size,
@@ -751,7 +853,12 @@
 
     gather = functools.partial(lax.all_gather, axis_name="fsdp", axis=0, tiled=True)
     weights = [
-        (gather(w_reduce[b]), gather(w_spatial[b]), gather(w_expand[b])) for b in range(blocks)
+        (
+            gather(w_reduce[b]),
+            None if b == 0 and owners == 8 and dp == 4 else gather(w_spatial[b]),
+            gather(w_expand[b]),
+        )
+        for b in range(blocks)
     ]
     sizes = [head.shape[1] for head in (head_a, head_b, head_c)]
     spans = [-(-size // 16) * 16 for size in sizes]
@@ -790,21 +897,41 @@
 
     x = prep(sh, jnp.transpose(features, (1, 0, 2)), mask)
     saved = []
-    h1, part = reduce_conv(sh, x, weights[0][0])
+
+    def in_order(*values):
+        return lax.optimization_barrier(values)
+
+    place = jnp.stack([lax.axis_index("dp"), lax.axis_index("fsdp")]).astype(jnp.int32).reshape(1, 2)
+    short = owners == 8 and dp == 4
+    w1 = weights[0][0]
+    if short:
+        width = inner // dp
+        quarter = lax.dynamic_slice_in_dim(w_spatial[0], place[0, 0] * width, width, 1)
+        x, *column = in_order(x, *flips(quarter, "fsdp", owners, 2))
+        column = jnp.stack(column)
+        own = jnp.stack(flips(column, "dp", dp, 1))
+        w1, own = in_order(w1, own)
+        mate = lax.ppermute(own, "fsdp", [(i, i ^ 1) for i in range(owners)])
+    h1, part = reduce_conv(sh, x, w1)
+    if short:
+        part, mate = in_order(part, mate)
     count = jnp.broadcast_to(jnp.sum(pixel_area), (2, inner))
-    both = total_of(jnp.concatenate([part, count], axis=0), devices)
+    both = total_of(jnp.concatenate([part, count], axis=0), (dp, owners))
+    if short:
+        both, first_spatial = in_order(both, assemble(place, own, mate))
+        weights[0] = (weights[0][0], first_spatial, weights[0][2])
     tot1, live_count = both[:2], both[2, 0]
     inv = (1.0 / live_count).reshape(1, 1)
     for b in range(blocks):
         w1, w2, w3 = weights[b]
         act1, h2, part = spatial_conv(sh, h1, tot1, inv, gb_mid[b, 0], mask, w2)
-        tot2 = total_of(part, devices)
+        tot2 = total_of(part, (dp, owners))
         act2, h3, part = expand_conv(sh, h2, tot2, inv, gb_mid[b, 1], mask, w3)
-        tot3 = total_of(part, devices)
+        tot3 = total_of(part, (dp, owners))
         saved.append((x, h1, tot1, act1, h2, tot2, act2, h3, tot3))
         if b + 1 < blocks:
             x, h1, part = join(sh, h3, x, tot3, inv, gb_out[b], mask, weights[b + 1][0])
-            tot1 = total_of(part, devices)
+            tot1 = total_of(part, (dp, owners))
     trunk, pooled = last_join(sh, h3, x, tot3, inv, gb_out[-1], mask, area, pick)
     merged, grad_logits = heads(
         pooled, labels, area, bits, head_all, sizes, offsets, sum(lanes)
@@ -820,10 +947,13 @@
     all_logits = gather(grad_logits)
     head_grad = tn(all_logits, mine).astype(BF)
 
+    def in_order(*values):
+        return lax.optimization_barrier(values)
+
     e3, part = top_grad(sh, merged, h3, x, tot3, inv, gb_out[-1], mask)
-    btot3 = total_of(part, devices)
+    btot3 = total_of(part, (dp, owners))
     scatter = functools.partial(lax.psum_scatter, axis_name="fsdp", scatter_dimension=0, tiled=True)
-    reduce_grads, spatial_grads, expand_grads = [], [], []
+    shards = {}
     sums_mid, sums_out = [], []
     for b in reversed(range(blocks)):
         w1, w2, w3 = weights[b]
@@ -831,13 +961,21 @@
         g3, e2, part = expand_back(
             sh, e3, h3, tot3, gb_out[b], btot3, inv, mask, w3, h2, tot2, gb_mid[b, 1]
         )
-        btot2 = total_of(part, devices)
-        expand_grads.insert(0, scatter(wgrad(act2, g3, inner)))
+        grad = wgrad(act2, g3, inner)
+        btot2 = total_of(part, (dp, owners))
+        btot2, grad = in_order(btot2, grad)
+        shards["expand", b] = scatter(grad)
         g2, e1, part = spatial_back(
             sh, e2, h2, tot2, gb_mid[b, 1], btot2, inv, mask, w2, h1, tot1, gb_mid[b, 0]
         )
-        btot1 = total_of(part, devices)
-        spatial_grads.insert(0, scatter(spatial_wgrad(sh, act1, g2)))
+        grad = spatial_wgrad(sh, act1, g2)
+        if b + 1 < blocks:
+            early = [head_grad] + [shards[k, b + 1] for k in ("reduce", "spatial", "expand")]
+            part, *early = in_order(part, *early)
+            early_halves = copies_sum(early, dp)
+        btot1 = total_of(part, (dp, owners))
+        btot1, grad = in_order(btot1, grad)
+        shards["spatial", b] = scatter(grad)
         sums_out.insert(0, (btot3, tot3))
         sums_mid.insert(0, ((btot1, tot1), (btot2, tot2)))
         if b > 0:
@@ -845,36 +983,50 @@
             g1, e3, part = reduce_back(
                 sh, e1, h1, tot1, gb_mid[b, 0], btot1, inv, mask, w1, e3, h3p, xp, tot3p, gb_out[b - 1]
             )
-            btot3 = total_of(part, devices)
+            grad = wgrad(x, g1, inner)
+            btot3 = total_of(part, (dp, owners))
+            btot3, grad = in_order(btot3, grad)
+            shards["reduce", b] = scatter(grad)
         else:
-            g1, grad_features = features_back(
+            grad = reduce_wgrad(sh, e1, h1, tot1, gb_mid[b, 0], btot1, inv, mask, x)
+            e3, grad = in_order(e3, grad)
+            shards["reduce", b] = scatter(grad)
+            grad_features = features_back(
                 sh, e1, h1, tot1, gb_mid[b, 0], btot1, inv, mask, w1, e3
             )
-        reduce_grads.insert(0, scatter(wgrad(x, g1, inner)))
-
-    reduced = lax.psum(
-        (jnp.stack(reduce_grads), jnp.stack(spatial_grads), jnp.stack(expand_grads), head_grad), "dp"
-    )
-    finals = [v.astype(F32) / SCALE for v in reduced]
+            (
+                grad_features,
+                shards["expand", b],
+                shards["spatial", b],
+                shards["reduce", b],
+            ) = in_order(
+                grad_features, shards["expand", b], shards["spatial", b], shards["reduce", b]
+            )
+
+    groups = [early, [shards["expand", 0], shards["spatial", 0]], [shards["reduce", 0]]]
+    halves = [early_halves, copies_sum(groups[1], dp), copies_sum(groups[2], dp)]
+    sums = [copies_out(h, g) for h, g in zip(halves, groups)]
+    head_grad, reduce_one, spatial_one, expand_one = sums[0]
+    (expand_zero, spatial_zero), (reduce_zero,) = sums[1:]
     at = [(place, size) for place, size in zip(offsets, sizes)]
 
     def gains(pair):
         btot, tot = pair
         mu = tot[0] / live_count
         var = jnp.maximum(tot[1] / live_count - mu * mu, 0.0)
-        return btot[1] * lax.rsqrt(var + EPS) / SCALE
+        return (btot[1] - mu * btot[0]) * lax.rsqrt(var + EPS) / SCALE
 
     return (
         jnp.transpose(trunk, (1, 0, 2)),
         jnp.transpose(grad_features, (1, 0, 2)),
-        finals[0],
-        finals[1],
-        finals[2],
+        jnp.stack([reduce_zero, reduce_one]),
+        jnp.stack([spatial_zero, spatial_one]),
+        jnp.stack([expand_zero, expand_one]),
         jnp.stack([jnp.stack([gains(p) for p in pairs]) for pairs in sums_mid]),
         jnp.stack([jnp.stack([p[0][0] / SCALE for p in pairs]) for pairs in sums_mid]),
         jnp.stack([gains(p) for p in sums_out]),
         jnp.stack([p[0][0] / SCALE for p in sums_out]),
-    ) + tuple(finals[3][place : place + size].T for place, size in at)
+    ) + tuple(head_grad[place : place + size].T for place, size in at)
 
 
 def solution(mesh):
@@ -888,5 +1040,5 @@
     out_specs = (
         P(AXES, None, None), P(AXES, None, None), rows, rows, rows, P(), P(), P(), P(), head, head, head,
     )
-    body = functools.partial(on_device, mesh.size, mesh.shape["fsdp"])
+    body = functools.partial(on_device, mesh.shape["dp"], mesh.shape["fsdp"])
     return jax.shard_map(body, mesh=mesh, in_specs=in_specs, out_specs=out_specs, check_vma=False)

time: 859 us -> 704 us (0.82)
  waiting for transfers between devices: 325 us -> 188 us
  blocking collectives: 138 us -> 31.5 us
  starting transfers between devices: 12.5 us -> 95.4 us
  local copies, waits for them, and re-layouts: 30.5 us -> 45.9 us
    all_to_all x9 -> x2, blocking collectives: 127 us -> 31.5 us  [total_of(): got = lax.all_to_all(spread, AXES, 0, 0, tiled=True)]
    ppermute x0 -> x47, waiting for transfers between devices: none -> 87 us  [the longest x12 36.7 us: copies_sum(): got = lax.ppermute(halves[h], 'dp', [(i, i ^ bit) for i in range(dp)])]
    psum x1 -> x0, waiting for transfers between devices: 80.5 us -> none  [on_device(): lax.psum((jnp.stack(reduce_grads), jnp.stack(spatial_grads), jnp.stack(ex...]
    ppermute x0 -> x47, starting transfers between devices: none -> 60.2 us  [the longest x24 33.6 us: others(): return sum([lax.ppermute(v, axis, way) for way in ways], v)]
    all_to_all x3 -> x6, waiting for transfers between devices: 67.8 us -> 20.7 us  [total_of(): got = lax.all_to_all(spread, AXES, 0, 0, tiled=True)]
    all_gather x2 -> x1, waiting for transfers between devices: 44.2 us -> 0.01 us  [on_device(): gather(w_spatial[b])]
    reduce_scatter x6, waiting for transfers between devices: 102 us -> 78.1 us  [the longest x2 78 us: on_device(): shards['spatial', b] = scatter(grad)]
    all_to_all x3 -> x6, starting transfers between devices: 10.9 us -> 30.5 us  [total_of(): got = lax.all_to_all(spread, AXES, 0, 0, tiled=True)]
  transfers between devices with their start and end apart: 18 -> 67, of which waited for: 12 -> 35; matrix products, arithmetic and copies ran while one was open for 5% -> 7% of each run, Pallas kernels for 35% -> 42%
where the time goes in v2:
time: 704 us; the launch traced here: 692 us
  Pallas kernels  296 us (42%)
  waiting for transfers between devices  188 us (27%)
  starting transfers between devices  95.4 us (14%)
  local copies, waits for them, and re-layouts  45.9 us (7%)
  blocking collectives  31.5 us (4%)
  other arithmetic  17.2 us (2%)
  between operations  16 us (2%)
    reduce_scatter x2, waiting for transfers between devices, on_device(): shards['spatial', b] = scatter(grad)  78 us
    ppermute x12, waiting for transfers between devices, copies_sum(): got = lax.ppermute(halves[h], 'dp', [(i, i ^ bit) for i in range(dp)])  36.7 us
    pallas_call x2, Pallas kernels, spatial_back(): pl.pallas_call(functools.partial(spatial_back_kernel, sh), grid=(SIDE + 1...  34.9 us
    ppermute x24, starting transfers between devices, others(): return sum([lax.ppermute(v, axis, way) for way in ways], v)  33.6 us
    pallas_call x2, Pallas kernels, spatial_conv(): pl.pallas_call(functools.partial(spatial_kernel, sh), grid=(SIDE + 1,), i...  32.7 us
    pallas_call x2, Pallas kernels, expand_back(): pl.pallas_call(expand_back_kernel, grid=(SIDE,), in_specs=[pl.BlockSpec(m...  31.7 us
    all_to_all x2, blocking collectives, total_of(): got = lax.all_to_all(spread, AXES, 0, 0, tiled=True)  31.5 us
    all_to_all x6, starting transfers between devices, total_of(): got = lax.all_to_all(spread, AXES, 0, 0, tiled=True)  30.5 us
  transfers between devices with their start and end apart: 67, of which 35 were waited for; matrix products, arithmetic and copies ran while one was open for 7% of the time, Pallas kernels for 42%

profile of v2, /device:TPU:0, one launch (start us, length us, event | category | flops | bytes accessed | tf_op | source)
XLA Modules:
  0.0 691.9 jit_solution(15426798774918535666)
XLA Ops:
  14.7 3.1 collective-permute-start
  17.8 2.6 collective-permute-start.1
  22.1 9.6 %prep.1.x = bf16[1792,2048]{1,0:T(8,128)(2,1)} custom-call(bf16[49,36,2048]{2,1,0:T(8,128)(2,1)} %bitcast.131, f32[1792,1]{1,0:T(8,128)} %bitcast.109), custom_call_target="tpu_custom_call" | custom-call | tf_op jit(solution)/shard_map/prep/pallas_call | solution.py:126
  31.7 5.5 collective-permute-done.1
  40.9 12.8 %collective-permute-done.3 = bf16[4,576,128]{2,1,0:T(8,128)(2,1)S(1)} collective-permute-done((bf16[4,576,128]{2,1,0:T(8,128)(2,1)S(1)}, bf16[4,576,128]{2,1,0:T(8,128)(2,1)S(1)}, u32[]{:S(2)}, u32[]{:S(2)}) %collective-permute-start.3) | collective-permute-done | bytes 589856 | tf_op jit(solution)/shard_map/ppermute | solution.py:779
  53.6 8.7 %collective-permute-done.4 = bf16[4,576,128]{2,1,0:T(8,128)(2,1)S(1)} collective-permute-done((bf16[4,576,128]{2,1,0:T(8,128)(2,1)S(1)}, bf16[4,576,128]{2,1,0:T(8,128)(2,1)S(1)}, u32[]{:S(2)}, u32[]{:S(2)}) %collective-permute-start.4) | collective-permute-done | bytes 589856 | tf_op jit(solution)/shard_map/ppermute | solution.py:779
  63.5 9.9 %reduce_conv.1 = (f32[1792,512]{1,0:T(8,128)}, f32[2,512]{1,0:T(2,128)}) custom-call(bf16[1792,2048]{1,0:T(8,128)(2,1)} %prep.1.x, bf16[2048,512]{1,0:T(8,128)(2,1)} %bitcast.136), custom_call_target="tpu_custom_call" | custom-call | flops 3758096384 | bytes 11010048 | tf_op jit(solution)/shard_map/reduce_conv/pallas_call | solution.py:150
  76.9 10.6 %all-to-all-start = ((f32[32,8,256]{2,1,0:T(8,128)}), f32[32,8,256]{2,1,0:T(8,128)S(1)}, u32[]{:S(2)}, u32[]{:S(2)}) async-start(f32[32,8,256]{2,1,0:T(8,128)} %broadcast_in_dim.67), calls=%async_computation | async-start | bytes 524288 | tf_op jit(solution)/shard_map/all_to_all | solution.py:801
  88.2 5.7 assemble.1.w
  93.9 4.1 all-to-all-done
  99.8 16.4 %spatial_conv.2 = (bf16[1792,512]{1,0:T(8,128)(2,1)}, f32[1792,512]{1,0:T(8,128)}, f32[2,512]{1,0:T(2,128)}) custom-call(f32[1,1]{1,0:T(1,128)} %bitcast.18.inv, f32[1792,512]{1,0:T(8,128)} %get-tuple-element.93.h1, f32[2,512]{1,0:T(2,128)} %slice.221.tot.tot1, f32[2,512]{1,0:T(2,128)} %get-tuple-element.179.gb.gb1, f32[1792,1]{1,0:T(8,128)} %bitcast.110, ...), custom_call_target="tpu_custom_call" | custom-call | flops 8455716864 | bytes 13893632 | tf_op jit(solution)/shard_map/spatial_conv/pallas_call | solution.py:203
  116.9 15.2 %all_to_all.45 = f32[32,8,128]{2,1,0:T(8,128)S(1)} all-to-all(f32[32,8,128]{2,1,0:T(8,128)S(1)} %broadcast_in_dim.69), channel_id=1, replica_groups=mesh['dp'=4,'fsdp'=8] {'dp','fsdp'}, dimensions={0} | all-to-all | bytes 262144 | tf_op jit(solution)/shard_map/all_to_all | solution.py:801
  132.8 10.7 %expand_conv.2 = (bf16[1792,512]{1,0:T(8,128)(2,1)}, bf16[1792,2048]{1,0:T(8,128)(2,1)}, f32[2,2048]{1,0:T(2,128)}) custom-call(f32[1,1]{1,0:T(1,128)} %bitcast.18.inv, f32[1792,512]{1,0:T(8,128)} %get-tuple-element.95.h2, f32[2,512]{1,0:T(2,128)} %reshape.509.tot.tot2, f32[2,512]{1,0:T(2,128)} %get-tuple-element.180.gb.gb2, f32[1792,1]{1,0:T(8,128)} %bitcast.112, ...), custom_call_target="tpu_custom_call" | custom-call | flops 3758096384 | bytes 12845056 | tf_op jit(solution)/shard_map/expand_conv/pallas_call | solution.py:246
  146.4 2.8 collective-permute-start.10
  150.9 4.2 collective-permute-done.8
  163.0 14.6 %join.1 = (bf16[1792,2048]{1,0:T(8,128)(2,1)}, f32[1792,512]{1,0:T(8,128)}, f32[2,512]{1,0:T(2,128)}) custom-call(f32[1,1]{1,0:T(1,128)} %bitcast.18.inv, bf16[1792,2048]{1,0:T(8,128)(2,1)} %get-tuple-element.97.h3, bf16[1792,2048]{1,0:T(8,128)(2,1)} %prep.1.x, f32[2,2048]{1,0:T(2,128)} %reshape.511.tot.tot3, f32[2,2048]{1,0:T(2,128)} %get-tuple-element.171.gb.gb3, ...), custom_call_target="tpu_custom_call" | custom-call | flops 3758096384 | bytes 25690112 | tf_op jit(solution)/shard_map/join/pallas_call | solution.py:283
  178.3 16.2 %all_to_all.46 = f32[32,8,128]{2,1,0:T(8,128)S(1)} all-to-all(f32[32,8,128]{2,1,0:T(8,128)S(1)} %broadcast_in_dim.71), channel_id=1, replica_groups=mesh['dp'=4,'fsdp'=8] {'dp','fsdp'}, dimensions={0} | all-to-all | bytes 262144 | tf_op jit(solution)/shard_map/all_to_all | solution.py:801
  195.2 16.4 %spatial_conv.3 = (bf16[1792,512]{1,0:T(8,128)(2,1)}, f32[1792,512]{1,0:T(8,128)}, f32[2,512]{1,0:T(2,128)}) custom-call(f32[1,1]{1,0:T(1,128)} %bitcast.18.inv, f32[1792,512]{1,0:T(8,128)} %get-tuple-element.99.h1, f32[2,512]{1,0:T(2,128)} %reshape.512.tot.tot1, f32[2,512]{1,0:T(2,128)} %get-tuple-element.181.gb.gb1, f32[1792,1]{1,0:T(8,128)} %bitcast.114, ...), custom_call_target="tpu_custom_call" | custom-call | flops 8455716864 | bytes 13893632 | tf_op jit(solution)/shard_map/spatial_conv/pallas_call | solution.py:203
  212.9 2.6 all-to-all-start.3
  216.2 15.1 %all-to-all-done.3 = f32[32,8,128]{2,1,0:T(8,128)S(1)} async-done(((f32[32,8,128]{2,1,0:T(8,128)}), f32[32,8,128]{2,1,0:T(8,128)S(1)}, u32[]{:S(2)}, u32[]{:S(2)}) %all-to-all-start.3) | async-done | bytes 131104 | tf_op jit(solution)/shard_map/all_to_all | solution.py:801
  232.0 10.8 %expand_conv.3 = (bf16[1792,512]{1,0:T(8,128)(2,1)}, bf16[1792,2048]{1,0:T(8,128)(2,1)}, f32[2,2048]{1,0:T(2,128)}) custom-call(f32[1,1]{1,0:T(1,128)} %bitcast.18.inv, f32[1792,512]{1,0:T(8,128)} %get-tuple-element.101.h2, f32[2,512]{1,0:T(2,128)} %reshape.513.tot.tot2, f32[2,512]{1,0:T(2,128)} %get-tuple-element.178.gb.gb2, f32[1792,1]{1,0:T(8,128)} %bitcast.116, ...), custom_call_target="tpu_custom_call" | custom-call | flops 3758096384 | bytes 12845056 | tf_op jit(solution)/shard_map/expand_conv/pallas_call | solution.py:246
  244.8 3.7 collective-permute-start.17
  260.3 13.5 %last_join.1 = (bf16[49,36,2048]{2,1,0:T(8,128)(2,1)}, bf16[48,2048]{1,0:T(8,128)(2,1)}) custom-call(f32[1,1]{1,0:T(1,128)} %bitcast.18.inv, bf16[1792,2048]{1,0:T(8,128)(2,1)} %get-tuple-element.103.h3, bf16[1792,2048]{1,0:T(8,128)(2,1)} %get-tuple-element.104.x.left, f32[2,2048]{1,0:T(2,128)} %reshape.515.tot.tot3, f32[2,2048]{1,0:T(2,128)} %get-tuple-element.170.gb.gb3, ...), custom_call_target="tpu_custom_call" | custom-call | flops 352321536 | bytes 22020096 | tf_op jit(solution)/shard_map/last_join/pallas_call | solution.py:326
  273.8 7.9 %heads.1 = (f32[48,2048]{1,0:T(8,128)}, bf16[48,1536]{1,0:T(8,128)(2,1)}) custom-call(bf16[48,2048]{1,0:T(8,128)(2,1)} %get-tuple-element.107.pooled, s32[48,3]{1,0:T(8,128)} %pad.26.labels, f32[48,1]{1,0:T(8,128)} %copy.96.area, s32[48,2048]{1,0:T(8,128)} %pad.27.bits, bf16[1424,2048]{1,0:T(8,128)(2,1)} %all-gather.13.cloned.1.call-done.w), custom_call_target="tpu_custom_call" | custom-call | flops 603979776 | bytes 5832704 | tf_op jit(solution)/shard_map/heads/pallas_call | solution.py:382
  281.7 16.2 %top_grad.1 = (bf16[1792,2048]{1,0:T(8,128)(2,1)}, f32[2,2048]{1,0:T(2,128)}) custom-call(f32[1,1]{1,0:T(1,128)} %bitcast.18.inv, f32[48,2048]{1,0:T(8,128)} %get-tuple-element.108.merged, bf16[1792,2048]{1,0:T(8,128)(2,1)} %get-tuple-element.103.h3, bf16[1792,2048]{1,0:T(8,128)(2,1)} %get-tuple-element.104.x.left, f32[2,2048]{1,0:T(2,128)} %reshape.515.tot.tot3, ...), custom_call_target="tpu_custom_call" | custom-call | flops 73400320 | bytes 22020096 | tf_op jit(solution)/shard_map/top_grad/pallas_call | solution.py:415
  301.1 2.6 collective-permute-start.24
  313.1 15.7 %expand_back.2 = (bf16[1792,2048]{1,0:T(8,128)(2,1)}, f32[1792,512]{1,0:T(8,128)}, f32[2,512]{1,0:T(2,128)}) custom-call(f32[1,1]{1,0:T(1,128)} %bitcast.18.inv, bf16[1792,2048]{1,0:T(8,128)(2,1)} %get-tuple-element.109.e3, bf16[1792,2048]{1,0:T(8,128)(2,1)} %get-tuple-element.103.h3, f32[2,2048]{1,0:T(2,128)} %reshape.515.tot.tot3, ...), custom_call_target="tpu_custom_call" | custom-call | flops 3758096384 | bytes 29360128 | tf_op jit(solution)/shard_map/expand_back/pallas_call | solution.py:458
  330.2 4.7 all-to-all-start.4
  335.0 8.2 %wgrad.3 = bf16[512,2048]{1,0:T(8,128)(2,1)} custom-call(bf16[1792,512]{1,0:T(8,128)(2,1)} %get-tuple-element.113.left, bf16[1792,2048]{1,0:T(8,128)(2,1)} %get-tuple-element.114.right), custom_call_target="tpu_custom_call" | custom-call | flops 3758096384 | bytes 11272192 | tf_op jit(solution)/shard_map/wgrad/pallas_call | solution.py:651
  343.8 17.5 %spatial_back.2 = (bf16[1792,512]{1,0:T(8,128)(2,1)}, f32[1792,512]{1,0:T(8,128)}, f32[2,512]{1,0:T(2,128)}) custom-call(f32[1,1]{1,0:T(1,128)} %bitcast.18.inv, f32[1792,512]{1,0:T(8,128)} %get-tuple-element.111.e2, f32[1792,512]{1,0:T(8,128)} %get-tuple-element.101.h2, f32[2,512]{1,0:T(2,128)} %reshape.513.tot.tot2, f32[2,512]{1,0:T(2,128)} %get-tuple-element.178.gb.gb2, ...), custom_call_target="tpu_custom_call" | custom-call | flops 8455716864 | bytes 21233664 | tf_op jit(solution)/shard_map/spatial_back/pallas_call | solution.py:517
  362.7 5.8 all-to-all-start.5
  368.7 12.5 %spatial_wgrad.2 = bf16[4608,512]{1,0:T(8,128)(2,1)} custom-call(bf16[1792,512]{1,0:T(8,128)(2,1)} %get-tuple-element.118.act, bf16[1792,512]{1,0:T(8,128)(2,1)} %get-tuple-element.119.g), custom_call_target="tpu_custom_call" | custom-call | flops 8455716864 | bytes 8388608 | tf_op jit(solution)/shard_map/spatial_wgrad/pallas_call | solution.py:724
  381.9 19.7 %reduce_back.1 = (bf16[1792,512]{1,0:T(8,128)(2,1)}, bf16[1792,2048]{1,0:T(8,128)(2,1)}, f32[2,2048]{1,0:T(2,128)}) custom-call(f32[1,1]{1,0:T(1,128)} %bitcast.18.inv, f32[1792,512]{1,0:T(8,128)} %get-tuple-element.116.e1, f32[1792,512]{1,0:T(8,128)} %get-tuple-element.99.h1, f32[2,512]{1,0:T(2,128)} %reshape.512.tot.tot1, ...), custom_call_target="tpu_custom_call" | custom-call | flops 3758096384 | bytes 38535168 | tf_op jit(solution)/shard_map/reduce_back/pallas_call | solution.py:572
  415.9 8.1 %wgrad.4 = bf16[2048,512]{1,0:T(8,128)(2,1)} custom-call(bf16[1792,2048]{1,0:T(8,128)(2,1)} %get-tuple-element.104.x.left, bf16[1792,512]{1,0:T(8,128)(2,1)} %get-tuple-element.123.right), custom_call_target="tpu_custom_call" | custom-call | flops 3758096384 | bytes 11272192 | tf_op jit(solution)/shard_map/wgrad/pallas_call | solution.py:651
  425.3 16.0 %expand_back.3 = (bf16[1792,2048]{1,0:T(8,128)(2,1)}, f32[1792,512]{1,0:T(8,128)}, f32[2,512]{1,0:T(2,128)}) custom-call(f32[1,1]{1,0:T(1,128)} %bitcast.18.inv, bf16[1792,2048]{1,0:T(8,128)(2,1)} %get-tuple-element.140.e3, bf16[1792,2048]{1,0:T(8,128)(2,1)} %get-tuple-element.97.h3, f32[2,2048]{1,0:T(2,128)} %reshape.511.tot.tot3, ...), custom_call_target="tpu_custom_call" | custom-call | flops 3758096384 | bytes 29360128 | tf_op jit(solution)/shard_map/expand_back/pallas_call | solution.py:458
  442.7 3.7 all-to-all-start.6
  446.7 8.2 %wgrad.5 = bf16[512,2048]{1,0:T(8,128)(2,1)} custom-call(bf16[1792,512]{1,0:T(8,128)(2,1)} %get-tuple-element.127.left, bf16[1792,2048]{1,0:T(8,128)(2,1)} %get-tuple-element.128.right), custom_call_target="tpu_custom_call" | custom-call | flops 3758096384 | bytes 11272192 | tf_op jit(solution)/shard_map/wgrad/pallas_call | solution.py:651
  457.8 3.7 all-to-all-start.7
  461.4 17.4 %spatial_back.3 = (bf16[1792,512]{1,0:T(8,128)(2,1)}, f32[1792,512]{1,0:T(8,128)}, f32[2,512]{1,0:T(2,128)}) custom-call(f32[1,1]{1,0:T(1,128)} %bitcast.18.inv, f32[1792,512]{1,0:T(8,128)} %get-tuple-element.125.e2, f32[1792,512]{1,0:T(8,128)} %get-tuple-element.95.h2, f32[2,512]{1,0:T(2,128)} %reshape.509.tot.tot2, f32[2,512]{1,0:T(2,128)} %get-tuple-element.180.gb.gb2, ...), custom_call_target="tpu_custom_call" | custom-call | flops 8455716864 | bytes 21233664 | tf_op jit(solution)/shard_map/spatial_back/pallas_call | solution.py:517
  480.9 36.6 %reduce-scatter.9.cloned.1.call-done = bf16[576,512]{1,0:T(8,128)(2,1)} async-done(((bf16[4608,512]{1,0:T(8,128)(2,1)}), bf16[576,512]{1,0:T(8,128)(2,1)}) %reduce-scatter.9.cloned.1.call-update) | async-done | bytes 589840 | tf_op jit(solution)/shard_map/reduce_scatter | solution.py:978
  518.2 3.0 all-to-all-start.8
  521.2 12.5 %spatial_wgrad.3 = bf16[4608,512]{1,0:T(8,128)(2,1)} custom-call(bf16[1792,512]{1,0:T(8,128)(2,1)} %get-tuple-element.137.act, bf16[1792,512]{1,0:T(8,128)(2,1)} %get-tuple-element.138.g), custom_call_target="tpu_custom_call" | custom-call | flops 8455716864 | bytes 8388608 | tf_op jit(solution)/shard_map/spatial_wgrad/pallas_call | solution.py:724
  534.3 11.7 %reduce_wgrad.1 = bf16[2048,512]{1,0:T(8,128)(2,1)} custom-call(f32[1,1]{1,0:T(1,128)} %bitcast.18.inv, f32[1792,512]{1,0:T(8,128)} %get-tuple-element.130.e1, f32[1792,512]{1,0:T(8,128)} %get-tuple-element.93.h1, f32[2,512]{1,0:T(2,128)} %slice.221.tot.tot1, f32[2,512]{1,0:T(2,128)} %get-tuple-element.179.gb.gb1, f32[2,512]{1,0:T(2,128)} %reshape.525.btot1, ...), custom_call_target="tpu_custom_call" | custom-call | flops 3758096384 | bytes 14680064 | tf_op jit(solution)/shard_map/reduce_wgrad/pallas_call | solution.py:679
  554.9 18.0 %collective-permute-done.39 = bf16[928,512]{1,0:T(8,128)(2,1)S(1)} collective-permute-done((bf16[928,512]{1,0:T(8,128)(2,1)S(1)}, bf16[928,512]{1,0:T(8,128)(2,1)S(1)}, u32[]{:S(2)}, u32[]{:S(2)}) %collective-permute-start.39) | collective-permute-done | bytes 950304 | tf_op jit(solution)/shard_map/ppermute | solution.py:814
  578.0 16.8 %features_back.1 = f32[49,36,2048]{2,1,0:T(8,128)} custom-call(f32[1,1]{1,0:T(1,128)} %bitcast.18.inv, f32[1792,512]{1,0:T(8,128)} %get-tuple-element.130.e1, f32[1792,512]{1,0:T(8,128)} %get-tuple-element.93.h1, f32[2,512]{1,0:T(2,128)} %slice.221.tot.tot1, f32[2,512]{1,0:T(2,128)} %get-tuple-element.179.gb.gb1, f32[2,512]{1,0:T(2,128)} %reshape.525.btot1, ...), custom_call_target="tpu_custom_call" | custom-call | flops 3758096384 | bytes 31195136 | tf_op jit(solution)/shard_map/features_back/pallas_call | solution.py:614
  605.8 41.4 %reduce-scatter.15.cloned.1.call-done = bf16[576,512]{1,0:T(8,128)(2,1)} async-done(((bf16[4608,512]{1,0:T(8,128)(2,1)}), bf16[576,512]{1,0:T(8,128)(2,1)}) %reduce-scatter.15.cloned.1.call-update) | async-done | bytes 589840 | tf_op jit(solution)/shard_map/reduce_scatter | solution.py:978
  662.2 6.9 collective-permute-done.38
  672.2 5.2 collective-permute-done.44
  (334 shorter events, 141.2 us)
Async XLA Ops:
  7.2 55.5 %all-gather.17.cloned.1.call-start = ((), (), s32[]{:S(2)}) async-start(), calls=%async_computation.23 | async-start | bytes 2359296 | tf_op jit(solution)/shard_map/all_gather | solution.py:857
  9.2 123.6 %all-gather.19.cloned.1.call-start = ((), (), s32[]{:S(2)}) async-start(), calls=%async_computation.24 | async-start | bytes 2359296 | tf_op jit(solution)/shard_map/all_gather | solution.py:859
  11.2 151.8 %all-gather.21.cloned.1.call-start = ((), (), s32[]{:S(2)}) async-start(), calls=%async_computation.25 | async-start | bytes 2359296 | tf_op jit(solution)/shard_map/all_gather | solution.py:857
  12.0 183.2 %all-gather.23.cloned.1.call-start = ((), (), s32[]{:S(2)}) async-start(), calls=%async_computation.26 | async-start | bytes 5308416 | tf_op jit(solution)/shard_map/all_gather | solution.py:858
  12.9 219.0 %all-gather.25.cloned.1.call-start = ((), (), s32[]{:S(2)}) async-start(), calls=%async_computation.27 | async-start | bytes 2359296 | tf_op jit(solution)/shard_map/all_gather | solution.py:859
  13.5 260.3 %all-gather.13.cloned.1.call-start = ((), (), s32[]{:S(2)}) async-start(), calls=%async_computation.15 | async-start | bytes 6561792 | tf_op jit(solution)/shard_map/all_gather | solution.py:874
  14.7 17.0 %collective-permute-start = (bf16[576,128]{1,0:T(8,128)(2,1)S(1)}, bf16[576,128]{1,0:T(8,128)(2,1)S(1)}, u32[]{:S(2)}, u32[]{:S(2)}) collective-permute-start(bf16[576,128]{1,0:T(8,128)(2,1)S(1)} %dynamic-slice_bitcast_fusion), channel_id=1, source_target_pairs={{0,2},{1,3},{2,0},{3,1},{4,6},{5,7},{6,4},{7,5},{8,10},{9,11},{10,... | collective-permute-start | bytes 442376 | tf_op jit(solution)/shard_map/ppermute | solution.py:779
  17.8 19.4 %collective-permute-start.1 = (bf16[576,128]{1,0:T(8,128)(2,1)S(1)}, bf16[576,128]{1,0:T(8,128)(2,1)S(1)}, u32[]{:S(2)}, u32[]{:S(2)}) collective-permute-start(bf16[576,128]{1,0:T(8,128)(2,1)S(1)} %dynamic-slice_bitcast_fusion), channel_id=1, source_target_pairs={{0,4},{1,5},{2,6},{3,7},{4,0},{5,1},{6,2},{7,3},{8,12},{9,13},{10,... | collective-permute-start | bytes 442376 | tf_op jit(solution)/shard_map/ppermute | solution.py:779
  20.4 16.8 %collective-permute-start.2 = (bf16[576,128]{1,0:T(8,128)(2,1)S(1)}, bf16[576,128]{1,0:T(8,128)(2,1)S(1)}, u32[]{:S(2)}, u32[]{:S(2)}) collective-permute-start(bf16[576,128]{1,0:T(8,128)(2,1)S(1)} %dynamic-slice_bitcast_fusion), channel_id=1, source_target_pairs={{0,6},{1,7},{2,4},{3,5},{4,2},{5,3},{6,0},{7,1},{8,14},{9,15},{10,... | collective-permute-start | bytes 442376 | tf_op jit(solution)/shard_map/ppermute | solution.py:779
  37.3 16.3 %collective-permute-start.3 = (bf16[4,576,128]{2,1,0:T(8,128)(2,1)S(1)}, bf16[4,576,128]{2,1,0:T(8,128)(2,1)S(1)}, u32[]{:S(2)}, u32[]{:S(2)}) collective-permute-start(bf16[4,576,128]{2,1,0:T(8,128)(2,1)S(1)} %get-tuple-element.159), channel_id=1, source_target_pairs={{0,8},{8,0},{16,24},{24,16},{1,9},{9,1},{17,25},{25,17},{2,10},{10... | collective-permute-start | bytes 1769480 | tf_op jit(solution)/shard_map/ppermute | solution.py:779
  38.9 23.4 %collective-permute-start.4 = (bf16[4,576,128]{2,1,0:T(8,128)(2,1)S(1)}, bf16[4,576,128]{2,1,0:T(8,128)(2,1)S(1)}, u32[]{:S(2)}, u32[]{:S(2)}) collective-permute-start(bf16[4,576,128]{2,1,0:T(8,128)(2,1)S(1)} %get-tuple-element.159), channel_id=1, source_target_pairs={{0,16},{8,24},{16,0},{24,8},{1,17},{9,25},{17,1},{25,9},{2,18},{10... | collective-permute-start | bytes 1769480 | tf_op jit(solution)/shard_map/ppermute | solution.py:779
  40.4 21.9 %collective-permute-start.5 = (bf16[4,576,128]{2,1,0:T(8,128)(2,1)S(1)}, bf16[4,576,128]{2,1,0:T(8,128)(2,1)S(1)}, u32[]{:S(2)}, u32[]{:S(2)}) collective-permute-start(bf16[4,576,128]{2,1,0:T(8,128)(2,1)S(1)} %get-tuple-element.159), channel_id=1, source_target_pairs={{0,24},{8,16},{16,8},{24,0},{1,25},{9,17},{17,9},{25,1},{2,26},{10... | collective-permute-start | bytes 1769480 | tf_op jit(solution)/shard_map/ppermute | solution.py:779
  62.7 10.8 %collective-permute-start.6 = (bf16[4,4,576,128]{3,2,1,0:T(8,128)(2,1)S(1)}, bf16[4,4,576,128]{3,2,1,0:T(8,128)(2,1)S(1)}, u32[]{:S(2)}, u32[]{:S(2)}) collective-permute-start(bf16[4,4,576,128]{3,2,1,0:T(8,128)(2,1)S(1)} %pad_maximum_fusion.own), channel_id=1, source_target_pairs={{0,1},{1,0},{2,3},{3,2},{4,5},{5,4},{6,7},{7,6},{8,9},{9,8},{10,11... | collective-permute-start | bytes 7077896 | tf_op jit(solution)/shard_map/ppermute | solution.py:914
  76.9 21.0 %all-to-all-start = ((f32[32,8,256]{2,1,0:T(8,128)}), f32[32,8,256]{2,1,0:T(8,128)S(1)}, u32[]{:S(2)}, u32[]{:S(2)}) async-start(f32[32,8,256]{2,1,0:T(8,128)} %broadcast_in_dim.67), calls=%async_computation | async-start | bytes 524288 | tf_op jit(solution)/shard_map/all_to_all | solution.py:801
  149.2 5.9 collective-permute-start.8
  149.2 6.6 collective-permute-start.9
  212.9 18.4 %all-to-all-start.3 = ((f32[32,8,128]{2,1,0:T(8,128)}), f32[32,8,128]{2,1,0:T(8,128)S(1)}, u32[]{:S(2)}, u32[]{:S(2)}) async-start(f32[32,8,128]{2,1,0:T(8,128)} %broadcast_in_dim.73), calls=%async_computation.3 | async-start | bytes 262144 | tf_op jit(solution)/shard_map/all_to_all | solution.py:801
  215.5 263.4 %all-gather.15.cloned.1.call-start = ((), (), s32[]{:S(2)}) async-start(), calls=%async_computation.16 | async-start | bytes 1327104 | tf_op jit(solution)/shard_map/all_gather | solution.py:947
  244.8 6.1 collective-permute-start.15
  244.8 6.0 collective-permute-start.16
  244.8 7.6 %collective-permute-start.17 = (f32[8,512]{1,0:T(8,128)S(1)}, f32[8,512]{1,0:T(8,128)S(1)}, u32[]{:S(2)}, u32[]{:S(2)}) collective-permute-start(f32[8,512]{1,0:T(8,128)S(1)} %add.242), channel_id=1, source_target_pairs={{0,6},{1,7},{2,0},{3,1},{4,2},{5,3},{6,4},{7,5},{8,14},{9,15},{10,... | collective-permute-start | bytes 49160 | tf_op jit(solution)/shard_map/ppermute | solution.py:789
  252.5 7.0 %collective-permute-start.18 = (f32[8,512]{1,0:T(8,128)S(1)}, f32[8,512]{1,0:T(8,128)S(1)}, u32[]{:S(2)}, u32[]{:S(2)}) collective-permute-start(f32[8,512]{1,0:T(8,128)S(1)} %add_add_fusion.5), channel_id=1, source_target_pairs={{0,8},{8,16},{16,24},{24,0},{1,9},{9,17},{17,25},{25,1},{2,10},{10... | collective-permute-start | bytes 49160 | tf_op jit(solution)/shard_map/ppermute | solution.py:789
  330.2 13.0 %all-to-all-start.4 = ((f32[32,8,128]{2,1,0:T(8,128)}), f32[32,8,128]{2,1,0:T(8,128)S(1)}, u32[]{:S(2)}, u32[]{:S(2)}) async-start(f32[32,8,128]{2,1,0:T(8,128)} %broadcast_in_dim.76), calls=%async_computation.4 | async-start | bytes 262144 | tf_op jit(solution)/shard_map/all_to_all | solution.py:801
  334.9 145.9 %reduce-scatter.11.cloned.1.call-start = ((), (), s32[]{:S(2)}) async-start(), calls=%async_computation.19 | async-start | bytes 2359296 | tf_op jit(solution)/shard_map/reduce_scatter | solution.py:967
  362.7 18.6 %all-to-all-start.5 = ((f32[32,8,128]{2,1,0:T(8,128)}), f32[32,8,128]{2,1,0:T(8,128)S(1)}, u32[]{:S(2)}, u32[]{:S(2)}) async-start(f32[32,8,128]{2,1,0:T(8,128)} %broadcast_in_dim.78), calls=%async_computation.5 | async-start | bytes 262144 | tf_op jit(solution)/shard_map/all_to_all | solution.py:801
  368.5 112.4 %reduce-scatter.7.cloned.1.call-start = ((), (), s32[]{:S(2)}) async-start(), calls=%async_computation.17 | async-start | bytes 2359296 | tf_op jit(solution)/shard_map/reduce_scatter | solution.py:989
  411.5 12.5 %collective-permute-start.32 = (f32[8,512]{1,0:T(8,128)S(1)}, f32[8,512]{1,0:T(8,128)S(1)}, u32[]{:S(2)}, u32[]{:S(2)}) collective-permute-start(f32[8,512]{1,0:T(8,128)S(1)} %add_add_fusion.1), channel_id=1, source_target_pairs={{0,8},{8,16},{16,24},{24,0},{1,9},{9,17},{17,25},{25,1},{2,10},{10... | collective-permute-start | bytes 49160 | tf_op jit(solution)/shard_map/ppermute | solution.py:789
  413.0 11.1 %collective-permute-start.33 = (f32[8,512]{1,0:T(8,128)S(1)}, f32[8,512]{1,0:T(8,128)S(1)}, u32[]{:S(2)}, u32[]{:S(2)}) collective-permute-start(f32[8,512]{1,0:T(8,128)S(1)} %add_add_fusion.1), channel_id=1, source_target_pairs={{0,16},{8,24},{16,0},{24,8},{1,17},{9,25},{17,1},{25,9},{2,18},{10... | collective-permute-start | bytes 49160 | tf_op jit(solution)/shard_map/ppermute | solution.py:789
  414.5 9.6 %collective-permute-start.34 = (f32[8,512]{1,0:T(8,128)S(1)}, f32[8,512]{1,0:T(8,128)S(1)}, u32[]{:S(2)}, u32[]{:S(2)}) collective-permute-start(f32[8,512]{1,0:T(8,128)S(1)} %add_add_fusion.1), channel_id=1, source_target_pairs={{0,24},{8,0},{16,8},{24,16},{1,25},{9,1},{17,9},{25,17},{2,26},{10... | collective-permute-start | bytes 49160 | tf_op jit(solution)/shard_map/ppermute | solution.py:789
  424.7 92.8 %reduce-scatter.9.cloned.1.call-start = ((), (), s32[]{:S(2)}) async-start(), calls=%async_computation.18 | async-start | bytes 5308416 | tf_op jit(solution)/shard_map/reduce_scatter | solution.py:978
  442.7 13.7 %all-to-all-start.6 = ((f32[32,8,128]{2,1,0:T(8,128)}), f32[32,8,128]{2,1,0:T(8,128)S(1)}, u32[]{:S(2)}, u32[]{:S(2)}) async-start(f32[32,8,128]{2,1,0:T(8,128)} %broadcast_in_dim.80), calls=%async_computation.6 | async-start | bytes 262144 | tf_op jit(solution)/shard_map/all_to_all | solution.py:801
  446.4 159.4 %reduce-scatter.13.cloned.1.call-start = ((), (), s32[]{:S(2)}) async-start(), calls=%async_computation.20 | async-start | bytes 2359296 | tf_op jit(solution)/shard_map/reduce_scatter | solution.py:967
  457.8 21.1 %all-to-all-start.7 = ((bf16[8,48,256]{2,1,0:T(8,128)(2,1)}), bf16[8,48,256]{2,1,0:T(8,128)(2,1)S(1)}, u32[]{:S(2)}, u32[]{:S(2)}) async-start(bf16[8,48,256]{2,1,0:T(8,128)(2,1)} %bitcast.106), calls=%async_computation.7 | async-start | bytes 393216 | tf_op jit(solution)/shard_map/all_to_all | solution.py:940
  518.2 15.5 %all-to-all-start.8 = ((f32[32,8,128]{2,1,0:T(8,128)}), f32[32,8,128]{2,1,0:T(8,128)S(1)}, u32[]{:S(2)}, u32[]{:S(2)}) async-start(f32[32,8,128]{2,1,0:T(8,128)} %broadcast_in_dim.82), calls=%async_computation.11 | async-start | bytes 262144 | tf_op jit(solution)/shard_map/all_to_all | solution.py:801
  521.2 84.6 %reduce-scatter.17.cloned.1.call-start = ((), (), s32[]{:S(2)}) async-start(), calls=%async_computation.22 | async-start | bytes 2359296 | tf_op jit(solution)/shard_map/reduce_scatter | solution.py:993
  546.0 101.1 %reduce-scatter.15.cloned.1.call-start = ((), (), s32[]{:S(2)}) async-start(), calls=%async_computation.21 | async-start | bytes 5308416 | tf_op jit(solution)/shard_map/reduce_scatter | solution.py:978
  549.7 23.3 %collective-permute-start.39 = (bf16[928,512]{1,0:T(8,128)(2,1)S(1)}, bf16[928,512]{1,0:T(8,128)(2,1)S(1)}, u32[]{:S(2)}, u32[]{:S(2)}) collective-permute-start(bf16[928,512]{1,0:T(8,128)(2,1)S(1)} %get-tuple-element.168), channel_id=1, source_target_pairs={{0,8},{8,0},{16,24},{24,16},{1,9},{9,1},{17,25},{25,17},{2,10},{10... | collective-permute-start | bytes 2850824 | tf_op jit(solution)/shard_map/ppermute | solution.py:814
  552.2 22.9 %collective-permute-start.41 = (bf16[928,512]{1,0:T(8,128)(2,1)S(1)}, bf16[928,512]{1,0:T(8,128)(2,1)S(1)}, u32[]{:S(2)}, u32[]{:S(2)}) collective-permute-start(bf16[928,512]{1,0:T(8,128)(2,1)S(1)} %get-tuple-element.169), channel_id=1, source_target_pairs={{0,16},{8,24},{16,0},{24,8},{1,17},{9,25},{17,1},{25,9},{2,18},{10... | collective-permute-start | bytes 2850824 | tf_op jit(solution)/shard_map/ppermute | solution.py:814
  573.3 22.6 %collective-permute-start.40 = (bf16[928,512]{1,0:T(8,128)(2,1)S(1)}, bf16[928,512]{1,0:T(8,128)(2,1)S(1)}, u32[]{:S(2)}, u32[]{:S(2)}) collective-permute-start(bf16[928,512]{1,0:T(8,128)(2,1)S(1)} %add_convert_fusion.3), channel_id=1, source_target_pairs={{0,16},{8,24},{16,0},{24,8},{1,17},{9,25},{17,1},{25,9},{2,18},{10... | collective-permute-start | bytes 2850824 | tf_op jit(solution)/shard_map/ppermute | solution.py:814
  575.3 22.2 %collective-permute-start.42 = (bf16[928,512]{1,0:T(8,128)(2,1)S(1)}, bf16[928,512]{1,0:T(8,128)(2,1)S(1)}, u32[]{:S(2)}, u32[]{:S(2)}) collective-permute-start(bf16[928,512]{1,0:T(8,128)(2,1)S(1)} %add_convert_fusion.1), channel_id=1, source_target_pairs={{0,8},{8,0},{16,24},{24,16},{1,9},{9,1},{17,25},{25,17},{2,10},{10... | collective-permute-start | bytes 2850824 | tf_op jit(solution)/shard_map/ppermute | solution.py:814
  648.2 5.9 collective-permute-start.35
  649.8 5.7 collective-permute-start.37
  655.6 6.5 collective-permute-start.36
  657.5 11.6 %collective-permute-start.43 = (bf16[416,512]{1,0:T(8,128)(2,1)S(1)}, bf16[416,512]{1,0:T(8,128)(2,1)S(1)}, u32[]{:S(2)}, u32[]{:S(2)}) collective-permute-start(bf16[416,512]{1,0:T(8,128)(2,1)S(1)} %get-tuple-element.156), channel_id=1, source_target_pairs={{0,8},{8,0},{16,24},{24,16},{1,9},{9,1},{17,25},{25,17},{2,10},{10... | collective-permute-start | bytes 1277960 | tf_op jit(solution)/shard_map/ppermute | solution.py:814
  658.2 11.5 %collective-permute-start.45 = (bf16[416,512]{1,0:T(8,128)(2,1)S(1)}, bf16[416,512]{1,0:T(8,128)(2,1)S(1)}, u32[]{:S(2)}, u32[]{:S(2)}) collective-permute-start(bf16[416,512]{1,0:T(8,128)(2,1)S(1)} %get-tuple-element.157), channel_id=1, source_target_pairs={{0,16},{8,24},{16,0},{24,8},{1,17},{9,25},{17,1},{25,9},{2,18},{10... | collective-permute-start | bytes 1277960 | tf_op jit(solution)/shard_map/ppermute | solution.py:814
  658.4 10.7 %collective-permute-start.38 = (bf16[128,512]{1,0:T(8,128)(2,1)S(1)}, bf16[128,512]{1,0:T(8,128)(2,1)S(1)}, u32[]{:S(2)}, u32[]{:S(2)}) collective-permute-start(bf16[128,512]{1,0:T(8,128)(2,1)S(1)} %get-tuple-element.165), channel_id=1, source_target_pairs={{0,8},{8,0},{16,24},{24,16},{1,9},{9,1},{17,25},{25,17},{2,10},{10... | collective-permute-start | bytes 393224 | tf_op jit(solution)/shard_map/ppermute | solution.py:814
  669.2 8.2 %collective-permute-start.44 = (bf16[416,512]{1,0:T(8,128)(2,1)S(1)}, bf16[416,512]{1,0:T(8,128)(2,1)S(1)}, u32[]{:S(2)}, u32[]{:S(2)}) collective-permute-start(bf16[416,512]{1,0:T(8,128)(2,1)S(1)} %add_convert_fusion.7), channel_id=1, source_target_pairs={{0,16},{8,24},{16,0},{24,8},{1,17},{9,25},{17,1},{25,9},{2,18},{10... | collective-permute-start | bytes 1277960 | tf_op jit(solution)/shard_map/ppermute | solution.py:814
  669.8 8.2 %collective-permute-start.46 = (bf16[416,512]{1,0:T(8,128)(2,1)S(1)}, bf16[416,512]{1,0:T(8,128)(2,1)S(1)}, u32[]{:S(2)}, u32[]{:S(2)}) collective-permute-start(bf16[416,512]{1,0:T(8,128)(2,1)S(1)} %add_convert_fusion.5), channel_id=1, source_target_pairs={{0,8},{8,0},{16,24},{24,16},{1,9},{9,1},{17,25},{25,17},{2,10},{10... | collective-permute-start | bytes 1277960 | tf_op jit(solution)/shard_map/ppermute | solution.py:814
  (52 other events, 426.4 us)
Sparse Core Ops, SparseCore 0:
  10.2 41.6 all-gather.16
  53.5 29.2 all-gather.18
  85.0 30.3 all-gather.20
  117.4 53.5 all-gather.22
  172.4 31.5 all-gather.24
  206.1 65.5 all-gather.12
  281.8 20.8 all-gather.14
  344.0 37.3 reduce-scatter.10
  424.8 35.2 reduce-scatter.6
  462.2 55.2 reduce-scatter.8
  519.8 34.1 reduce-scatter.12
  556.7 34.4 reduce-scatter.16
  593.5 53.6 reduce-scatter.14

commit v3 on v2

--- a/solution.py
+++ b/solution.py
@@ -698,7 +698,29 @@
     )(inv, e1, h1, tot1, gb1, btot1, mask, x)
 
 
-def spatial_wgrad_kernel(sh, act, g, out, pat, scr):
+def put_owned(place, val, outs, first):
+    dps, chips, rows, width = outs[0].shape
+    last, at = first + val.shape[0], first
+    while at < last:
+        chip, start = at // (2 * rows), at % (2 * rows)
+        stop = min(2 * rows, start + last - at)
+        for side in range(2):
+            low, high = max(start, side * rows), min(stop, (side + 1) * rows)
+            if low >= high:
+                continue
+            source = pl.ds(at - first + low - start, high - low)
+            for q in range(dps):
+                piece = val[source, q * width : (q + 1) * width]
+                for e, out in enumerate(outs):
+
+                    @pl.when((place[0, 1] & 1) == (side ^ e))
+                    def _(piece=piece, out=out, low=low, high=high, q=q):
+                        out[q ^ place[0, 0], chip ^ (place[0, 1] >> 1), low - side * rows : high - side * rows, :] = piece
+        at += stop - start
+
+
+def spatial_wgrad_kernel(sh, owned, place, act, g, *rest):
+    *outs, pat, scr, val = rest
     j = pl.program_id(0)
     m = act.shape[1]
 
@@ -716,25 +738,31 @@
         def _(k=k):
             rows = slice(k * sh.rows, (k + SIDE) * sh.rows)
             for l in range(TAPS):
-                out[l * m : (l + 1) * m, :] = tn(pat[rows, l * m : (l + 1) * m], g[...]).astype(BF)
-
-
-def spatial_wgrad(sh, act, g):
+                into = val if owned else outs[0]
+                into[l * m : (l + 1) * m, :] = tn(pat[rows, l * m : (l + 1) * m], g[...]).astype(BF)
+            if owned:
+                put_owned(place, val, outs, k * TAPS * m)
+
+
+def spatial_wgrad(sh, act, g, place, owners, dp, owned):
     m = act.shape[1]
-    return pl.pallas_call(
-        functools.partial(spatial_wgrad_kernel, sh),
+    rows = TAPS * TAPS * m
+    owned_shape = (dp, owners // 2, rows // owners, m // dp)
+    return pl.pallas_call(
+        functools.partial(spatial_wgrad_kernel, sh, owned),
         grid=(TAPS,),
-        in_specs=[whole(act.shape), whole(g.shape)],
-        out_specs=pl.BlockSpec((TAPS * m, m), lambda j: (j, 0)),
-        out_shape=sds((TAPS * TAPS * m, m), BF),
+        in_specs=[pl.BlockSpec(memory_space=pltpu.SMEM), whole(act.shape), whole(g.shape)],
+        out_specs=[whole(owned_shape)] * 2 if owned else [pl.BlockSpec((TAPS * m, m), lambda j: (j, 0))],
+        out_shape=[sds(owned_shape, BF)] * 2 if owned else [sds((rows, m), BF)],
         scratch_shapes=[
             pltpu.VMEM(((SIDE + 2) * sh.rows, TAPS * m), BF),
             pltpu.VMEM((sh.low + 16, m), F32),
+            pltpu.VMEM((TAPS * m, m), BF),
         ],
         compiler_params=params(1),
         cost_estimate=cost(18 * sh.total * m * m, 4 * sh.total * m + 18 * m * m),
         name="spatial_wgrad",
-    )(act, g)
+    )(place, act, g)
 
 
 def assemble_kernel(place, own, mate, out, sem):
@@ -802,18 +830,44 @@
     return jnp.sum(got, axis=0).reshape(v.shape)
 
 
-def copies_sum(arrays, dp):
+def added(*terms):
+    return sum([v.astype(F32) for v in terms[1:]], terms[0].astype(F32)).astype(BF)
+
+
+def copies_halves(arrays):
     flat = [v.reshape(-1, 512) for v in arrays]
     flat = jnp.concatenate(flat, axis=0) if len(flat) > 1 else flat[0]
     cut = flat.shape[0] // 32 * 16
-    halves = [flat[:cut], flat[cut:]]
+    return [flat[:cut], flat[cut:]]
+
+
+def copies_swap(halves, dp, turn):
     bits = [1 << k for k in range(dp.bit_length() - 1)]
-    for turn in range(len(bits)):
-        for h in range(2):
-            bit = (bits, bits[::-1])[h][turn]
-            got = lax.ppermute(halves[h], "dp", [(i, i ^ bit) for i in range(dp)])
-            halves[h] = (halves[h].astype(F32) + got.astype(F32)).astype(BF)
+    return [
+        lax.ppermute(half, "dp", [(i, i ^ (bits, bits[::-1])[h][turn]) for i in range(dp)])
+        for h, half in enumerate(halves)
+    ]
+
+
+def copies_add(halves, got):
+    return [added(half, other) for half, other in zip(halves, got)]
+
+
+def copies_sum(halves, dp, first=0):
+    for turn in range(first, dp.bit_length() - 1):
+        halves = copies_add(halves, copies_swap(halves, dp, turn))
     return halves
+
+
+def swap_core(parts, owners):
+    return lax.ppermute(parts[1], "fsdp", [(i, i ^ 1) for i in range(owners)])
+
+
+def swap_rest(blocks, axis, size, unit):
+    return [
+        lax.ppermute(blocks[k], axis, [(i, i ^ (unit * k)) for i in range(size)])
+        for k in range(1, len(blocks))
+    ]
 
 
 def copies_out(halves, arrays):
@@ -945,15 +999,15 @@
         tiled=True,
     ).reshape(owners * sh.padded, channels // owners)
     all_logits = gather(grad_logits)
-    head_grad = tn(all_logits, mine).astype(BF)
 
     def in_order(*values):
         return lax.optimization_barrier(values)
 
     e3, part = top_grad(sh, merged, h3, x, tot3, inv, gb_out[-1], mask)
+    part, mine = in_order(part, mine)
     btot3 = total_of(part, (dp, owners))
     scatter = functools.partial(lax.psum_scatter, axis_name="fsdp", scatter_dimension=0, tiled=True)
-    shards = {}
+    shards, swaps = {}, {}
     sums_mid, sums_out = [], []
     for b in reversed(range(blocks)):
         w1, w2, w3 = weights[b]
@@ -962,20 +1016,36 @@
             sh, e3, h3, tot3, gb_out[b], btot3, inv, mask, w3, h2, tot2, gb_mid[b, 1]
         )
         grad = wgrad(act2, g3, inner)
+        if short and b + 1 < blocks:
+            terms = swaps[b + 1]
+            part, *got = in_order(part, *swap_rest(terms, "dp", dp, 1))
+            total = added(terms[0], *got)
+            swaps[b + 1] = [total[k] for k in range(owners // 2)]
         btot2 = total_of(part, (dp, owners))
         btot2, grad = in_order(btot2, grad)
         shards["expand", b] = scatter(grad)
+        if b + 1 == blocks:
+            head_grad = tn(all_logits, mine).astype(BF)
         g2, e1, part = spatial_back(
             sh, e2, h2, tot2, gb_mid[b, 1], btot2, inv, mask, w2, h1, tot1, gb_mid[b, 0]
         )
-        grad = spatial_wgrad(sh, act1, g2)
-        if b + 1 < blocks:
-            early = [head_grad] + [shards[k, b + 1] for k in ("reduce", "spatial", "expand")]
-            part, *early = in_order(part, *early)
-            early_halves = copies_sum(early, dp)
+        grad = spatial_wgrad(sh, act1, g2, place, owners, dp, short)
+        if short and b + 1 < blocks:
+            part, *got = in_order(part, *swap_rest(swaps[b + 1], "fsdp", owners, 2))
+            shards["spatial", b + 1] = added(swaps[b + 1][0], *got)
+        if b == 0:
+            early = [head_grad] + [shards["reduce", k] for k in range(1, blocks)]
+            early += [shards["expand", k] for k in range(1, blocks)]
+            halves = copies_halves(early)
+            part, *swapped = in_order(part, *copies_swap(halves, dp, 0))
+            halves = copies_add(halves, swapped)
+            swapped = copies_swap(halves, dp, 1)
         btot1 = total_of(part, (dp, owners))
-        btot1, grad = in_order(btot1, grad)
-        shards["spatial", b] = scatter(grad)
+        btot1, *grad = in_order(btot1, *grad)
+        if short:
+            other = swap_core(grad, owners)
+        else:
+            shards["spatial", b] = scatter(grad[0])
         sums_out.insert(0, (btot3, tot3))
         sums_mid.insert(0, ((btot1, tot1), (btot2, tot2)))
         if b > 0:
@@ -983,31 +1053,50 @@
             g1, e3, part = reduce_back(
                 sh, e1, h1, tot1, gb_mid[b, 0], btot1, inv, mask, w1, e3, h3p, xp, tot3p, gb_out[b - 1]
             )
+            if short:
+                part, other = in_order(part, other)
+                swaps[b] = [added(grad[0][j], other[j]) for j in range(dp)]
             grad = wgrad(x, g1, inner)
             btot3 = total_of(part, (dp, owners))
             btot3, grad = in_order(btot3, grad)
             shards["reduce", b] = scatter(grad)
         else:
+            spatial = grad
             grad = reduce_wgrad(sh, e1, h1, tot1, gb_mid[b, 0], btot1, inv, mask, x)
-            e3, grad = in_order(e3, grad)
+            grad, *swapped = in_order(grad, *swapped)
+            halves = copies_add(halves, swapped)
+            if short:
+                grad, other = in_order(grad, other)
+                swaps[b] = [added(spatial[0][j], other[j]) for j in range(dp)]
+                e3, grad, *swaps[b] = in_order(e3, grad, *swaps[b])
+                got = swap_rest(swaps[b], "dp", dp, 1)
+            else:
+                e3, grad = in_order(e3, grad)
+                got = [shards["spatial", k] for k in range(blocks)]
             shards["reduce", b] = scatter(grad)
             grad_features = features_back(
                 sh, e1, h1, tot1, gb_mid[b, 0], btot1, inv, mask, w1, e3
             )
-            (
-                grad_features,
-                shards["expand", b],
-                shards["spatial", b],
-                shards["reduce", b],
-            ) = in_order(
-                grad_features, shards["expand", b], shards["spatial", b], shards["reduce", b]
+            grad_features, shards["reduce", b], shards["expand", b], *got = in_order(
+                grad_features, shards["reduce", b], shards["expand", b], *got
             )
 
-    groups = [early, [shards["expand", 0], shards["spatial", 0]], [shards["reduce", 0]]]
-    halves = [early_halves, copies_sum(groups[1], dp), copies_sum(groups[2], dp)]
-    sums = [copies_out(h, g) for h, g in zip(halves, groups)]
-    head_grad, reduce_one, spatial_one, expand_one = sums[0]
-    (expand_zero, spatial_zero), (reduce_zero,) = sums[1:]
+    if short:
+        total = added(swaps[0][0], *got)
+        total = [total[k] for k in range(owners // 2)]
+        shards["spatial", 0] = added(total[0], *swap_rest(total, "fsdp", owners, 2))
+        flat = jnp.stack([shards["spatial", b] for b in range(blocks)])
+        flat = jnp.broadcast_to(flat[None], (dp,) + flat.shape)
+        flat = lax.all_to_all(flat, "dp", 0, 0, tiled=True)
+        spatial = jnp.transpose(flat, (1, 2, 0, 3)).reshape(w_spatial.shape).astype(F32) / SCALE
+    sums = copies_out(halves, early)
+    late = [shards["reduce", 0], shards["expand", 0]] + ([] if short else got)
+    lates = copies_out(copies_sum(copies_halves(late), dp), late)
+    head_grad = sums[0]
+    reduce_all = jnp.stack([lates[0]] + sums[1:blocks])
+    expand_all = jnp.stack([lates[1]] + sums[blocks:])
+    if not short:
+        spatial = jnp.stack(lates[2:])
     at = [(place, size) for place, size in zip(offsets, sizes)]
 
     def gains(pair):
@@ -1019,9 +1108,9 @@
     return (
         jnp.transpose(trunk, (1, 0, 2)),
         jnp.transpose(grad_features, (1, 0, 2)),
-        jnp.stack([reduce_zero, reduce_one]),
-        jnp.stack([spatial_zero, spatial_one]),
-        jnp.stack([expand_zero, expand_one]),
+        reduce_all,
+        spatial,
+        expand_all,
         jnp.stack([jnp.stack([gains(p) for p in pairs]) for pairs in sums_mid]),
         jnp.stack([jnp.stack([p[0][0] / SCALE for p in pairs]) for pairs in sums_mid]),
         jnp.stack([gains(p) for p in sums_out]),

time: 704 us -> 651 us (0.925)
  waiting for transfers between devices: 188 us -> 95.9 us
  starting transfers between devices: 95.4 us -> 119 us
  other arithmetic: 17.2 us -> 34 us
    reduce_scatter x2 -> x0, waiting for transfers between devices: 78 us -> none  [on_device(): shards['spatial', b] = scatter(grad)]
    convert_element_type x9 -> x11, other arithmetic: 1.55 us -> 15.3 us  [added(): sum([v.astype(F32) for v in terms[1:]], terms[0].astype(F32)).astype(BF)]
    ppermute x12 -> x22, waiting for transfers between devices: 36.7 us -> 25.7 us  [the longest x12 18.6 us: swap_rest(): lax.ppermute(blocks[k], axis, [(i, i ^ unit * k) for i in range(size)])]
    ppermute x12 -> x22, starting transfers between devices: 15.5 us -> 25.7 us  [the longest x12 15.8 us: swap_rest(): lax.ppermute(blocks[k], axis, [(i, i ^ unit * k) for i in range(size)])]
    all_to_all x6, waiting for transfers between devices: 20.7 us -> 12.6 us  [total_of(): got = lax.all_to_all(spread, AXES, 0, 0, tiled=True)]
  transfers between devices with their start and end apart: 67 -> 76, of which waited for: 35 -> 35; matrix products, arithmetic and copies ran while one was open for 7% -> 12% of each run, Pallas kernels for 42% -> 46%
where the time goes in v3:
time: 651 us; the launch traced here: 639 us
  Pallas kernels  302 us (46%)
  starting transfers between devices  119 us (18%)
  waiting for transfers between devices  95.9 us (15%)
  local copies, waits for them, and re-layouts  45.7 us (7%)
  other arithmetic  34 us (5%)
  blocking collectives  25.3 us (4%)
  between operations  16 us (2%)
    ppermute x24, starting transfers between devices, others(): return sum([lax.ppermute(v, axis, way) for way in ways], v)  39.9 us
    pallas_call x2, Pallas kernels, spatial_back(): pl.pallas_call(functools.partial(spatial_back_kernel, sh), grid=(SIDE + 1...  34.9 us
    all_to_all x6, starting transfers between devices, total_of(): got = lax.all_to_all(spread, AXES, 0, 0, tiled=True)  33.8 us
    pallas_call x2, Pallas kernels, spatial_conv(): pl.pallas_call(functools.partial(spatial_kernel, sh), grid=(SIDE + 1,), i...  32.7 us
    pallas_call x2, Pallas kernels, expand_back(): pl.pallas_call(expand_back_kernel, grid=(SIDE,), in_specs=[pl.BlockSpec(m...  31.8 us
    pallas_call x2, Pallas kernels, spatial_wgrad(): pl.pallas_call(functools.partial(spatial_wgrad_kernel, sh, owned), grid=(...  30.3 us
    ppermute x6, waiting for transfers between devices, flips(): lax.ppermute(v, axis, [(i, i ^ unit * k) for i in range(size)])  26 us
    all_to_all x2, blocking collectives, total_of(): got = lax.all_to_all(spread, AXES, 0, 0, tiled=True)  25.3 us
  transfers between devices with their start and end apart: 76, of which 35 were waited for; matrix products, arithmetic and copies ran while one was open for 12% of the time, Pallas kernels for 46%

profile of v3, /device:TPU:0, one launch (start us, length us, event | category | flops | bytes accessed | tf_op | source)
XLA Modules:
  0.0 638.9 jit_solution(6635327756697705942)
XLA Ops:
  21.1 9.5 %prep.1.x = bf16[1792,2048]{1,0:T(8,128)(2,1)} custom-call(bf16[49,36,2048]{2,1,0:T(8,128)(2,1)} %bitcast.176, f32[1792,1]{1,0:T(8,128)} %bitcast.154), custom_call_target="tpu_custom_call" | custom-call | tf_op jit(solution)/shard_map/prep/pallas_call | solution.py:126
  30.7 5.0 collective-permute-done.1
  39.4 12.8 %collective-permute-done.3 = bf16[4,576,128]{2,1,0:T(8,128)(2,1)S(1)} collective-permute-done((bf16[4,576,128]{2,1,0:T(8,128)(2,1)S(1)}, bf16[4,576,128]{2,1,0:T(8,128)(2,1)S(1)}, u32[]{:S(2)}, u32[]{:S(2)}) %collective-permute-start.3) | collective-permute-done | bytes 589856 | tf_op jit(solution)/shard_map/ppermute | solution.py:807
  52.1 8.2 %collective-permute-done.4 = bf16[4,576,128]{2,1,0:T(8,128)(2,1)S(1)} collective-permute-done((bf16[4,576,128]{2,1,0:T(8,128)(2,1)S(1)}, bf16[4,576,128]{2,1,0:T(8,128)(2,1)S(1)}, u32[]{:S(2)}, u32[]{:S(2)}) %collective-permute-start.4) | collective-permute-done | bytes 589856 | tf_op jit(solution)/shard_map/ppermute | solution.py:807
  61.5 10.0 %reduce_conv.1 = (f32[1792,512]{1,0:T(8,128)}, f32[2,512]{1,0:T(2,128)}) custom-call(bf16[1792,2048]{1,0:T(8,128)(2,1)} %prep.1.x, bf16[2048,512]{1,0:T(8,128)(2,1)} %bitcast.181), custom_call_target="tpu_custom_call" | custom-call | flops 3758096384 | bytes 11010048 | tf_op jit(solution)/shard_map/reduce_conv/pallas_call | solution.py:150
  75.0 10.6 %all-to-all-start = ((f32[32,8,256]{2,1,0:T(8,128)}), f32[32,8,256]{2,1,0:T(8,128)S(1)}, u32[]{:S(2)}, u32[]{:S(2)}) async-start(f32[32,8,256]{2,1,0:T(8,128)} %broadcast_in_dim.73), calls=%async_computation | async-start | bytes 524288 | tf_op jit(solution)/shard_map/all_to_all | solution.py:829
  86.3 5.5 assemble.1.w
  91.8 4.2 all-to-all-done
  97.9 16.4 %spatial_conv.2 = (bf16[1792,512]{1,0:T(8,128)(2,1)}, f32[1792,512]{1,0:T(8,128)}, f32[2,512]{1,0:T(2,128)}) custom-call(f32[1,1]{1,0:T(1,128)} %bitcast.18.inv, f32[1792,512]{1,0:T(8,128)} %get-tuple-element.120.h1, f32[2,512]{1,0:T(2,128)} %slice.279.tot.tot1, f32[2,512]{1,0:T(2,128)} %get-tuple-element.240.gb.gb1, f32[1792,1]{1,0:T(8,128)} %bitcast.155, ...), custom_call_target="tpu_custom_call" | custom-call | flops 8455716864 | bytes 13893632 | tf_op jit(solution)/shard_map/spatial_conv/pallas_call | solution.py:203
  115.0 11.4 %all_to_all.50 = f32[32,8,128]{2,1,0:T(8,128)S(1)} all-to-all(f32[32,8,128]{2,1,0:T(8,128)S(1)} %broadcast_in_dim.75), channel_id=1, replica_groups=mesh['dp'=4,'fsdp'=8] {'dp','fsdp'}, dimensions={0} | all-to-all | bytes 262144 | tf_op jit(solution)/shard_map/all_to_all | solution.py:829
  127.1 10.7 %expand_conv.2 = (bf16[1792,512]{1,0:T(8,128)(2,1)}, bf16[1792,2048]{1,0:T(8,128)(2,1)}, f32[2,2048]{1,0:T(2,128)}) custom-call(f32[1,1]{1,0:T(1,128)} %bitcast.18.inv, f32[1792,512]{1,0:T(8,128)} %get-tuple-element.122.h2, f32[2,512]{1,0:T(2,128)} %reshape.521.tot.tot2, f32[2,512]{1,0:T(2,128)} %get-tuple-element.241.gb.gb2, f32[1792,1]{1,0:T(8,128)} %bitcast.157, ...), custom_call_target="tpu_custom_call" | custom-call | flops 3758096384 | bytes 12845056 | tf_op jit(solution)/shard_map/expand_conv/pallas_call | solution.py:246
  154.3 14.6 %join.1 = (bf16[1792,2048]{1,0:T(8,128)(2,1)}, f32[1792,512]{1,0:T(8,128)}, f32[2,512]{1,0:T(2,128)}) custom-call(f32[1,1]{1,0:T(1,128)} %bitcast.18.inv, bf16[1792,2048]{1,0:T(8,128)(2,1)} %get-tuple-element.124.h3, bf16[1792,2048]{1,0:T(8,128)(2,1)} %prep.1.x, f32[2,2048]{1,0:T(2,128)} %reshape.523.tot.tot3, f32[2,2048]{1,0:T(2,128)} %get-tuple-element.232.gb.gb3, ...), custom_call_target="tpu_custom_call" | custom-call | flops 3758096384 | bytes 25690112 | tf_op jit(solution)/shard_map/join/pallas_call | solution.py:283
  169.6 13.9 %all_to_all.51 = f32[32,8,128]{2,1,0:T(8,128)S(1)} all-to-all(f32[32,8,128]{2,1,0:T(8,128)S(1)} %broadcast_in_dim.77), channel_id=1, replica_groups=mesh['dp'=4,'fsdp'=8] {'dp','fsdp'}, dimensions={0} | all-to-all | bytes 262144 | tf_op jit(solution)/shard_map/all_to_all | solution.py:829
  184.1 16.3 %spatial_conv.3 = (bf16[1792,512]{1,0:T(8,128)(2,1)}, f32[1792,512]{1,0:T(8,128)}, f32[2,512]{1,0:T(2,128)}) custom-call(f32[1,1]{1,0:T(1,128)} %bitcast.18.inv, f32[1792,512]{1,0:T(8,128)} %get-tuple-element.126.h1, f32[2,512]{1,0:T(2,128)} %reshape.524.tot.tot1, f32[2,512]{1,0:T(2,128)} %get-tuple-element.242.gb.gb1, f32[1792,1]{1,0:T(8,128)} %bitcast.159, ...), custom_call_target="tpu_custom_call" | custom-call | flops 8455716864 | bytes 13893632 | tf_op jit(solution)/shard_map/spatial_conv/pallas_call | solution.py:203
  201.8 4.1 all-to-all-start.3
  206.6 7.5 %all-to-all-done.3 = f32[32,8,128]{2,1,0:T(8,128)S(1)} async-done(((f32[32,8,128]{2,1,0:T(8,128)}), f32[32,8,128]{2,1,0:T(8,128)S(1)}, u32[]{:S(2)}, u32[]{:S(2)}) %all-to-all-start.3) | async-done | bytes 131104 | tf_op jit(solution)/shard_map/all_to_all | solution.py:829
  214.8 10.8 %expand_conv.3 = (bf16[1792,512]{1,0:T(8,128)(2,1)}, bf16[1792,2048]{1,0:T(8,128)(2,1)}, f32[2,2048]{1,0:T(2,128)}) custom-call(f32[1,1]{1,0:T(1,128)} %bitcast.18.inv, f32[1792,512]{1,0:T(8,128)} %get-tuple-element.128.h2, f32[2,512]{1,0:T(2,128)} %reshape.525.tot.tot2, f32[2,512]{1,0:T(2,128)} %get-tuple-element.239.gb.gb2, f32[1792,1]{1,0:T(8,128)} %bitcast.161, ...), custom_call_target="tpu_custom_call" | custom-call | flops 3758096384 | bytes 12845056 | tf_op jit(solution)/shard_map/expand_conv/pallas_call | solution.py:246
  227.6 5.5 collective-permute-start.15
  233.1 4.2 collective-permute-start.16
  239.5 6.4 %collective-permute-done.17 = f32[8,512]{1,0:T(8,128)S(1)} collective-permute-done((f32[8,512]{1,0:T(8,128)S(1)}, f32[8,512]{1,0:T(8,128)S(1)}, u32[]{:S(2)}, u32[]{:S(2)}) %collective-permute-start.17) | collective-permute-done | bytes 16416 | tf_op jit(solution)/shard_map/ppermute | solution.py:817
  253.2 13.5 %last_join.1 = (bf16[49,36,2048]{2,1,0:T(8,128)(2,1)}, bf16[48,2048]{1,0:T(8,128)(2,1)}) custom-call(f32[1,1]{1,0:T(1,128)} %bitcast.18.inv, bf16[1792,2048]{1,0:T(8,128)(2,1)} %get-tuple-element.130.h3, bf16[1792,2048]{1,0:T(8,128)(2,1)} %get-tuple-element.131.x.left, f32[2,2048]{1,0:T(2,128)} %reshape.527.tot.tot3, f32[2,2048]{1,0:T(2,128)} %get-tuple-element.231.gb.gb3, ...), custom_call_target="tpu_custom_call" | custom-call | flops 352321536 | bytes 22020096 | tf_op jit(solution)/shard_map/last_join/pallas_call | solution.py:326
  266.7 7.9 %heads.1 = (f32[48,2048]{1,0:T(8,128)}, bf16[48,1536]{1,0:T(8,128)(2,1)}) custom-call(bf16[48,2048]{1,0:T(8,128)(2,1)} %get-tuple-element.134.pooled, s32[48,3]{1,0:T(8,128)} %pad.26.labels, f32[48,1]{1,0:T(8,128)} %copy.122.area, s32[48,2048]{1,0:T(8,128)} %pad.27.bits, bf16[1424,2048]{1,0:T(8,128)(2,1)} %all-gather.13.cloned.1.call-done.w), custom_call_target="tpu_custom_call" | custom-call | flops 603979776 | bytes 5832704 | tf_op jit(solution)/shard_map/heads/pallas_call | solution.py:382
  275.3 3.4 all-to-all-start.4
  278.7 16.2 %top_grad.1 = (bf16[1792,2048]{1,0:T(8,128)(2,1)}, f32[2,2048]{1,0:T(2,128)}) custom-call(f32[1,1]{1,0:T(1,128)} %bitcast.18.inv, f32[48,2048]{1,0:T(8,128)} %get-tuple-element.135.merged, bf16[1792,2048]{1,0:T(8,128)(2,1)} %get-tuple-element.130.h3, bf16[1792,2048]{1,0:T(8,128)(2,1)} %get-tuple-element.131.x.left, f32[2,2048]{1,0:T(2,128)} %reshape.527.tot.tot3, ...), custom_call_target="tpu_custom_call" | custom-call | flops 73400320 | bytes 22020096 | tf_op jit(solution)/shard_map/top_grad/pallas_call | solution.py:415
  312.4 15.8 %expand_back.2 = (bf16[1792,2048]{1,0:T(8,128)(2,1)}, f32[1792,512]{1,0:T(8,128)}, f32[2,512]{1,0:T(2,128)}) custom-call(f32[1,1]{1,0:T(1,128)} %bitcast.18.inv, bf16[1792,2048]{1,0:T(8,128)(2,1)} %get-tuple-element.136.e3, bf16[1792,2048]{1,0:T(8,128)(2,1)} %get-tuple-element.130.h3, f32[2,2048]{1,0:T(2,128)} %reshape.527.tot.tot3, ...), custom_call_target="tpu_custom_call" | custom-call | flops 3758096384 | bytes 29360128 | tf_op jit(solution)/shard_map/expand_back/pallas_call | solution.py:458
  329.5 4.4 all-to-all-start.5
  334.0 8.2 %wgrad.3 = bf16[512,2048]{1,0:T(8,128)(2,1)} custom-call(bf16[1792,512]{1,0:T(8,128)(2,1)} %get-tuple-element.141.left, bf16[1792,2048]{1,0:T(8,128)(2,1)} %get-tuple-element.142.right), custom_call_target="tpu_custom_call" | custom-call | flops 3758096384 | bytes 11272192 | tf_op jit(solution)/shard_map/wgrad/pallas_call | solution.py:651
  342.9 17.5 %spatial_back.2 = (bf16[1792,512]{1,0:T(8,128)(2,1)}, f32[1792,512]{1,0:T(8,128)}, f32[2,512]{1,0:T(2,128)}) custom-call(f32[1,1]{1,0:T(1,128)} %bitcast.18.inv, f32[1792,512]{1,0:T(8,128)} %get-tuple-element.139.e2, f32[1792,512]{1,0:T(8,128)} %get-tuple-element.128.h2, f32[2,512]{1,0:T(2,128)} %reshape.525.tot.tot2, f32[2,512]{1,0:T(2,128)} %get-tuple-element.239.gb.gb2, ...), custom_call_target="tpu_custom_call" | custom-call | flops 8455716864 | bytes 21233664 | tf_op jit(solution)/shard_map/spatial_back/pallas_call | solution.py:517
  361.7 5.8 all-to-all-start.6
  368.0 15.1 %spatial_wgrad.2 = (bf16[4,4,576,128]{3,2,1,0:T(8,128)(2,1)}, bf16[4,4,576,128]{3,2,1,0:T(8,128)(2,1)}) custom-call(s32[1,2]{1,0:T(1,128)} %copy-done.26, bf16[1792,512]{1,0:T(8,128)(2,1)} %get-tuple-element.146.act, bf16[1792,512]{1,0:T(8,128)(2,1)} %get-tuple-element.147.g), custom_call_target="tpu_custom_call" | custom-call | flops 8455716864 | bytes 8388608 | tf_op jit(solution)/shard_map/spatial_wgrad/pallas_call | solution.py:751
  384.1 19.8 %reduce_back.1 = (bf16[1792,512]{1,0:T(8,128)(2,1)}, bf16[1792,2048]{1,0:T(8,128)(2,1)}, f32[2,2048]{1,0:T(2,128)}) custom-call(f32[1,1]{1,0:T(1,128)} %bitcast.18.inv, f32[1792,512]{1,0:T(8,128)} %get-tuple-element.144.e1, f32[1792,512]{1,0:T(8,128)} %get-tuple-element.126.h1, f32[2,512]{1,0:T(2,128)} %reshape.524.tot.tot1, ...), custom_call_target="tpu_custom_call" | custom-call | flops 3758096384 | bytes 38535168 | tf_op jit(solution)/shard_map/reduce_back/pallas_call | solution.py:572
  418.3 8.1 %wgrad.4 = bf16[2048,512]{1,0:T(8,128)(2,1)} custom-call(bf16[1792,2048]{1,0:T(8,128)(2,1)} %get-tuple-element.131.x.left, bf16[1792,512]{1,0:T(8,128)(2,1)} %get-tuple-element.155.right), custom_call_target="tpu_custom_call" | custom-call | flops 3758096384 | bytes 11272192 | tf_op jit(solution)/shard_map/wgrad/pallas_call | solution.py:651
  430.2 3.5 fusion.11
  437.2 16.0 %expand_back.3 = (bf16[1792,2048]{1,0:T(8,128)(2,1)}, f32[1792,512]{1,0:T(8,128)}, f32[2,512]{1,0:T(2,128)}) custom-call(f32[1,1]{1,0:T(1,128)} %bitcast.18.inv, bf16[1792,2048]{1,0:T(8,128)(2,1)} %get-tuple-element.188.e3, bf16[1792,2048]{1,0:T(8,128)(2,1)} %get-tuple-element.124.h3, f32[2,2048]{1,0:T(2,128)} %reshape.523.tot.tot3, ...), custom_call_target="tpu_custom_call" | custom-call | flops 3758096384 | bytes 29360128 | tf_op jit(solution)/shard_map/expand_back/pallas_call | solution.py:458
  453.2 8.2 %wgrad.5 = bf16[512,2048]{1,0:T(8,128)(2,1)} custom-call(bf16[1792,512]{1,0:T(8,128)(2,1)} %get-tuple-element.162.left, bf16[1792,2048]{1,0:T(8,128)(2,1)} %get-tuple-element.163.right), custom_call_target="tpu_custom_call" | custom-call | flops 3758096384 | bytes 11272192 | tf_op jit(solution)/shard_map/wgrad/pallas_call | solution.py:651
  461.4 8.3 %collective-permute-done.38 = bf16[4,576,128]{2,1,0:T(8,128)(2,1)} collective-permute-done((bf16[4,576,128]{2,1,0:T(8,128)(2,1)}, bf16[4,576,128]{2,1,0:T(8,128)(2,1)}, u32[]{:S(2)}, u32[]{:S(2)}) %collective-permute-start.38) | collective-permute-done | bytes 589856 | tf_op jit(solution)/shard_map/ppermute | solution.py:868
  470.4 4.2 all-to-all-start.7
  486.6 17.4 %spatial_back.3 = (bf16[1792,512]{1,0:T(8,128)(2,1)}, f32[1792,512]{1,0:T(8,128)}, f32[2,512]{1,0:T(2,128)}) custom-call(f32[1,1]{1,0:T(1,128)} %bitcast.18.inv, f32[1792,512]{1,0:T(8,128)} %get-tuple-element.157.e2, f32[1792,512]{1,0:T(8,128)} %get-tuple-element.122.h2, f32[2,512]{1,0:T(2,128)} %reshape.521.tot.tot2, f32[2,512]{1,0:T(2,128)} %get-tuple-element.241.gb.gb2, ...), custom_call_target="tpu_custom_call" | custom-call | flops 8455716864 | bytes 21233664 | tf_op jit(solution)/shard_map/spatial_back/pallas_call | solution.py:517
  505.5 4.6 all-to-all-start.8
  510.4 15.2 %spatial_wgrad.3 = (bf16[4,4,576,128]{3,2,1,0:T(8,128)(2,1)}, bf16[4,4,576,128]{3,2,1,0:T(8,128)(2,1)}) custom-call(s32[1,2]{1,0:T(1,128)} %copy-done.26, bf16[1792,512]{1,0:T(8,128)(2,1)} %get-tuple-element.176.act, bf16[1792,512]{1,0:T(8,128)(2,1)} %get-tuple-element.177.g), custom_call_target="tpu_custom_call" | custom-call | flops 8455716864 | bytes 8388608 | tf_op jit(solution)/shard_map/spatial_wgrad/pallas_call | solution.py:751
  531.8 12.0 %reduce_wgrad.1 = bf16[2048,512]{1,0:T(8,128)(2,1)} custom-call(f32[1,1]{1,0:T(1,128)} %bitcast.18.inv, f32[1792,512]{1,0:T(8,128)} %get-tuple-element.165.e1, f32[1792,512]{1,0:T(8,128)} %get-tuple-element.120.h1, f32[2,512]{1,0:T(2,128)} %slice.279.tot.tot1, f32[2,512]{1,0:T(2,128)} %get-tuple-element.240.gb.gb1, f32[2,512]{1,0:T(2,128)} %reshape.539.btot1, ...), custom_call_target="tpu_custom_call" | custom-call | flops 3758096384 | bytes 14680064 | tf_op jit(solution)/shard_map/reduce_wgrad/pallas_call | solution.py:679
  546.4 4.0 fusion.16
  566.9 16.8 %features_back.1 = f32[49,36,2048]{2,1,0:T(8,128)} custom-call(f32[1,1]{1,0:T(1,128)} %bitcast.18.inv, f32[1792,512]{1,0:T(8,128)} %get-tuple-element.165.e1, f32[1792,512]{1,0:T(8,128)} %get-tuple-element.120.h1, f32[2,512]{1,0:T(2,128)} %slice.279.tot.tot1, f32[2,512]{1,0:T(2,128)} %get-tuple-element.240.gb.gb1, f32[2,512]{1,0:T(2,128)} %reshape.539.btot1, ...), custom_call_target="tpu_custom_call" | custom-call | flops 3758096384 | bytes 31195136 | tf_op jit(solution)/shard_map/features_back/pallas_call | solution.py:614
  583.7 5.6 collective-permute-done.48
  604.9 3.3 collective-permute-done.55
  614.2 3.9 all-to-all-start.9
  618.1 4.1 collective-permute-done.51
  626.8 3.4 all-to-all-done.9
  (354 shorter events, 169.0 us)
Async XLA Ops:
  7.2 53.5 %all-gather.17.cloned.1.call-start = ((), (), s32[]{:S(2)}) async-start(), calls=%async_computation.20 | async-start | bytes 2359296 | tf_op jit(solution)/shard_map/all_gather | solution.py:911
  9.2 117.8 %all-gather.19.cloned.1.call-start = ((), (), s32[]{:S(2)}) async-start(), calls=%async_computation.21 | async-start | bytes 2359296 | tf_op jit(solution)/shard_map/all_gather | solution.py:913
  10.2 144.1 %all-gather.21.cloned.1.call-start = ((), (), s32[]{:S(2)}) async-start(), calls=%async_computation.22 | async-start | bytes 2359296 | tf_op jit(solution)/shard_map/all_gather | solution.py:911
  10.9 173.2 %all-gather.23.cloned.1.call-start = ((), (), s32[]{:S(2)}) async-start(), calls=%async_computation.23 | async-start | bytes 5308416 | tf_op jit(solution)/shard_map/all_gather | solution.py:912
  11.9 202.8 %all-gather.25.cloned.1.call-start = ((), (), s32[]{:S(2)}) async-start(), calls=%async_computation.24 | async-start | bytes 2359296 | tf_op jit(solution)/shard_map/all_gather | solution.py:913
  12.5 254.1 %all-gather.13.cloned.1.call-start = ((), (), s32[]{:S(2)}) async-start(), calls=%async_computation.14 | async-start | bytes 6561792 | tf_op jit(solution)/shard_map/all_gather | solution.py:928
  13.7 17.0 %collective-permute-start = (bf16[576,128]{1,0:T(8,128)(2,1)S(1)}, bf16[576,128]{1,0:T(8,128)(2,1)S(1)}, u32[]{:S(2)}, u32[]{:S(2)}) collective-permute-start(bf16[576,128]{1,0:T(8,128)(2,1)S(1)} %dynamic-slice_bitcast_fusion), channel_id=1, source_target_pairs={{0,2},{1,3},{2,0},{3,1},{4,6},{5,7},{6,4},{7,5},{8,10},{9,11},{10,... | collective-permute-start | bytes 442376 | tf_op jit(solution)/shard_map/ppermute | solution.py:807
  16.8 18.9 %collective-permute-start.1 = (bf16[576,128]{1,0:T(8,128)(2,1)S(1)}, bf16[576,128]{1,0:T(8,128)(2,1)S(1)}, u32[]{:S(2)}, u32[]{:S(2)}) collective-permute-start(bf16[576,128]{1,0:T(8,128)(2,1)S(1)} %dynamic-slice_bitcast_fusion), channel_id=1, source_target_pairs={{0,4},{1,5},{2,6},{3,7},{4,0},{5,1},{6,2},{7,3},{8,12},{9,13},{10,... | collective-permute-start | bytes 442376 | tf_op jit(solution)/shard_map/ppermute | solution.py:807
  19.4 16.3 %collective-permute-start.2 = (bf16[576,128]{1,0:T(8,128)(2,1)S(1)}, bf16[576,128]{1,0:T(8,128)(2,1)S(1)}, u32[]{:S(2)}, u32[]{:S(2)}) collective-permute-start(bf16[576,128]{1,0:T(8,128)(2,1)S(1)} %dynamic-slice_bitcast_fusion), channel_id=1, source_target_pairs={{0,6},{1,7},{2,4},{3,5},{4,2},{5,3},{6,0},{7,1},{8,14},{9,15},{10,... | collective-permute-start | bytes 442376 | tf_op jit(solution)/shard_map/ppermute | solution.py:807
  35.8 16.3 %collective-permute-start.3 = (bf16[4,576,128]{2,1,0:T(8,128)(2,1)S(1)}, bf16[4,576,128]{2,1,0:T(8,128)(2,1)S(1)}, u32[]{:S(2)}, u32[]{:S(2)}) collective-permute-start(bf16[4,576,128]{2,1,0:T(8,128)(2,1)S(1)} %get-tuple-element.226), channel_id=1, source_target_pairs={{0,8},{8,0},{16,24},{24,16},{1,9},{9,1},{17,25},{25,17},{2,10},{10... | collective-permute-start | bytes 1769480 | tf_op jit(solution)/shard_map/ppermute | solution.py:807
  37.4 23.0 %collective-permute-start.4 = (bf16[4,576,128]{2,1,0:T(8,128)(2,1)S(1)}, bf16[4,576,128]{2,1,0:T(8,128)(2,1)S(1)}, u32[]{:S(2)}, u32[]{:S(2)}) collective-permute-start(bf16[4,576,128]{2,1,0:T(8,128)(2,1)S(1)} %get-tuple-element.226), channel_id=1, source_target_pairs={{0,16},{8,24},{16,0},{24,8},{1,17},{9,25},{17,1},{25,9},{2,18},{10... | collective-permute-start | bytes 1769480 | tf_op jit(solution)/shard_map/ppermute | solution.py:807
  38.9 21.4 %collective-permute-start.5 = (bf16[4,576,128]{2,1,0:T(8,128)(2,1)S(1)}, bf16[4,576,128]{2,1,0:T(8,128)(2,1)S(1)}, u32[]{:S(2)}, u32[]{:S(2)}) collective-permute-start(bf16[4,576,128]{2,1,0:T(8,128)(2,1)S(1)} %get-tuple-element.226), channel_id=1, source_target_pairs={{0,24},{8,16},{16,8},{24,0},{1,25},{9,17},{17,9},{25,1},{2,26},{10... | collective-permute-start | bytes 1769480 | tf_op jit(solution)/shard_map/ppermute | solution.py:807
  60.7 10.8 %collective-permute-start.6 = (bf16[4,4,576,128]{3,2,1,0:T(8,128)(2,1)S(1)}, bf16[4,4,576,128]{3,2,1,0:T(8,128)(2,1)S(1)}, u32[]{:S(2)}, u32[]{:S(2)}) collective-permute-start(bf16[4,4,576,128]{3,2,1,0:T(8,128)(2,1)S(1)} %pad_maximum_fusion.own), channel_id=1, source_target_pairs={{0,1},{1,0},{2,3},{3,2},{4,5},{5,4},{6,7},{7,6},{8,9},{9,8},{10,11... | collective-permute-start | bytes 7077896 | tf_op jit(solution)/shard_map/ppermute | solution.py:968
  75.0 21.0 %all-to-all-start = ((f32[32,8,256]{2,1,0:T(8,128)}), f32[32,8,256]{2,1,0:T(8,128)S(1)}, u32[]{:S(2)}, u32[]{:S(2)}) async-start(f32[32,8,256]{2,1,0:T(8,128)} %broadcast_in_dim.73), calls=%async_computation | async-start | bytes 524288 | tf_op jit(solution)/shard_map/all_to_all | solution.py:829
  201.8 12.3 %all-to-all-start.3 = ((f32[32,8,128]{2,1,0:T(8,128)}), f32[32,8,128]{2,1,0:T(8,128)S(1)}, u32[]{:S(2)}, u32[]{:S(2)}) async-start(f32[32,8,128]{2,1,0:T(8,128)} %broadcast_in_dim.79), calls=%async_computation.3 | async-start | bytes 262144 | tf_op jit(solution)/shard_map/all_to_all | solution.py:829
  205.9 221.2 %all-gather.15.cloned.1.call-start = ((), (), s32[]{:S(2)}) async-start(), calls=%async_computation.15 | async-start | bytes 1327104 | tf_op jit(solution)/shard_map/all_gather | solution.py:1001
  227.6 11.2 %collective-permute-start.15 = (f32[8,512]{1,0:T(8,128)S(1)}, f32[8,512]{1,0:T(8,128)S(1)}, u32[]{:S(2)}, u32[]{:S(2)}) collective-permute-start(f32[8,512]{1,0:T(8,128)S(1)} %add.294), channel_id=1, source_target_pairs={{0,2},{1,3},{2,4},{3,5},{4,6},{5,7},{6,0},{7,1},{8,10},{9,11},{10,... | collective-permute-start | bytes 49160 | tf_op jit(solution)/shard_map/ppermute | solution.py:817
  275.3 19.6 %all-to-all-start.4 = ((bf16[8,48,256]{2,1,0:T(8,128)(2,1)}), bf16[8,48,256]{2,1,0:T(8,128)(2,1)S(1)}, u32[]{:S(2)}, u32[]{:S(2)}) async-start(bf16[8,48,256]{2,1,0:T(8,128)(2,1)} %bitcast.151), calls=%async_computation.4 | async-start | bytes 393216 | tf_op jit(solution)/shard_map/all_to_all | solution.py:994
  329.5 12.7 %all-to-all-start.5 = ((f32[32,8,128]{2,1,0:T(8,128)}), f32[32,8,128]{2,1,0:T(8,128)S(1)}, u32[]{:S(2)}, u32[]{:S(2)}) async-start(f32[32,8,128]{2,1,0:T(8,128)} %broadcast_in_dim.82), calls=%async_computation.5 | async-start | bytes 262144 | tf_op jit(solution)/shard_map/all_to_all | solution.py:829
  334.0 149.5 %reduce-scatter.7.cloned.1.call-start = ((), (), s32[]{:S(2)}) async-start(), calls=%async_computation.17 | async-start | bytes 2359296 | tf_op jit(solution)/shard_map/reduce_scatter | solution.py:1026
  361.7 21.4 %all-to-all-start.6 = ((f32[32,8,128]{2,1,0:T(8,128)}), f32[32,8,128]{2,1,0:T(8,128)S(1)}, u32[]{:S(2)}, u32[]{:S(2)}) async-start(f32[32,8,128]{2,1,0:T(8,128)} %broadcast_in_dim.84), calls=%async_computation.6 | async-start | bytes 262144 | tf_op jit(solution)/shard_map/all_to_all | solution.py:829
  367.5 117.1 %reduce-scatter.5.cloned.1.call-start = ((), (), s32[]{:S(2)}) async-start(), calls=%async_computation.16 | async-start | bytes 2359296 | tf_op jit(solution)/shard_map/reduce_scatter | solution.py:1062
  383.8 20.1 %collective-permute-start.28 = (bf16[4,4,576,128]{3,2,1,0:T(8,128)(2,1)}, bf16[4,4,576,128]{3,2,1,0:T(8,128)(2,1)}, u32[]{:S(2)}, u32[]{:S(2)}) collective-permute-start(bf16[4,4,576,128]{3,2,1,0:T(8,128)(2,1)} %get-tuple-element.153), channel_id=1, source_target_pairs={{0,1},{1,0},{2,3},{3,2},{4,5},{5,4},{6,7},{7,6},{8,9},{9,8},{10,11... | collective-permute-start | bytes 7077896 | tf_op jit(solution)/shard_map/ppermute | solution.py:863
  413.7 12.7 %collective-permute-start.33 = (f32[8,512]{1,0:T(8,128)S(1)}, f32[8,512]{1,0:T(8,128)S(1)}, u32[]{:S(2)}, u32[]{:S(2)}) collective-permute-start(f32[8,512]{1,0:T(8,128)S(1)} %add_add_fusion.1), channel_id=1, source_target_pairs={{0,8},{8,16},{16,24},{24,0},{1,9},{9,17},{17,25},{25,1},{2,10},{10... | collective-permute-start | bytes 49160 | tf_op jit(solution)/shard_map/ppermute | solution.py:817
  415.2 11.2 %collective-permute-start.34 = (f32[8,512]{1,0:T(8,128)S(1)}, f32[8,512]{1,0:T(8,128)S(1)}, u32[]{:S(2)}, u32[]{:S(2)}) collective-permute-start(f32[8,512]{1,0:T(8,128)S(1)} %add_add_fusion.1), channel_id=1, source_target_pairs={{0,16},{8,24},{16,0},{24,8},{1,17},{9,25},{17,1},{25,9},{2,18},{10... | collective-permute-start | bytes 49160 | tf_op jit(solution)/shard_map/ppermute | solution.py:817
  429.5 74.5 %collective-permute-start.42 = (bf16[640,512]{1,0:T(8,128)(2,1)S(1)}, bf16[640,512]{1,0:T(8,128)(2,1)S(1)}, u32[]{:S(2)}, u32[]{:S(2)}) collective-permute-start(bf16[640,512]{1,0:T(8,128)(2,1)S(1)} %slice.302), channel_id=1, source_target_pairs={{0,8},{8,0},{16,24},{24,16},{1,9},{9,1},{17,25},{25,17},{2,10},{10... | collective-permute-start | bytes 1966088 | tf_op jit(solution)/shard_map/ppermute | solution.py:847
  433.7 27.8 %collective-permute-start.36 = (bf16[4,576,128]{2,1,0:T(8,128)(2,1)}, bf16[4,576,128]{2,1,0:T(8,128)(2,1)S(1)}, u32[]{:S(2)}, u32[]{:S(2)}) collective-permute-start(bf16[4,576,128]{2,1,0:T(8,128)(2,1)} %get-tuple-element.212), channel_id=1, source_target_pairs={{0,8},{8,0},{16,24},{24,16},{1,9},{9,1},{17,25},{25,17},{2,10},{10... | collective-permute-start | bytes 1769480 | tf_op jit(solution)/shard_map/ppermute | solution.py:868
  435.1 26.3 %collective-permute-start.37 = (bf16[4,576,128]{2,1,0:T(8,128)(2,1)}, bf16[4,576,128]{2,1,0:T(8,128)(2,1)}, u32[]{:S(2)}, u32[]{:S(2)}) collective-permute-start(bf16[4,576,128]{2,1,0:T(8,128)(2,1)} %get-tuple-element.211), channel_id=1, source_target_pairs={{0,16},{8,24},{16,0},{24,8},{1,17},{9,25},{17,1},{25,9},{2,18},{10... | collective-permute-start | bytes 1769480 | tf_op jit(solution)/shard_map/ppermute | solution.py:868
  435.6 34.1 %collective-permute-start.38 = (bf16[4,576,128]{2,1,0:T(8,128)(2,1)}, bf16[4,576,128]{2,1,0:T(8,128)(2,1)}, u32[]{:S(2)}, u32[]{:S(2)}) collective-permute-start(bf16[4,576,128]{2,1,0:T(8,128)(2,1)} %get-tuple-element.210), channel_id=1, source_target_pairs={{0,24},{8,16},{16,8},{24,0},{1,25},{9,17},{17,9},{25,1},{2,26},{10... | collective-permute-start | bytes 1769480 | tf_op jit(solution)/shard_map/ppermute | solution.py:868
  470.4 12.4 %all-to-all-start.7 = ((f32[32,8,128]{2,1,0:T(8,128)}), f32[32,8,128]{2,1,0:T(8,128)S(1)}, u32[]{:S(2)}, u32[]{:S(2)}) async-start(f32[32,8,128]{2,1,0:T(8,128)} %broadcast_in_dim.86), calls=%async_computation.7 | async-start | bytes 262144 | tf_op jit(solution)/shard_map/all_to_all | solution.py:829
  474.6 109.1 %reduce-scatter.11.cloned.1.call-start = ((), (), s32[]{:S(2)}) async-start(), calls=%async_computation.19 | async-start | bytes 2359296 | tf_op jit(solution)/shard_map/reduce_scatter | solution.py:1026
  477.5 26.6 %collective-permute-start.39 = (bf16[576,128]{1,0:T(8,128)(2,1)S(1)}, bf16[576,128]{1,0:T(8,128)(2,1)}, u32[]{:S(2)}, u32[]{:S(2)}) collective-permute-start(bf16[576,128]{1,0:T(8,128)(2,1)S(1)} %get-tuple-element.224), channel_id=1, source_target_pairs={{0,2},{1,3},{2,0},{3,1},{4,6},{5,7},{6,4},{7,5},{8,10},{9,11},{10,... | collective-permute-start | bytes 442376 | tf_op jit(solution)/shard_map/ppermute | solution.py:868
  479.3 24.7 %collective-permute-start.40 = (bf16[576,128]{1,0:T(8,128)(2,1)S(1)}, bf16[576,128]{1,0:T(8,128)(2,1)}, u32[]{:S(2)}, u32[]{:S(2)}) collective-permute-start(bf16[576,128]{1,0:T(8,128)(2,1)S(1)} %get-tuple-element.223), channel_id=1, source_target_pairs={{0,4},{1,5},{2,6},{3,7},{4,0},{5,1},{6,2},{7,3},{8,12},{9,13},{10,... | collective-permute-start | bytes 442376 | tf_op jit(solution)/shard_map/ppermute | solution.py:868
  481.7 22.3 %collective-permute-start.41 = (bf16[576,128]{1,0:T(8,128)(2,1)S(1)}, bf16[576,128]{1,0:T(8,128)(2,1)}, u32[]{:S(2)}, u32[]{:S(2)}) collective-permute-start(bf16[576,128]{1,0:T(8,128)(2,1)S(1)} %get-tuple-element.222), channel_id=1, source_target_pairs={{0,6},{1,7},{2,4},{3,5},{4,2},{5,3},{6,0},{7,1},{8,14},{9,15},{10,... | collective-permute-start | bytes 442376 | tf_op jit(solution)/shard_map/ppermute | solution.py:868
  485.6 18.5 %collective-permute-start.43 = (bf16[640,512]{1,0:T(8,128)(2,1)S(1)}, bf16[640,512]{1,0:T(8,128)(2,1)}, u32[]{:S(2)}, u32[]{:S(2)}) collective-permute-start(bf16[640,512]{1,0:T(8,128)(2,1)S(1)} %pad_maximum_fusion.3), channel_id=1, source_target_pairs={{0,16},{8,24},{16,0},{24,8},{1,17},{9,25},{17,1},{25,9},{2,18},{10... | collective-permute-start | bytes 1966088 | tf_op jit(solution)/shard_map/ppermute | solution.py:847
  505.5 20.1 %all-to-all-start.8 = ((f32[32,8,128]{2,1,0:T(8,128)}), f32[32,8,128]{2,1,0:T(8,128)S(1)}, u32[]{:S(2)}, u32[]{:S(2)}) async-start(f32[32,8,128]{2,1,0:T(8,128)} %broadcast_in_dim.88), calls=%async_computation.10 | async-start | bytes 262144 | tf_op jit(solution)/shard_map/all_to_all | solution.py:829
  510.1 80.6 %reduce-scatter.9.cloned.1.call-start = ((), (), s32[]{:S(2)}) async-start(), calls=%async_computation.18 | async-start | bytes 2359296 | tf_op jit(solution)/shard_map/reduce_scatter | solution.py:1076
  526.2 20.2 %collective-permute-start.46 = (bf16[4,4,576,128]{3,2,1,0:T(8,128)(2,1)}, bf16[4,4,576,128]{3,2,1,0:T(8,128)(2,1)}, u32[]{:S(2)}, u32[]{:S(2)}) collective-permute-start(bf16[4,4,576,128]{3,2,1,0:T(8,128)(2,1)} %get-tuple-element.184), channel_id=1, source_target_pairs={{0,1},{1,0},{2,3},{3,2},{4,5},{5,4},{6,7},{7,6},{8,9},{9,8},{10,11... | collective-permute-start | bytes 7077896 | tf_op jit(solution)/shard_map/ppermute | solution.py:863
  527.7 17.1 %collective-permute-start.45 = (bf16[640,512]{1,0:T(8,128)(2,1)S(1)}, bf16[640,512]{1,0:T(8,128)(2,1)}, u32[]{:S(2)}, u32[]{:S(2)}) collective-permute-start(bf16[640,512]{1,0:T(8,128)(2,1)S(1)} %add_convert_fusion.2), channel_id=1, source_target_pairs={{0,8},{8,0},{16,24},{24,16},{1,9},{9,1},{17,25},{25,17},{2,10},{10... | collective-permute-start | bytes 1966088 | tf_op jit(solution)/shard_map/ppermute | solution.py:847
  529.6 16.8 %collective-permute-start.44 = (bf16[640,512]{1,0:T(8,128)(2,1)S(1)}, bf16[640,512]{1,0:T(8,128)(2,1)S(1)}, u32[]{:S(2)}, u32[]{:S(2)}) collective-permute-start(bf16[640,512]{1,0:T(8,128)(2,1)S(1)} %add_convert_fusion.3), channel_id=1, source_target_pairs={{0,16},{8,24},{16,0},{24,8},{1,17},{9,25},{17,1},{25,9},{2,18},{10... | collective-permute-start | bytes 1966088 | tf_op jit(solution)/shard_map/ppermute | solution.py:847
  562.3 21.3 %collective-permute-start.47 = (bf16[4,576,128]{2,1,0:T(8,128)(2,1)}, bf16[4,576,128]{2,1,0:T(8,128)(2,1)}, u32[]{:S(2)}, u32[]{:S(2)}) collective-permute-start(bf16[4,576,128]{2,1,0:T(8,128)(2,1)} %get-tuple-element.191), channel_id=1, source_target_pairs={{0,8},{8,0},{16,24},{24,16},{1,9},{9,1},{17,25},{25,17},{2,10},{10... | collective-permute-start | bytes 1769480 | tf_op jit(solution)/shard_map/ppermute | solution.py:868
  562.7 26.6 %collective-permute-start.48 = (bf16[4,576,128]{2,1,0:T(8,128)(2,1)}, bf16[4,576,128]{2,1,0:T(8,128)(2,1)}, u32[]{:S(2)}, u32[]{:S(2)}) collective-permute-start(bf16[4,576,128]{2,1,0:T(8,128)(2,1)} %get-tuple-element.192), channel_id=1, source_target_pairs={{0,16},{8,24},{16,0},{24,8},{1,17},{9,25},{17,1},{25,9},{2,18},{10... | collective-permute-start | bytes 1769480 | tf_op jit(solution)/shard_map/ppermute | solution.py:868
  564.4 26.3 %collective-permute-start.49 = (bf16[4,576,128]{2,1,0:T(8,128)(2,1)}, bf16[4,576,128]{2,1,0:T(8,128)(2,1)}, u32[]{:S(2)}, u32[]{:S(2)}) collective-permute-start(bf16[4,576,128]{2,1,0:T(8,128)(2,1)} %get-tuple-element.193), channel_id=1, source_target_pairs={{0,24},{8,16},{16,8},{24,0},{1,25},{9,17},{17,9},{25,1},{2,26},{10... | collective-permute-start | bytes 1769480 | tf_op jit(solution)/shard_map/ppermute | solution.py:868
  590.7 18.7 %collective-permute-start.50 = (bf16[256,512]{1,0:T(8,128)(2,1)}, bf16[256,512]{1,0:T(8,128)(2,1)}, u32[]{:S(2)}, u32[]{:S(2)}) collective-permute-start(bf16[256,512]{1,0:T(8,128)(2,1)} %reduce-scatter.9.cloned.1.call-done), channel_id=1, source_target_pairs={{0,8},{8,0},{16,24},{24,16},{1,9},{9,1},{17,25},{25,17},{2,10},{10... | collective-permute-start | bytes 786440 | tf_op jit(solution)/shard_map/ppermute | solution.py:847
  594.1 10.8 %collective-permute-start.54 = (bf16[576,128]{1,0:T(8,128)(2,1)}, bf16[576,128]{1,0:T(8,128)(2,1)}, u32[]{:S(2)}, u32[]{:S(2)}) collective-permute-start(bf16[576,128]{1,0:T(8,128)(2,1)} %get-tuple-element.219), channel_id=1, source_target_pairs={{0,2},{1,3},{2,0},{3,1},{4,6},{5,7},{6,4},{7,5},{8,10},{9,11},{10,... | collective-permute-start | bytes 442376 | tf_op jit(solution)/shard_map/ppermute | solution.py:868
  595.5 12.6 %collective-permute-start.55 = (bf16[576,128]{1,0:T(8,128)(2,1)}, bf16[576,128]{1,0:T(8,128)(2,1)}, u32[]{:S(2)}, u32[]{:S(2)}) collective-permute-start(bf16[576,128]{1,0:T(8,128)(2,1)} %get-tuple-element.221), channel_id=1, source_target_pairs={{0,4},{1,5},{2,6},{3,7},{4,0},{5,1},{6,2},{7,3},{8,12},{9,13},{10,... | collective-permute-start | bytes 442376 | tf_op jit(solution)/shard_map/ppermute | solution.py:868
  610.4 11.8 %collective-permute-start.51 = (bf16[256,512]{1,0:T(8,128)(2,1)S(1)}, bf16[256,512]{1,0:T(8,128)(2,1)S(1)}, u32[]{:S(2)}, u32[]{:S(2)}) collective-permute-start(bf16[256,512]{1,0:T(8,128)(2,1)S(1)} %add_convert_fusion.16), channel_id=1, source_target_pairs={{0,16},{8,24},{16,0},{24,8},{1,17},{9,25},{17,1},{25,9},{2,18},{10... | collective-permute-start | bytes 786440 | tf_op jit(solution)/shard_map/ppermute | solution.py:847
  614.2 16.1 %all-to-all-start.9 = ((bf16[4,2,576,128]{3,2,1,0:T(8,128)(2,1)}), bf16[4,2,576,128]{3,2,1,0:T(8,128)(2,1)S(1)}, u32[]{:S(2)}, u32[]{:S(2)}) async-start(bf16[4,2,576,128]{3,2,1,0:T(8,128)(2,1)} %broadcast_in_dim.89), calls=%async_computation.13 | async-start | bytes 2359296 | tf_op jit(solution)/shard_map/all_to_all | solution.py:1090
  (61 other events, 484.0 us)
Sparse Core Ops, SparseCore 0:
  10.2 40.6 all-gather.16
  52.5 29.2 all-gather.18
  83.9 29.3 all-gather.20
  115.4 52.1 all-gather.22
  169.1 30.2 all-gather.24
  201.3 63.2 all-gather.12
  274.7 23.8 all-gather.14
  343.0 37.3 reduce-scatter.6
  427.2 34.6 reduce-scatter.4
  483.6 38.7 reduce-scatter.10
  550.5 35.8 reduce-scatter.8

commit v4 on v3

--- a/solution.py
+++ b/solution.py
@@ -107,6 +107,8 @@
         self.low = (SIDE + 1) * self.rest
         self.rows = self.top + self.low
         self.total = SIDE * self.rows
+        self.step = self.total // 4
+        self.half = self.total // 2
         self.padded = self.main + 16
 
 
@@ -149,9 +151,9 @@
     c, m = w.shape
     return pl.pallas_call(
         reduce_kernel,
-        grid=(SIDE,),
-        in_specs=[tile(sh.rows, c), whole((c, m))],
-        out_specs=[tile(sh.rows, m), whole((2, m))],
+        grid=(sh.total // sh.step,),
+        in_specs=[tile(sh.step, c), whole((c, m))],
+        out_specs=[tile(sh.step, m), whole((2, m))],
         out_shape=[sds((sh.total, m), F32), sds((2, m), F32)],
         compiler_params=params(1),
         cost_estimate=cost(2 * sh.total * c * m, 2 * sh.total * c + 4 * sh.total * m),
@@ -245,16 +247,16 @@
     m, c = w.shape
     return pl.pallas_call(
         expand_kernel,
-        grid=(SIDE,),
+        grid=(sh.total // sh.step,),
         in_specs=[
             pl.BlockSpec(memory_space=pltpu.SMEM),
-            tile(sh.rows, m),
-            whole((2, m)),
-            whole((2, m)),
-            tile(sh.rows, 1),
+            tile(sh.step, m),
+            whole((2, m)),
+            whole((2, m)),
+            tile(sh.step, 1),
             whole((m, c)),
         ],
-        out_specs=[tile(sh.rows, m), tile(sh.rows, c), whole((2, c))],
+        out_specs=[tile(sh.step, m), tile(sh.step, c), whole((2, c))],
         out_shape=[sds((sh.total, m), BF), sds((sh.total, c), BF), sds((2, c), F32)],
         compiler_params=params(1),
         cost_estimate=cost(2 * sh.total * c * m, 2 * sh.total * c + 6 * sh.total * m),
@@ -282,17 +284,17 @@
     c, m = w.shape
     return pl.pallas_call(
         join_kernel,
-        grid=(SIDE,),
+        grid=(sh.total // sh.step,),
         in_specs=[
             pl.BlockSpec(memory_space=pltpu.SMEM),
-            tile(sh.rows, c),
-            tile(sh.rows, c),
+            tile(sh.step, c),
+            tile(sh.step, c),
             whole((2, c)),
             whole((2, c)),
-            tile(sh.rows, 1),
+            tile(sh.step, 1),
             whole((c, m)),
         ],
-        out_specs=[tile(sh.rows, c), tile(sh.rows, m), whole((2, m))],
+        out_specs=[tile(sh.step, c), tile(sh.step, m), whole((2, m))],
         out_shape=[sds((sh.total, c), BF), sds((sh.total, m), F32), sds((2, m), F32)],
         compiler_params=params(1),
         cost_estimate=cost(2 * sh.total * c * m, 6 * sh.total * c + 4 * sh.total * m),
@@ -457,21 +459,21 @@
     m, c = w.shape
     return pl.pallas_call(
         expand_back_kernel,
-        grid=(SIDE,),
+        grid=(sh.total // sh.half,),
         in_specs=[
             pl.BlockSpec(memory_space=pltpu.SMEM),
-            tile(sh.rows, c),
-            tile(sh.rows, c),
+            tile(sh.half, c),
+            tile(sh.half, c),
             whole((2, c)),
             whole((2, c)),
             whole((2, c)),
-            tile(sh.rows, 1),
+            tile(sh.half, 1),
             whole((m, c)),
-            tile(sh.rows, m),
-            whole((2, m)),
-            whole((2, m)),
-        ],
-        out_specs=[tile(sh.rows, c), tile(sh.rows, m), whole((2, m))],
+            tile(sh.half, m),
+            whole((2, m)),
+            whole((2, m)),
+        ],
+        out_specs=[tile(sh.half, c), tile(sh.half, m), whole((2, m))],
         out_shape=[sds((sh.total, c), BF), sds((sh.total, m), F32), sds((2, m), F32)],
         compiler_params=params(1),
         cost_estimate=cost(2 * sh.total * c * m, 6 * sh.total * c + 8 * sh.total * m),
@@ -571,23 +573,23 @@
     c, m = w.shape
     return pl.pallas_call(
         reduce_back_kernel,
-        grid=(SIDE,),
+        grid=(sh.total // sh.step,),
         in_specs=[
             pl.BlockSpec(memory_space=pltpu.SMEM),
-            tile(sh.rows, m),
-            tile(sh.rows, m),
-            whole((2, m)),
-            whole((2, m)),
-            whole((2, m)),
-            tile(sh.rows, 1),
+            tile(sh.step, m),
+            tile(sh.step, m),
+            whole((2, m)),
+            whole((2, m)),
+            whole((2, m)),
+            tile(sh.step, 1),
             whole((c, m)),
-            tile(sh.rows, c),
-            tile(sh.rows, c),
-            tile(sh.rows, c),
+            tile(sh.step, c),
+            tile(sh.step, c),
+            tile(sh.step, c),
             whole((2, c)),
             whole((2, c)),
         ],
-        out_specs=[tile(sh.rows, m), tile(sh.rows, c), whole((2, c))],
+        out_specs=[tile(sh.step, m), tile(sh.step, c), whole((2, c))],
         out_shape=[sds((sh.total, m), BF), sds((sh.total, c), BF), sds((2, c), F32)],
         compiler_params=params(1),
         cost_estimate=cost(2 * sh.total * c * m, 8 * sh.total * c + 10 * sh.total * m),
@@ -669,7 +671,7 @@
     for c in range(0, x.shape[1], step):
         acc[c : c + step, :] += tn(x[:, c : c + step], g)
 
-    @pl.when(pl.program_id(0) == SIDE - 1)
+    @pl.when(pl.program_id(0) == pl.num_programs(0) - 1)
     def _():
         out[...] = acc[...].astype(BF)
 
@@ -678,16 +680,16 @@
     c, m = x.shape[1], e1.shape[1]
     return pl.pallas_call(
         reduce_wgrad_kernel,
-        grid=(SIDE,),
+        grid=(sh.total // sh.step,),
         in_specs=[
             pl.BlockSpec(memory_space=pltpu.SMEM),
-            tile(sh.rows, m),
-            tile(sh.rows, m),
-            whole((2, m)),
-            whole((2, m)),
-            whole((2, m)),
-            tile(sh.rows, 1),
-            tile(sh.rows, c),
+            tile(sh.step, m),
+            tile(sh.step, m),
+            whole((2, m)),
+            whole((2, m)),
+            whole((2, m)),
+            tile(sh.step, 1),
+            tile(sh.step, c),
         ],
         out_specs=whole((c, m)),
         out_shape=sds((c, m), BF),
@@ -817,10 +819,10 @@
     return sum([lax.ppermute(v, axis, way) for way in ways], v)
 
 
-def total_of(v, sizes):
+def total_of(v, sizes, beside=False):
     dp, fsdp = sizes
     flat = v.reshape(8, -1)
-    if flat.size > 2048:
+    if flat.size > 2048 and not beside:
         flat = flat + lax.ppermute(flat, "fsdp", [(i, i ^ 1) for i in range(fsdp)])
         flat = others(flat, "fsdp", fsdp, 2)
         return others(flat, "dp", dp, 1).reshape(v.shape)
@@ -1031,8 +1033,7 @@
         )
         grad = spatial_wgrad(sh, act1, g2, place, owners, dp, short)
         if short and b + 1 < blocks:
-            part, *got = in_order(part, *swap_rest(swaps[b + 1], "fsdp", owners, 2))
-            shards["spatial", b + 1] = added(swaps[b + 1][0], *got)
+            part, *chips = in_order(part, *swap_rest(swaps[b + 1], "fsdp", owners, 2))
         if b == 0:
             early = [head_grad] + [shards["reduce", k] for k in range(1, blocks)]
             early += [shards["expand", k] for k in range(1, blocks)]
@@ -1041,6 +1042,8 @@
             halves = copies_add(halves, swapped)
             swapped = copies_swap(halves, dp, 1)
         btot1 = total_of(part, (dp, owners))
+        if b == 0:
+            btot1, *swapped = in_order(btot1, *swapped)
         btot1, *grad = in_order(btot1, *grad)
         if short:
             other = swap_core(grad, owners)
@@ -1057,46 +1060,59 @@
                 part, other = in_order(part, other)
                 swaps[b] = [added(grad[0][j], other[j]) for j in range(dp)]
             grad = wgrad(x, g1, inner)
-            btot3 = total_of(part, (dp, owners))
+            btot3 = total_of(part, (dp, owners), True)
             btot3, grad = in_order(btot3, grad)
             shards["reduce", b] = scatter(grad)
         else:
-            spatial = grad
-            grad = reduce_wgrad(sh, e1, h1, tot1, gb_mid[b, 0], btot1, inv, mask, x)
-            grad, *swapped = in_order(grad, *swapped)
-            halves = copies_add(halves, swapped)
             if short:
-                grad, other = in_order(grad, other)
-                swaps[b] = [added(spatial[0][j], other[j]) for j in range(dp)]
-                e3, grad, *swaps[b] = in_order(e3, grad, *swaps[b])
+                swaps[b] = [added(grad[0][j], other[j]) for j in range(dp)]
+                e1, *swaps[b] = in_order(e1, *swaps[b])
                 got = swap_rest(swaps[b], "dp", dp, 1)
             else:
-                e3, grad = in_order(e3, grad)
                 got = [shards["spatial", k] for k in range(blocks)]
+            grad = reduce_wgrad(sh, e1, h1, tot1, gb_mid[b, 0], btot1, inv, mask, x)
+            if short:
+                grad, *got[:2] = in_order(grad, *got[:2])
+            expand_halves = copies_halves([shards["expand", b]])
+            grad, *other = in_order(grad, *copies_swap(expand_halves, dp, 0))
+            expand_halves = copies_add(expand_halves, other)
+            e3, grad = in_order(e3, grad)
             shards["reduce", b] = scatter(grad)
             grad_features = features_back(
                 sh, e1, h1, tot1, gb_mid[b, 0], btot1, inv, mask, w1, e3
             )
-            grad_features, shards["reduce", b], shards["expand", b], *got = in_order(
-                grad_features, shards["reduce", b], shards["expand", b], *got
+            grad_features, *rest = in_order(
+                grad_features, *swapped, *got, *(chips if short else [])
             )
+            grad_features, shards["reduce", b] = in_order(grad_features, shards["reduce", b])
+            swapped = rest[:2]
+            got, chips = rest[2 : 2 + len(got)], rest[2 + len(got) :]
 
     if short:
         total = added(swaps[0][0], *got)
         total = [total[k] for k in range(owners // 2)]
-        shards["spatial", 0] = added(total[0], *swap_rest(total, "fsdp", owners, 2))
+        late_halves = copies_halves([shards["reduce", 0]])
+        steps = in_order(*swap_rest(total, "fsdp", owners, 2), *copies_swap(late_halves, dp, 0), *swapped)
+        shards["spatial", 0] = added(total[0], *steps[:-4])
+        late_halves, swapped = copies_add(late_halves, steps[-4:-2]), steps[-2:]
+        shards["spatial", 1] = added(swaps[1][0], *chips)
         flat = jnp.stack([shards["spatial", b] for b in range(blocks)])
         flat = jnp.broadcast_to(flat[None], (dp,) + flat.shape)
         flat = lax.all_to_all(flat, "dp", 0, 0, tiled=True)
         spatial = jnp.transpose(flat, (1, 2, 0, 3)).reshape(w_spatial.shape).astype(F32) / SCALE
+    halves = copies_add(halves, swapped)
     sums = copies_out(halves, early)
-    late = [shards["reduce", 0], shards["expand", 0]] + ([] if short else got)
-    lates = copies_out(copies_sum(copies_halves(late), dp), late)
+    late = [shards["reduce", 0]] + ([] if short else got)
+    if short:
+        lates = copies_out(copies_sum(late_halves, dp, 1), late)
+    else:
+        lates = copies_out(copies_sum(copies_halves(late), dp), late)
+    expand_sum = copies_out(copies_sum(expand_halves, dp, 1), [shards["expand", 0]])
     head_grad = sums[0]
     reduce_all = jnp.stack([lates[0]] + sums[1:blocks])
-    expand_all = jnp.stack([lates[1]] + sums[blocks:])
+    expand_all = jnp.stack(expand_sum + sums[blocks:])
     if not short:
-        spatial = jnp.stack(lates[2:])
+        spatial = jnp.stack(lates[1:])
     at = [(place, size) for place, size in zip(offsets, sizes)]
 
     def gains(pair):

time: 651 us -> 643 us (0.988)
  Pallas kernels: 302 us -> 289 us
  waiting for transfers between devices: 95.9 us -> 103 us
    ppermute x24 -> x18, starting transfers between devices: 39.9 us -> 25.5 us  [others(): return sum([lax.ppermute(v, axis, way) for way in ways], v)]
    all_gather x1, waiting for transfers between devices: 0.01 us -> 14.3 us  [on_device(): head_all = lax.all_gather(head_t, 'fsdp', axis=1, tiled=True)]
    pallas_call x8, Pallas kernels: 110 us -> 96.6 us  [the longest x2 26.3 us: expand_back(): pl.pallas_call(expand_back_kernel, grid=(sh.total // sh.half,), in_specs=...]
    ppermute x24 -> x18, waiting for transfers between devices: 23.2 us -> 15.3 us  [others(): return sum([lax.ppermute(v, axis, way) for way in ways], v)]
    all_to_all x6 -> x7, waiting for transfers between devices: 12.6 us -> 19.7 us  [total_of(): got = lax.all_to_all(spread, AXES, 0, 0, tiled=True)]
    ppermute x8 -> x12, starting transfers between devices: 9.36 us -> 13.8 us  [copies_swap(): lax.ppermute(half, 'dp', [(i, i ^ (bits, bits[::-1])[h][turn]) for i in r...]
    all_to_all x6 -> x7, starting transfers between devices: 33.8 us -> 38.1 us  [total_of(): got = lax.all_to_all(spread, AXES, 0, 0, tiled=True)]
    convert_element_type x11 -> x12, other arithmetic: 15.3 us -> 14.8 us  [added(): sum([v.astype(F32) for v in terms[1:]], terms[0].astype(F32)).astype(BF)]
  transfers between devices with their start and end apart: 76 -> 74, of which waited for: 35 -> 33; matrix products, arithmetic and copies ran while one was open for 12% -> 11% of each run, Pallas kernels for 46% -> 44%
where the time goes in v4:
time: 643 us; the launch traced here: 632 us
  Pallas kernels  289 us (45%)
  starting transfers between devices  114 us (18%)
  waiting for transfers between devices  103 us (16%)
  local copies, waits for them, and re-layouts  48 us (7%)
  other arithmetic  36 us (6%)
  blocking collectives  24.1 us (4%)
  between operations  16 us (2%)
    all_to_all x7, starting transfers between devices, total_of(): got = lax.all_to_all(spread, AXES, 0, 0, tiled=True)  38.1 us
    pallas_call x2, Pallas kernels, spatial_back(): pl.pallas_call(functools.partial(spatial_back_kernel, sh), grid=(SIDE + 1...  34.9 us
    pallas_call x2, Pallas kernels, spatial_conv(): pl.pallas_call(functools.partial(spatial_kernel, sh), grid=(SIDE + 1,), i...  32.7 us
    pallas_call x2, Pallas kernels, spatial_wgrad(): pl.pallas_call(functools.partial(spatial_wgrad_kernel, sh, owned), grid=(...  30.5 us
    pallas_call x2, Pallas kernels, expand_back(): pl.pallas_call(expand_back_kernel, grid=(sh.total // sh.half,), in_specs=...  26.3 us
    ppermute x6, waiting for transfers between devices, flips(): lax.ppermute(v, axis, [(i, i ^ unit * k) for i in range(size)])  26 us
    ppermute x18, starting transfers between devices, others(): return sum([lax.ppermute(v, axis, way) for way in ways], v)  25.5 us
    pallas_call x3, Pallas kernels, wgrad(): pl.pallas_call(wgrad_kernel, grid=(max(a, b) // step,), in_specs=specs, o...  24.5 us
  transfers between devices with their start and end apart: 74, of which 33 were waited for; matrix products, arithmetic and copies ran while one was open for 11% of the time, Pallas kernels for 44%

profile of v4, /device:TPU:0, one launch (start us, length us, event | category | flops | bytes accessed | tf_op | source)
XLA Modules:
  0.0 632.0 jit_solution(11001489867373802296)
XLA Ops:
  13.7 3.1 collective-permute-start
  16.8 2.6 collective-permute-start.1
  21.1 9.5 %prep.1.x = bf16[1792,2048]{1,0:T(8,128)(2,1)} custom-call(bf16[49,36,2048]{2,1,0:T(8,128)(2,1)} %bitcast.178, f32[1792,1]{1,0:T(8,128)} %bitcast.156), custom_call_target="tpu_custom_call" | custom-call | tf_op jit(solution)/shard_map/prep/pallas_call | solution.py:128
  30.7 5.0 collective-permute-done.1
  39.3 12.8 %collective-permute-done.3 = bf16[4,576,128]{2,1,0:T(8,128)(2,1)S(1)} collective-permute-done((bf16[4,576,128]{2,1,0:T(8,128)(2,1)S(1)}, bf16[4,576,128]{2,1,0:T(8,128)(2,1)S(1)}, u32[]{:S(2)}, u32[]{:S(2)}) %collective-permute-start.3) | collective-permute-done | bytes 589856 | tf_op jit(solution)/shard_map/ppermute | solution.py:809
  52.1 8.2 %collective-permute-done.4 = bf16[4,576,128]{2,1,0:T(8,128)(2,1)S(1)} collective-permute-done((bf16[4,576,128]{2,1,0:T(8,128)(2,1)S(1)}, bf16[4,576,128]{2,1,0:T(8,128)(2,1)S(1)}, u32[]{:S(2)}, u32[]{:S(2)}) %collective-permute-start.4) | collective-permute-done | bytes 589856 | tf_op jit(solution)/shard_map/ppermute | solution.py:809
  61.5 8.5 %reduce_conv.1 = (f32[1792,512]{1,0:T(8,128)}, f32[2,512]{1,0:T(2,128)}) custom-call(bf16[1792,2048]{1,0:T(8,128)(2,1)} %prep.1.x, bf16[2048,512]{1,0:T(8,128)(2,1)} %bitcast.183), custom_call_target="tpu_custom_call" | custom-call | flops 3758096384 | bytes 11010048 | tf_op jit(solution)/shard_map/reduce_conv/pallas_call | solution.py:152
  73.5 10.7 %all-to-all-start = ((f32[32,8,256]{2,1,0:T(8,128)}), f32[32,8,256]{2,1,0:T(8,128)S(1)}, u32[]{:S(2)}, u32[]{:S(2)}) async-start(f32[32,8,256]{2,1,0:T(8,128)} %broadcast_in_dim.80), calls=%async_computation | async-start | bytes 524288 | tf_op jit(solution)/shard_map/all_to_all | solution.py:831
  84.8 5.5 assemble.1.w
  90.3 4.2 all-to-all-done
  96.4 16.4 %spatial_conv.2 = (bf16[1792,512]{1,0:T(8,128)(2,1)}, f32[1792,512]{1,0:T(8,128)}, f32[2,512]{1,0:T(2,128)}) custom-call(f32[1,1]{1,0:T(1,128)} %bitcast.18.inv, f32[1792,512]{1,0:T(8,128)} %get-tuple-element.137.h1, f32[2,512]{1,0:T(2,128)} %slice.291.tot.tot1, f32[2,512]{1,0:T(2,128)} %get-tuple-element.278.gb.gb1, f32[1792,1]{1,0:T(8,128)} %bitcast.157, ...), custom_call_target="tpu_custom_call" | custom-call | flops 8455716864 | bytes 13893632 | tf_op jit(solution)/shard_map/spatial_conv/pallas_call | solution.py:205
  113.5 10.5 %all_to_all.55 = f32[32,8,128]{2,1,0:T(8,128)S(1)} all-to-all(f32[32,8,128]{2,1,0:T(8,128)S(1)} %broadcast_in_dim.82), channel_id=1, replica_groups=mesh['dp'=4,'fsdp'=8] {'dp','fsdp'}, dimensions={0} | all-to-all | bytes 262144 | tf_op jit(solution)/shard_map/all_to_all | solution.py:831
  124.7 9.1 %expand_conv.2 = (bf16[1792,512]{1,0:T(8,128)(2,1)}, bf16[1792,2048]{1,0:T(8,128)(2,1)}, f32[2,2048]{1,0:T(2,128)}) custom-call(f32[1,1]{1,0:T(1,128)} %bitcast.18.inv, f32[1792,512]{1,0:T(8,128)} %get-tuple-element.139.h2, f32[2,512]{1,0:T(2,128)} %reshape.567.tot.tot2, f32[2,512]{1,0:T(2,128)} %get-tuple-element.279.gb.gb2, f32[1792,1]{1,0:T(8,128)} %bitcast.159, ...), custom_call_target="tpu_custom_call" | custom-call | flops 3758096384 | bytes 12845056 | tf_op jit(solution)/shard_map/expand_conv/pallas_call | solution.py:248
  140.3 2.8 collective-permute-done.8
  149.9 13.5 %join.1 = (bf16[1792,2048]{1,0:T(8,128)(2,1)}, f32[1792,512]{1,0:T(8,128)}, f32[2,512]{1,0:T(2,128)}) custom-call(f32[1,1]{1,0:T(1,128)} %bitcast.18.inv, bf16[1792,2048]{1,0:T(8,128)(2,1)} %get-tuple-element.141.h3, bf16[1792,2048]{1,0:T(8,128)(2,1)} %prep.1.x, f32[2,2048]{1,0:T(2,128)} %reshape.569.tot.tot3, f32[2,2048]{1,0:T(2,128)} %get-tuple-element.270.gb.gb3, ...), custom_call_target="tpu_custom_call" | custom-call | flops 3758096384 | bytes 25690112 | tf_op jit(solution)/shard_map/join/pallas_call | solution.py:285
  164.1 13.6 %all_to_all.56 = f32[32,8,128]{2,1,0:T(8,128)S(1)} all-to-all(f32[32,8,128]{2,1,0:T(8,128)S(1)} %broadcast_in_dim.84), channel_id=1, replica_groups=mesh['dp'=4,'fsdp'=8] {'dp','fsdp'}, dimensions={0} | all-to-all | bytes 262144 | tf_op jit(solution)/shard_map/all_to_all | solution.py:831
  178.4 16.3 %spatial_conv.3 = (bf16[1792,512]{1,0:T(8,128)(2,1)}, f32[1792,512]{1,0:T(8,128)}, f32[2,512]{1,0:T(2,128)}) custom-call(f32[1,1]{1,0:T(1,128)} %bitcast.18.inv, f32[1792,512]{1,0:T(8,128)} %get-tuple-element.143.h1, f32[2,512]{1,0:T(2,128)} %reshape.570.tot.tot1, f32[2,512]{1,0:T(2,128)} %get-tuple-element.280.gb.gb1, f32[1792,1]{1,0:T(8,128)} %bitcast.161, ...), custom_call_target="tpu_custom_call" | custom-call | flops 8455716864 | bytes 13893632 | tf_op jit(solution)/shard_map/spatial_conv/pallas_call | solution.py:205
  199.5 7.3 %all-to-all-done.3 = f32[32,8,128]{2,1,0:T(8,128)S(1)} async-done(((f32[32,8,128]{2,1,0:T(8,128)}), f32[32,8,128]{2,1,0:T(8,128)S(1)}, u32[]{:S(2)}, u32[]{:S(2)}) %all-to-all-start.3) | async-done | bytes 131104 | tf_op jit(solution)/shard_map/all_to_all | solution.py:831
  207.4 9.4 %expand_conv.3 = (bf16[1792,512]{1,0:T(8,128)(2,1)}, bf16[1792,2048]{1,0:T(8,128)(2,1)}, f32[2,2048]{1,0:T(2,128)}) custom-call(f32[1,1]{1,0:T(1,128)} %bitcast.18.inv, f32[1792,512]{1,0:T(8,128)} %get-tuple-element.145.h2, f32[2,512]{1,0:T(2,128)} %reshape.571.tot.tot2, f32[2,512]{1,0:T(2,128)} %get-tuple-element.277.gb.gb2, f32[1792,1]{1,0:T(8,128)} %bitcast.163, ...), custom_call_target="tpu_custom_call" | custom-call | flops 3758096384 | bytes 12845056 | tf_op jit(solution)/shard_map/expand_conv/pallas_call | solution.py:248
  234.5 13.5 %last_join.1 = (bf16[49,36,2048]{2,1,0:T(8,128)(2,1)}, bf16[48,2048]{1,0:T(8,128)(2,1)}) custom-call(f32[1,1]{1,0:T(1,128)} %bitcast.18.inv, bf16[1792,2048]{1,0:T(8,128)(2,1)} %get-tuple-element.147.h3, bf16[1792,2048]{1,0:T(8,128)(2,1)} %get-tuple-element.148.x.left, f32[2,2048]{1,0:T(2,128)} %reshape.573.tot.tot3, f32[2,2048]{1,0:T(2,128)} %get-tuple-element.269.gb.gb3, ...), custom_call_target="tpu_custom_call" | custom-call | flops 352321536 | bytes 22020096 | tf_op jit(solution)/shard_map/last_join/pallas_call | solution.py:328
  248.0 14.3 %all-gather.13.cloned.1.call-done.w = bf16[1424,2048]{1,0:T(8,128)(2,1)} async-done(((bf16[1424,256]{1,0:T(8,128)(2,1)}), bf16[1424,2048]{1,0:T(8,128)(2,1)}) %all-gather.13.cloned.1.call-update) | async-done | bytes 5832720 | tf_op jit(solution)/shard_map/all_gather | solution.py:930
  262.3 7.9 %heads.1 = (f32[48,2048]{1,0:T(8,128)}, bf16[48,1536]{1,0:T(8,128)(2,1)}) custom-call(bf16[48,2048]{1,0:T(8,128)(2,1)} %get-tuple-element.151.pooled, s32[48,3]{1,0:T(8,128)} %pad.26.labels, f32[48,1]{1,0:T(8,128)} %copy.122.area, s32[48,2048]{1,0:T(8,128)} %pad.27.bits, bf16[1424,2048]{1,0:T(8,128)(2,1)} %all-gather.13.cloned.1.call-done.w), custom_call_target="tpu_custom_call" | custom-call | flops 603979776 | bytes 5832704 | tf_op jit(solution)/shard_map/heads/pallas_call | solution.py:384
  271.0 3.4 all-to-all-start.4
  274.4 16.2 %top_grad.1 = (bf16[1792,2048]{1,0:T(8,128)(2,1)}, f32[2,2048]{1,0:T(2,128)}) custom-call(f32[1,1]{1,0:T(1,128)} %bitcast.18.inv, f32[48,2048]{1,0:T(8,128)} %get-tuple-element.152.merged, bf16[1792,2048]{1,0:T(8,128)(2,1)} %get-tuple-element.147.h3, bf16[1792,2048]{1,0:T(8,128)(2,1)} %get-tuple-element.148.x.left, f32[2,2048]{1,0:T(2,128)} %reshape.573.tot.tot3, ...), custom_call_target="tpu_custom_call" | custom-call | flops 73400320 | bytes 22020096 | tf_op jit(solution)/shard_map/top_grad/pallas_call | solution.py:417
  308.4 13.2 %expand_back.2 = (bf16[1792,2048]{1,0:T(8,128)(2,1)}, f32[1792,512]{1,0:T(8,128)}, f32[2,512]{1,0:T(2,128)}) custom-call(f32[1,1]{1,0:T(1,128)} %bitcast.18.inv, bf16[1792,2048]{1,0:T(8,128)(2,1)} %get-tuple-element.153.e3, bf16[1792,2048]{1,0:T(8,128)(2,1)} %get-tuple-element.147.h3, f32[2,2048]{1,0:T(2,128)} %reshape.573.tot.tot3, ...), custom_call_target="tpu_custom_call" | custom-call | flops 3758096384 | bytes 29360128 | tf_op jit(solution)/shard_map/expand_back/pallas_call | solution.py:460
  323.0 5.4 all-to-all-start.5
  328.5 8.2 %wgrad.3 = bf16[512,2048]{1,0:T(8,128)(2,1)} custom-call(bf16[1792,512]{1,0:T(8,128)(2,1)} %get-tuple-element.158.left, bf16[1792,2048]{1,0:T(8,128)(2,1)} %get-tuple-element.159.right), custom_call_target="tpu_custom_call" | custom-call | flops 3758096384 | bytes 11272192 | tf_op jit(solution)/shard_map/wgrad/pallas_call | solution.py:653
  337.3 17.5 %spatial_back.2 = (bf16[1792,512]{1,0:T(8,128)(2,1)}, f32[1792,512]{1,0:T(8,128)}, f32[2,512]{1,0:T(2,128)}) custom-call(f32[1,1]{1,0:T(1,128)} %bitcast.18.inv, f32[1792,512]{1,0:T(8,128)} %get-tuple-element.156.e2, f32[1792,512]{1,0:T(8,128)} %get-tuple-element.145.h2, f32[2,512]{1,0:T(2,128)} %reshape.571.tot.tot2, f32[2,512]{1,0:T(2,128)} %get-tuple-element.277.gb.gb2, ...), custom_call_target="tpu_custom_call" | custom-call | flops 8455716864 | bytes 21233664 | tf_op jit(solution)/shard_map/spatial_back/pallas_call | solution.py:519
  356.2 6.3 all-to-all-start.6
  362.5 15.1 %spatial_wgrad.2 = (bf16[4,4,576,128]{3,2,1,0:T(8,128)(2,1)}, bf16[4,4,576,128]{3,2,1,0:T(8,128)(2,1)}) custom-call(s32[1,2]{1,0:T(1,128)} %copy-done.30, bf16[1792,512]{1,0:T(8,128)(2,1)} %get-tuple-element.163.act, bf16[1792,512]{1,0:T(8,128)(2,1)} %get-tuple-element.164.g), custom_call_target="tpu_custom_call" | custom-call | flops 8455716864 | bytes 8388608 | tf_op jit(solution)/shard_map/spatial_wgrad/pallas_call | solution.py:753
  378.6 19.2 %reduce_back.1 = (bf16[1792,512]{1,0:T(8,128)(2,1)}, bf16[1792,2048]{1,0:T(8,128)(2,1)}, f32[2,2048]{1,0:T(2,128)}) custom-call(f32[1,1]{1,0:T(1,128)} %bitcast.18.inv, f32[1792,512]{1,0:T(8,128)} %get-tuple-element.161.e1, f32[1792,512]{1,0:T(8,128)} %get-tuple-element.143.h1, f32[2,512]{1,0:T(2,128)} %reshape.570.tot.tot1, ...), custom_call_target="tpu_custom_call" | custom-call | flops 3758096384 | bytes 38535168 | tf_op jit(solution)/shard_map/reduce_back/pallas_call | solution.py:574
  399.5 5.7 all-to-all-start.7
  405.2 8.2 %wgrad.4 = bf16[2048,512]{1,0:T(8,128)(2,1)} custom-call(bf16[1792,2048]{1,0:T(8,128)(2,1)} %get-tuple-element.148.x.left, bf16[1792,512]{1,0:T(8,128)(2,1)} %get-tuple-element.172.right), custom_call_target="tpu_custom_call" | custom-call | flops 3758096384 | bytes 11272192 | tf_op jit(solution)/shard_map/wgrad/pallas_call | solution.py:653
  413.4 8.1 %all-to-all-done.7 = f32[32,8,512]{2,1,0:T(8,128)S(1)} async-done(((f32[32,8,512]{2,1,0:T(8,128)}), f32[32,8,512]{2,1,0:T(8,128)S(1)}, u32[]{:S(2)}, u32[]{:S(2)}) %all-to-all-start.7) | async-done | bytes 524320 | tf_op jit(solution)/shard_map/all_to_all | solution.py:831
  422.3 2.9 fusion.11
  431.2 13.1 %expand_back.3 = (bf16[1792,2048]{1,0:T(8,128)(2,1)}, f32[1792,512]{1,0:T(8,128)}, f32[2,512]{1,0:T(2,128)}) custom-call(f32[1,1]{1,0:T(1,128)} %bitcast.18.inv, bf16[1792,2048]{1,0:T(8,128)(2,1)} %get-tuple-element.209.e3, bf16[1792,2048]{1,0:T(8,128)(2,1)} %get-tuple-element.141.h3, f32[2,2048]{1,0:T(2,128)} %reshape.569.tot.tot3, ...), custom_call_target="tpu_custom_call" | custom-call | flops 3758096384 | bytes 29360128 | tf_op jit(solution)/shard_map/expand_back/pallas_call | solution.py:460
  444.3 9.3 %collective-permute-done.30 = bf16[4,576,128]{2,1,0:T(8,128)(2,1)} collective-permute-done((bf16[4,576,128]{2,1,0:T(8,128)(2,1)}, bf16[4,576,128]{2,1,0:T(8,128)(2,1)}, u32[]{:S(2)}, u32[]{:S(2)}) %collective-permute-start.30) | collective-permute-done | bytes 589856 | tf_op jit(solution)/shard_map/ppermute | solution.py:870
  465.6 8.2 %wgrad.5 = bf16[512,2048]{1,0:T(8,128)(2,1)} custom-call(bf16[1792,512]{1,0:T(8,128)(2,1)} %get-tuple-element.179.left, bf16[1792,2048]{1,0:T(8,128)(2,1)} %get-tuple-element.180.right), custom_call_target="tpu_custom_call" | custom-call | flops 3758096384 | bytes 11272192 | tf_op jit(solution)/shard_map/wgrad/pallas_call | solution.py:653
  478.3 17.4 %spatial_back.3 = (bf16[1792,512]{1,0:T(8,128)(2,1)}, f32[1792,512]{1,0:T(8,128)}, f32[2,512]{1,0:T(2,128)}) custom-call(f32[1,1]{1,0:T(1,128)} %bitcast.18.inv, f32[1792,512]{1,0:T(8,128)} %get-tuple-element.174.e2, f32[1792,512]{1,0:T(8,128)} %get-tuple-element.139.h2, f32[2,512]{1,0:T(2,128)} %reshape.567.tot.tot2, f32[2,512]{1,0:T(2,128)} %get-tuple-element.279.gb.gb2, ...), custom_call_target="tpu_custom_call" | custom-call | flops 8455716864 | bytes 21233664 | tf_op jit(solution)/shard_map/spatial_back/pallas_call | solution.py:519
  499.0 4.8 all-to-all-start.9
  503.8 15.4 %spatial_wgrad.3 = (bf16[4,4,576,128]{3,2,1,0:T(8,128)(2,1)}, bf16[4,4,576,128]{3,2,1,0:T(8,128)(2,1)}) custom-call(s32[1,2]{1,0:T(1,128)} %copy-done.30, bf16[1792,512]{1,0:T(8,128)(2,1)} %get-tuple-element.196.act, bf16[1792,512]{1,0:T(8,128)(2,1)} %get-tuple-element.197.g), custom_call_target="tpu_custom_call" | custom-call | flops 8455716864 | bytes 8388608 | tf_op jit(solution)/shard_map/spatial_wgrad/pallas_call | solution.py:753
  524.7 3.3 fusion.16
  533.3 10.7 %reduce_wgrad.1 = bf16[2048,512]{1,0:T(8,128)(2,1)} custom-call(f32[1,1]{1,0:T(1,128)} %bitcast.18.inv, f32[1792,512]{1,0:T(8,128)} %get-tuple-element.202.e1, f32[1792,512]{1,0:T(8,128)} %get-tuple-element.137.h1, f32[2,512]{1,0:T(2,128)} %slice.291.tot.tot1, f32[2,512]{1,0:T(2,128)} %get-tuple-element.278.gb.gb1, f32[2,512]{1,0:T(2,128)} %reshape.584.btot1, ...), custom_call_target="tpu_custom_call" | custom-call | flops 3758096384 | bytes 14680064 | tf_op jit(solution)/shard_map/reduce_wgrad/pallas_call | solution.py:681
  557.1 16.8 %features_back.1 = f32[49,36,2048]{2,1,0:T(8,128)} custom-call(f32[1,1]{1,0:T(1,128)} %bitcast.18.inv, f32[1792,512]{1,0:T(8,128)} %get-tuple-element.202.e1, f32[1792,512]{1,0:T(8,128)} %get-tuple-element.137.h1, f32[2,512]{1,0:T(2,128)} %slice.291.tot.tot1, f32[2,512]{1,0:T(2,128)} %get-tuple-element.278.gb.gb1, f32[2,512]{1,0:T(2,128)} %reshape.584.btot1, ...), custom_call_target="tpu_custom_call" | custom-call | flops 3758096384 | bytes 31195136 | tf_op jit(solution)/shard_map/features_back/pallas_call | solution.py:616
  581.8 3.1 reduce-scatter.11.cloned.1.call-done
  601.8 4.4 all-to-all-start.10
  616.9 3.9 collective-permute-done.50
  622.0 3.0 copy_bitcast_fusion
  (364 shorter events, 168.5 us)
Async XLA Ops:
  7.2 53.4 %all-gather.17.cloned.1.call-start = ((), (), s32[]{:S(2)}) async-start(), calls=%async_computation.21 | async-start | bytes 2359296 | tf_op jit(solution)/shard_map/all_gather | solution.py:913
  9.2 115.4 %all-gather.19.cloned.1.call-start = ((), (), s32[]{:S(2)}) async-start(), calls=%async_computation.22 | async-start | bytes 2359296 | tf_op jit(solution)/shard_map/all_gather | solution.py:915
  10.1 139.8 %all-gather.21.cloned.1.call-start = ((), (), s32[]{:S(2)}) async-start(), calls=%async_computation.23 | async-start | bytes 2359296 | tf_op jit(solution)/shard_map/all_gather | solution.py:913
  10.9 167.4 %all-gather.23.cloned.1.call-start = ((), (), s32[]{:S(2)}) async-start(), calls=%async_computation.24 | async-start | bytes 5308416 | tf_op jit(solution)/shard_map/all_gather | solution.py:914
  11.9 195.5 %all-gather.25.cloned.1.call-start = ((), (), s32[]{:S(2)}) async-start(), calls=%async_computation.25 | async-start | bytes 2359296 | tf_op jit(solution)/shard_map/all_gather | solution.py:915
  12.5 249.8 %all-gather.13.cloned.1.call-start = ((), (), s32[]{:S(2)}) async-start(), calls=%async_computation.15 | async-start | bytes 6561792 | tf_op jit(solution)/shard_map/all_gather | solution.py:930
  13.7 17.0 %collective-permute-start = (bf16[576,128]{1,0:T(8,128)(2,1)S(1)}, bf16[576,128]{1,0:T(8,128)(2,1)S(1)}, u32[]{:S(2)}, u32[]{:S(2)}) collective-permute-start(bf16[576,128]{1,0:T(8,128)(2,1)S(1)} %dynamic-slice_bitcast_fusion), channel_id=1, source_target_pairs={{0,2},{1,3},{2,0},{3,1},{4,6},{5,7},{6,4},{7,5},{8,10},{9,11},{10,... | collective-permute-start | bytes 442376 | tf_op jit(solution)/shard_map/ppermute | solution.py:809
  16.8 18.9 %collective-permute-start.1 = (bf16[576,128]{1,0:T(8,128)(2,1)S(1)}, bf16[576,128]{1,0:T(8,128)(2,1)S(1)}, u32[]{:S(2)}, u32[]{:S(2)}) collective-permute-start(bf16[576,128]{1,0:T(8,128)(2,1)S(1)} %dynamic-slice_bitcast_fusion), channel_id=1, source_target_pairs={{0,4},{1,5},{2,6},{3,7},{4,0},{5,1},{6,2},{7,3},{8,12},{9,13},{10,... | collective-permute-start | bytes 442376 | tf_op jit(solution)/shard_map/ppermute | solution.py:809
  19.4 16.3 %collective-permute-start.2 = (bf16[576,128]{1,0:T(8,128)(2,1)S(1)}, bf16[576,128]{1,0:T(8,128)(2,1)S(1)}, u32[]{:S(2)}, u32[]{:S(2)}) collective-permute-start(bf16[576,128]{1,0:T(8,128)(2,1)S(1)} %dynamic-slice_bitcast_fusion), channel_id=1, source_target_pairs={{0,6},{1,7},{2,4},{3,5},{4,2},{5,3},{6,0},{7,1},{8,14},{9,15},{10,... | collective-permute-start | bytes 442376 | tf_op jit(solution)/shard_map/ppermute | solution.py:809
  35.8 16.3 %collective-permute-start.3 = (bf16[4,576,128]{2,1,0:T(8,128)(2,1)S(1)}, bf16[4,576,128]{2,1,0:T(8,128)(2,1)S(1)}, u32[]{:S(2)}, u32[]{:S(2)}) collective-permute-start(bf16[4,576,128]{2,1,0:T(8,128)(2,1)S(1)} %get-tuple-element.258), channel_id=1, source_target_pairs={{0,8},{8,0},{16,24},{24,16},{1,9},{9,1},{17,25},{25,17},{2,10},{10... | collective-permute-start | bytes 1769480 | tf_op jit(solution)/shard_map/ppermute | solution.py:809
  37.3 23.0 %collective-permute-start.4 = (bf16[4,576,128]{2,1,0:T(8,128)(2,1)S(1)}, bf16[4,576,128]{2,1,0:T(8,128)(2,1)S(1)}, u32[]{:S(2)}, u32[]{:S(2)}) collective-permute-start(bf16[4,576,128]{2,1,0:T(8,128)(2,1)S(1)} %get-tuple-element.258), channel_id=1, source_target_pairs={{0,16},{8,24},{16,0},{24,8},{1,17},{9,25},{17,1},{25,9},{2,18},{10... | collective-permute-start | bytes 1769480 | tf_op jit(solution)/shard_map/ppermute | solution.py:809
  38.9 21.4 %collective-permute-start.5 = (bf16[4,576,128]{2,1,0:T(8,128)(2,1)S(1)}, bf16[4,576,128]{2,1,0:T(8,128)(2,1)S(1)}, u32[]{:S(2)}, u32[]{:S(2)}) collective-permute-start(bf16[4,576,128]{2,1,0:T(8,128)(2,1)S(1)} %get-tuple-element.258), channel_id=1, source_target_pairs={{0,24},{8,16},{16,8},{24,0},{1,25},{9,17},{17,9},{25,1},{2,26},{10... | collective-permute-start | bytes 1769480 | tf_op jit(solution)/shard_map/ppermute | solution.py:809
  73.5 21.1 %all-to-all-start = ((f32[32,8,256]{2,1,0:T(8,128)}), f32[32,8,256]{2,1,0:T(8,128)S(1)}, u32[]{:S(2)}, u32[]{:S(2)}) async-start(f32[32,8,256]{2,1,0:T(8,128)} %broadcast_in_dim.80), calls=%async_computation | async-start | bytes 524288 | tf_op jit(solution)/shard_map/all_to_all | solution.py:831
  196.0 10.8 %all-to-all-start.3 = ((f32[32,8,128]{2,1,0:T(8,128)}), f32[32,8,128]{2,1,0:T(8,128)S(1)}, u32[]{:S(2)}, u32[]{:S(2)}) async-start(f32[32,8,128]{2,1,0:T(8,128)} %broadcast_in_dim.86), calls=%async_computation.3 | async-start | bytes 262144 | tf_op jit(solution)/shard_map/all_to_all | solution.py:831
  198.6 230.1 %all-gather.15.cloned.1.call-start = ((), (), s32[]{:S(2)}) async-start(), calls=%async_computation.16 | async-start | bytes 1327104 | tf_op jit(solution)/shard_map/all_gather | solution.py:1003
  271.0 19.6 %all-to-all-start.4 = ((bf16[8,48,256]{2,1,0:T(8,128)(2,1)}), bf16[8,48,256]{2,1,0:T(8,128)(2,1)S(1)}, u32[]{:S(2)}, u32[]{:S(2)}) async-start(bf16[8,48,256]{2,1,0:T(8,128)(2,1)} %bitcast.153), calls=%async_computation.4 | async-start | bytes 393216 | tf_op jit(solution)/shard_map/all_to_all | solution.py:996
  323.0 13.7 %all-to-all-start.5 = ((f32[32,8,128]{2,1,0:T(8,128)}), f32[32,8,128]{2,1,0:T(8,128)S(1)}, u32[]{:S(2)}, u32[]{:S(2)}) async-start(f32[32,8,128]{2,1,0:T(8,128)} %broadcast_in_dim.89), calls=%async_computation.5 | async-start | bytes 262144 | tf_op jit(solution)/shard_map/all_to_all | solution.py:831
  328.4 146.0 %reduce-scatter.7.cloned.1.call-start = ((), (), s32[]{:S(2)}) async-start(), calls=%async_computation.18 | async-start | bytes 2359296 | tf_op jit(solution)/shard_map/reduce_scatter | solution.py:1028
  356.2 21.4 %all-to-all-start.6 = ((f32[32,8,128]{2,1,0:T(8,128)}), f32[32,8,128]{2,1,0:T(8,128)S(1)}, u32[]{:S(2)}, u32[]{:S(2)}) async-start(f32[32,8,128]{2,1,0:T(8,128)} %broadcast_in_dim.91), calls=%async_computation.6 | async-start | bytes 262144 | tf_op jit(solution)/shard_map/all_to_all | solution.py:831
  378.2 19.6 %collective-permute-start.28 = (bf16[4,4,576,128]{3,2,1,0:T(8,128)(2,1)}, bf16[4,4,576,128]{3,2,1,0:T(8,128)(2,1)}, u32[]{:S(2)}, u32[]{:S(2)}) collective-permute-start(bf16[4,4,576,128]{3,2,1,0:T(8,128)(2,1)} %get-tuple-element.170), channel_id=1, source_target_pairs={{0,1},{1,0},{2,3},{3,2},{4,5},{5,4},{6,7},{7,6},{8,9},{9,8},{10,11... | collective-permute-start | bytes 7077896 | tf_op jit(solution)/shard_map/ppermute | solution.py:865
  399.5 22.1 %all-to-all-start.7 = ((f32[32,8,512]{2,1,0:T(8,128)}), f32[32,8,512]{2,1,0:T(8,128)S(1)}, u32[]{:S(2)}, u32[]{:S(2)}) async-start(f32[32,8,512]{2,1,0:T(8,128)} %broadcast_in_dim.93), calls=%async_computation.7 | async-start | bytes 1048576 | tf_op jit(solution)/shard_map/all_to_all | solution.py:831
  405.2 70.4 %reduce-scatter.5.cloned.1.call-start = ((), (), s32[]{:S(2)}) async-start(), calls=%async_computation.17 | async-start | bytes 2359296 | tf_op jit(solution)/shard_map/reduce_scatter | solution.py:1065
  425.2 19.1 %collective-permute-start.29 = (bf16[4,576,128]{2,1,0:T(8,128)(2,1)}, bf16[4,576,128]{2,1,0:T(8,128)(2,1)}, u32[]{:S(2)}, u32[]{:S(2)}) collective-permute-start(bf16[4,576,128]{2,1,0:T(8,128)(2,1)} %get-tuple-element.246), channel_id=1, source_target_pairs={{0,8},{8,0},{16,24},{24,16},{1,9},{9,1},{17,25},{25,17},{2,10},{10... | collective-permute-start | bytes 1769480 | tf_op jit(solution)/shard_map/ppermute | solution.py:870
  425.2 28.4 %collective-permute-start.30 = (bf16[4,576,128]{2,1,0:T(8,128)(2,1)}, bf16[4,576,128]{2,1,0:T(8,128)(2,1)}, u32[]{:S(2)}, u32[]{:S(2)}) collective-permute-start(bf16[4,576,128]{2,1,0:T(8,128)(2,1)} %get-tuple-element.245), channel_id=1, source_target_pairs={{0,16},{8,24},{16,0},{24,8},{1,17},{9,25},{17,1},{25,9},{2,18},{10... | collective-permute-start | bytes 1769480 | tf_op jit(solution)/shard_map/ppermute | solution.py:870
  426.3 28.0 %collective-permute-start.31 = (bf16[4,576,128]{2,1,0:T(8,128)(2,1)}, bf16[4,576,128]{2,1,0:T(8,128)(2,1)}, u32[]{:S(2)}, u32[]{:S(2)}) collective-permute-start(bf16[4,576,128]{2,1,0:T(8,128)(2,1)} %get-tuple-element.244), channel_id=1, source_target_pairs={{0,24},{8,16},{16,8},{24,0},{1,25},{9,17},{17,9},{25,1},{2,26},{10... | collective-permute-start | bytes 1769480 | tf_op jit(solution)/shard_map/ppermute | solution.py:870
  431.1 64.7 %collective-permute-start.35 = (bf16[640,512]{1,0:T(8,128)(2,1)S(1)}, bf16[640,512]{1,0:T(8,128)(2,1)S(1)}, u32[]{:S(2)}, u32[]{:S(2)}) collective-permute-start(bf16[640,512]{1,0:T(8,128)(2,1)S(1)} %slice.314), channel_id=1, source_target_pairs={{0,8},{8,0},{16,24},{24,16},{1,9},{9,1},{17,25},{25,17},{2,10},{10... | collective-permute-start | bytes 1966088 | tf_op jit(solution)/shard_map/ppermute | solution.py:849
  455.7 18.1 %all-to-all-start.8 = ((f32[32,8,128]{2,1,0:T(8,128)}), f32[32,8,128]{2,1,0:T(8,128)S(1)}, u32[]{:S(2)}, u32[]{:S(2)}) async-start(f32[32,8,128]{2,1,0:T(8,128)} %broadcast_in_dim.95), calls=%async_computation.8 | async-start | bytes 262144 | tf_op jit(solution)/shard_map/all_to_all | solution.py:831
  458.3 72.9 %reduce-scatter.9.cloned.1.call-start = ((), (), s32[]{:S(2)}) async-start(), calls=%async_computation.19 | async-start | bytes 2359296 | tf_op jit(solution)/shard_map/reduce_scatter | solution.py:1028
  461.2 34.5 %collective-permute-start.32 = (bf16[576,128]{1,0:T(8,128)(2,1)}, bf16[576,128]{1,0:T(8,128)(2,1)}, u32[]{:S(2)}, u32[]{:S(2)}) collective-permute-start(bf16[576,128]{1,0:T(8,128)(2,1)} %get-tuple-element.256), channel_id=1, source_target_pairs={{0,2},{1,3},{2,0},{3,1},{4,6},{5,7},{6,4},{7,5},{8,10},{9,11},{10,... | collective-permute-start | bytes 442376 | tf_op jit(solution)/shard_map/ppermute | solution.py:870
  462.9 32.8 %collective-permute-start.33 = (bf16[576,128]{1,0:T(8,128)(2,1)}, bf16[576,128]{1,0:T(8,128)(2,1)}, u32[]{:S(2)}, u32[]{:S(2)}) collective-permute-start(bf16[576,128]{1,0:T(8,128)(2,1)} %get-tuple-element.255), channel_id=1, source_target_pairs={{0,4},{1,5},{2,6},{3,7},{4,0},{5,1},{6,2},{7,3},{8,12},{9,13},{10,... | collective-permute-start | bytes 442376 | tf_op jit(solution)/shard_map/ppermute | solution.py:870
  465.4 30.4 %collective-permute-start.34 = (bf16[576,128]{1,0:T(8,128)(2,1)S(1)}, bf16[576,128]{1,0:T(8,128)(2,1)}, u32[]{:S(2)}, u32[]{:S(2)}) collective-permute-start(bf16[576,128]{1,0:T(8,128)(2,1)S(1)} %get-tuple-element.254), channel_id=1, source_target_pairs={{0,6},{1,7},{2,4},{3,5},{4,2},{5,3},{6,0},{7,1},{8,14},{9,15},{10,... | collective-permute-start | bytes 442376 | tf_op jit(solution)/shard_map/ppermute | solution.py:870
  476.6 19.2 %collective-permute-start.36 = (bf16[640,512]{1,0:T(8,128)(2,1)S(1)}, bf16[640,512]{1,0:T(8,128)(2,1)S(1)}, u32[]{:S(2)}, u32[]{:S(2)}) collective-permute-start(bf16[640,512]{1,0:T(8,128)(2,1)S(1)} %pad_maximum_fusion.3), channel_id=1, source_target_pairs={{0,16},{8,24},{16,0},{24,8},{1,17},{9,25},{17,1},{25,9},{2,18},{10... | collective-permute-start | bytes 1966088 | tf_op jit(solution)/shard_map/ppermute | solution.py:849
  496.0 23.9 %collective-permute-start.38 = (bf16[640,512]{1,0:T(8,128)(2,1)S(1)}, bf16[640,512]{1,0:T(8,128)(2,1)}, u32[]{:S(2)}, u32[]{:S(2)}) collective-permute-start(bf16[640,512]{1,0:T(8,128)(2,1)S(1)} %add_convert_fusion.2), channel_id=1, source_target_pairs={{0,8},{8,0},{16,24},{24,16},{1,9},{9,1},{17,25},{25,17},{2,10},{10... | collective-permute-start | bytes 1966088 | tf_op jit(solution)/shard_map/ppermute | solution.py:849
  497.7 22.1 %collective-permute-start.37 = (bf16[640,512]{1,0:T(8,128)(2,1)S(1)}, bf16[640,512]{1,0:T(8,128)(2,1)S(1)}, u32[]{:S(2)}, u32[]{:S(2)}) collective-permute-start(bf16[640,512]{1,0:T(8,128)(2,1)S(1)} %add_convert_fusion.3), channel_id=1, source_target_pairs={{0,16},{8,24},{16,0},{24,8},{1,17},{9,25},{17,1},{25,9},{2,18},{10... | collective-permute-start | bytes 1966088 | tf_op jit(solution)/shard_map/ppermute | solution.py:849
  499.0 20.2 %all-to-all-start.9 = ((f32[32,8,128]{2,1,0:T(8,128)}), f32[32,8,128]{2,1,0:T(8,128)S(1)}, u32[]{:S(2)}, u32[]{:S(2)}) async-start(f32[32,8,128]{2,1,0:T(8,128)} %broadcast_in_dim.97), calls=%async_computation.11 | async-start | bytes 262144 | tf_op jit(solution)/shard_map/all_to_all | solution.py:831
  503.7 81.2 %reduce-scatter.11.cloned.1.call-start = ((), (), s32[]{:S(2)}) async-start(), calls=%async_computation.20 | async-start | bytes 2359296 | tf_op jit(solution)/shard_map/reduce_scatter | solution.py:1080
  527.9 16.5 %collective-permute-start.40 = (bf16[4,576,128]{2,1,0:T(8,128)(2,1)}, bf16[4,576,128]{2,1,0:T(8,128)(2,1)}, u32[]{:S(2)}, u32[]{:S(2)}) collective-permute-start(bf16[4,576,128]{2,1,0:T(8,128)(2,1)} %get-tuple-element.204), channel_id=1, source_target_pairs={{0,8},{8,0},{16,24},{24,16},{1,9},{9,1},{17,25},{25,17},{2,10},{10... | collective-permute-start | bytes 1769480 | tf_op jit(solution)/shard_map/ppermute | solution.py:870
  529.7 16.5 %collective-permute-start.41 = (bf16[4,576,128]{2,1,0:T(8,128)(2,1)}, bf16[4,576,128]{2,1,0:T(8,128)(2,1)}, u32[]{:S(2)}, u32[]{:S(2)}) collective-permute-start(bf16[4,576,128]{2,1,0:T(8,128)(2,1)} %get-tuple-element.205), channel_id=1, source_target_pairs={{0,16},{8,24},{16,0},{24,8},{1,17},{9,25},{17,1},{25,9},{2,18},{10... | collective-permute-start | bytes 1769480 | tf_op jit(solution)/shard_map/ppermute | solution.py:870
  532.2 14.3 %collective-permute-start.42 = (bf16[128,512]{1,0:T(8,128)(2,1)S(1)}, bf16[128,512]{1,0:T(8,128)(2,1)}, u32[]{:S(2)}, u32[]{:S(2)}) collective-permute-start(bf16[128,512]{1,0:T(8,128)(2,1)S(1)} %slice.325), channel_id=1, source_target_pairs={{0,8},{8,0},{16,24},{24,16},{1,9},{9,1},{17,25},{25,17},{2,10},{10... | collective-permute-start | bytes 393224 | tf_op jit(solution)/shard_map/ppermute | solution.py:849
  533.0 14.8 %collective-permute-start.43 = (bf16[128,512]{1,0:T(8,128)(2,1)S(1)}, bf16[128,512]{1,0:T(8,128)(2,1)S(1)}, u32[]{:S(2)}, u32[]{:S(2)}) collective-permute-start(bf16[128,512]{1,0:T(8,128)(2,1)S(1)} %slice.327), channel_id=1, source_target_pairs={{0,16},{8,24},{16,0},{24,8},{1,17},{9,25},{17,1},{25,9},{2,18},{10... | collective-permute-start | bytes 393224 | tf_op jit(solution)/shard_map/ppermute | solution.py:849
  552.5 21.4 %collective-permute-start.44 = (bf16[4,576,128]{2,1,0:T(8,128)(2,1)S(1)}, bf16[4,576,128]{2,1,0:T(8,128)(2,1)S(1)}, u32[]{:S(2)}, u32[]{:S(2)}) collective-permute-start(bf16[4,576,128]{2,1,0:T(8,128)(2,1)S(1)} %get-tuple-element.214), channel_id=1, source_target_pairs={{0,24},{8,16},{16,8},{24,0},{1,25},{9,17},{17,9},{25,1},{2,26},{10... | collective-permute-start | bytes 1769480 | tf_op jit(solution)/shard_map/ppermute | solution.py:870
  554.9 26.9 %collective-permute-start.52 = (bf16[128,512]{1,0:T(8,128)(2,1)S(1)}, bf16[128,512]{1,0:T(8,128)(2,1)S(1)}, u32[]{:S(2)}, u32[]{:S(2)}) collective-permute-start(bf16[128,512]{1,0:T(8,128)(2,1)S(1)} %add_convert_fusion.16), channel_id=1, source_target_pairs={{0,16},{8,24},{16,0},{24,8},{1,17},{9,25},{17,1},{25,9},{2,18},{10... | collective-permute-start | bytes 393224 | tf_op jit(solution)/shard_map/ppermute | solution.py:849
  555.4 33.0 %collective-permute-start.53 = (bf16[128,512]{1,0:T(8,128)(2,1)S(1)}, bf16[128,512]{1,0:T(8,128)(2,1)}, u32[]{:S(2)}, u32[]{:S(2)}) collective-permute-start(bf16[128,512]{1,0:T(8,128)(2,1)S(1)} %add_convert_fusion.14), channel_id=1, source_target_pairs={{0,8},{8,0},{16,24},{24,16},{1,9},{9,1},{17,25},{25,17},{2,10},{10... | collective-permute-start | bytes 393224 | tf_op jit(solution)/shard_map/ppermute | solution.py:849
  576.3 15.7 %collective-permute-start.45 = (bf16[576,128]{1,0:T(8,128)(2,1)}, bf16[576,128]{1,0:T(8,128)(2,1)}, u32[]{:S(2)}, u32[]{:S(2)}) collective-permute-start(bf16[576,128]{1,0:T(8,128)(2,1)} %get-tuple-element.253), channel_id=1, source_target_pairs={{0,2},{1,3},{2,0},{3,1},{4,6},{5,7},{6,4},{7,5},{8,10},{9,11},{10,... | collective-permute-start | bytes 442376 | tf_op jit(solution)/shard_map/ppermute | solution.py:870
  577.8 14.2 %collective-permute-start.46 = (bf16[576,128]{1,0:T(8,128)(2,1)}, bf16[576,128]{1,0:T(8,128)(2,1)}, u32[]{:S(2)}, u32[]{:S(2)}) collective-permute-start(bf16[576,128]{1,0:T(8,128)(2,1)} %get-tuple-element.252), channel_id=1, source_target_pairs={{0,4},{1,5},{2,6},{3,7},{4,0},{5,1},{6,2},{7,3},{8,12},{9,13},{10,... | collective-permute-start | bytes 442376 | tf_op jit(solution)/shard_map/ppermute | solution.py:870
  580.2 11.8 %collective-permute-start.47 = (bf16[576,128]{1,0:T(8,128)(2,1)}, bf16[576,128]{1,0:T(8,128)(2,1)}, u32[]{:S(2)}, u32[]{:S(2)}) collective-permute-start(bf16[576,128]{1,0:T(8,128)(2,1)} %get-tuple-element.251), channel_id=1, source_target_pairs={{0,6},{1,7},{2,4},{3,5},{4,2},{5,3},{6,0},{7,1},{8,14},{9,15},{10,... | collective-permute-start | bytes 442376 | tf_op jit(solution)/shard_map/ppermute | solution.py:870
  601.8 20.2 %all-to-all-start.10 = ((bf16[4,2,576,128]{3,2,1,0:T(8,128)(2,1)}), bf16[4,2,576,128]{3,2,1,0:T(8,128)(2,1)}, u32[]{:S(2)}, u32[]{:S(2)}) async-start(bf16[4,2,576,128]{3,2,1,0:T(8,128)(2,1)} %broadcast_in_dim.98), calls=%async_computation.14 | async-start | bytes 2359296 | tf_op jit(solution)/shard_map/all_to_all | solution.py:1101
  608.8 12.1 %collective-permute-start.50 = (bf16[128,512]{1,0:T(8,128)(2,1)S(1)}, bf16[128,512]{1,0:T(8,128)(2,1)S(1)}, u32[]{:S(2)}, u32[]{:S(2)}) collective-permute-start(bf16[128,512]{1,0:T(8,128)(2,1)S(1)} %get-tuple-element.263), channel_id=1, source_target_pairs={{0,16},{8,24},{16,0},{24,8},{1,17},{9,25},{17,1},{25,9},{2,18},{10... | collective-permute-start | bytes 393224 | tf_op jit(solution)/shard_map/ppermute | solution.py:849
  (64 other events, 447.4 us)
Sparse Core Ops, SparseCore 0:
  10.2 40.6 all-gather.16
  52.5 29.2 all-gather.18
  83.9 28.5 all-gather.20
  114.6 52.5 all-gather.22
  168.6 27.8 all-gather.24
  198.5 63.7 all-gather.12
  270.4 23.9 all-gather.14
  337.5 37.4 reduce-scatter.6
  422.4 33.2 reduce-scatter.4
  474.5 37.9 reduce-scatter.8
  548.0 36.9 reduce-scatter.10

commit v5 on v4

--- a/solution.py
+++ b/solution.py
@@ -96,6 +96,12 @@
 def add_stats(st, top, low, cols=slice(None)):
     st[0:1, cols] += top
     st[1:2, cols] += low
+
+
+def chunks(rows, columns, height, width=256):
+    for c in range(0, columns, width):
+        for r in range(0, rows, height):
+            yield slice(r, r + height), slice(c, c + width)
 
 
 class Shape:
@@ -399,16 +405,13 @@
         for s in range(SIDE + 1):
             scr[s * sh.rest : (s + 1) * sh.rest, :] = merged[sh.main : sh.images, :]
 
-    half = 0.5 * mask[...]
     mu, rstd, a, b = forward_consts(tot, inv[0, 0], gb)
-    step = 256
-    for c in range(0, x.shape[1], step):
-        cols = slice(c, c + step)
-        h = h3[:, cols].astype(F32)
-        v = h * a[:, cols] + b[:, cols] + x[:, cols].astype(F32)
-        up = jnp.concatenate([merged[0 : sh.main, cols]] * SIDE + [scr[:, cols]], axis=0)
-        e = half * up * slope_twice(0.5 * v)
-        e3[:, cols] = e.astype(BF)
+    for rows, cols in chunks(sh.rows, x.shape[1], sh.main):
+        h = h3[rows, cols].astype(F32)
+        v = h * a[:, cols] + b[:, cols] + x[rows, cols].astype(F32)
+        up = scr[:, cols] if rows.start >= sh.top else merged[0 : sh.main, cols]
+        e = (0.5 * mask[rows, :]) * up * slope_twice(0.5 * v)
+        e3[rows, cols] = e.astype(BF)
         add_stats(st, rowsum(e), rowsum(e * h), cols)
 
 

time: 643 us -> 642 us (level)
  no operation moved by 1% of the time
where the time goes in v5:
time: 642 us; the launch traced here: 631 us
  Pallas kernels  288 us (45%)
  starting transfers between devices  114 us (18%)
  waiting for transfers between devices  104 us (16%)
  local copies, waits for them, and re-layouts  48 us (7%)
  other arithmetic  36 us (6%)
  blocking collectives  24.1 us (4%)
  between operations  16 us (2%)
    all_to_all x7, starting transfers between devices, total_of(): got = lax.all_to_all(spread, AXES, 0, 0, tiled=True)  38.1 us
    pallas_call x2, Pallas kernels, spatial_back(): pl.pallas_call(functools.partial(spatial_back_kernel, sh), grid=(SIDE + 1...  34.9 us
    pallas_call x2, Pallas kernels, spatial_conv(): pl.pallas_call(functools.partial(spatial_kernel, sh), grid=(SIDE + 1,), i...  32.7 us
    pallas_call x2, Pallas kernels, spatial_wgrad(): pl.pallas_call(functools.partial(spatial_wgrad_kernel, sh, owned), grid=(...  30.5 us
    pallas_call x2, Pallas kernels, expand_back(): pl.pallas_call(expand_back_kernel, grid=(sh.total // sh.half,), in_specs=...  26.2 us
    ppermute x6, waiting for transfers between devices, flips(): lax.ppermute(v, axis, [(i, i ^ unit * k) for i in range(size)])  26 us
    ppermute x18, starting transfers between devices, others(): return sum([lax.ppermute(v, axis, way) for way in ways], v)  25.5 us
    pallas_call x3, Pallas kernels, wgrad(): pl.pallas_call(wgrad_kernel, grid=(max(a, b) // step,), in_specs=specs, o...  24.5 us
  transfers between devices with their start and end apart: 74, of which 33 were waited for; matrix products, arithmetic and copies ran while one was open for 11% of the time, Pallas kernels for 44%

profile of v5, /device:TPU:0, one launch (start us, length us, event | category | flops | bytes accessed | tf_op | source)
XLA Modules:
  0.0 631.4 jit_solution(12826938789528599510)
XLA Ops:
  13.7 3.1 collective-permute-start
  16.8 2.6 collective-permute-start.1
  21.1 9.5 %prep.1.x = bf16[1792,2048]{1,0:T(8,128)(2,1)} custom-call(bf16[49,36,2048]{2,1,0:T(8,128)(2,1)} %bitcast.178, f32[1792,1]{1,0:T(8,128)} %bitcast.156), custom_call_target="tpu_custom_call" | custom-call | tf_op jit(solution)/shard_map/prep/pallas_call | solution.py:134
  30.7 5.0 collective-permute-done.1
  39.3 12.8 %collective-permute-done.3 = bf16[4,576,128]{2,1,0:T(8,128)(2,1)S(1)} collective-permute-done((bf16[4,576,128]{2,1,0:T(8,128)(2,1)S(1)}, bf16[4,576,128]{2,1,0:T(8,128)(2,1)S(1)}, u32[]{:S(2)}, u32[]{:S(2)}) %collective-permute-start.3) | collective-permute-done | bytes 589856 | tf_op jit(solution)/shard_map/ppermute | solution.py:812
  52.1 8.2 %collective-permute-done.4 = bf16[4,576,128]{2,1,0:T(8,128)(2,1)S(1)} collective-permute-done((bf16[4,576,128]{2,1,0:T(8,128)(2,1)S(1)}, bf16[4,576,128]{2,1,0:T(8,128)(2,1)S(1)}, u32[]{:S(2)}, u32[]{:S(2)}) %collective-permute-start.4) | collective-permute-done | bytes 589856 | tf_op jit(solution)/shard_map/ppermute | solution.py:812
  61.5 8.5 %reduce_conv.1 = (f32[1792,512]{1,0:T(8,128)}, f32[2,512]{1,0:T(2,128)}) custom-call(bf16[1792,2048]{1,0:T(8,128)(2,1)} %prep.1.x, bf16[2048,512]{1,0:T(8,128)(2,1)} %bitcast.183), custom_call_target="tpu_custom_call" | custom-call | flops 3758096384 | bytes 11010048 | tf_op jit(solution)/shard_map/reduce_conv/pallas_call | solution.py:158
  73.5 10.7 %all-to-all-start = ((f32[32,8,256]{2,1,0:T(8,128)}), f32[32,8,256]{2,1,0:T(8,128)S(1)}, u32[]{:S(2)}, u32[]{:S(2)}) async-start(f32[32,8,256]{2,1,0:T(8,128)} %broadcast_in_dim.80), calls=%async_computation | async-start | bytes 524288 | tf_op jit(solution)/shard_map/all_to_all | solution.py:834
  84.8 5.5 assemble.1.w
  90.3 4.2 all-to-all-done
  96.4 16.4 %spatial_conv.2 = (bf16[1792,512]{1,0:T(8,128)(2,1)}, f32[1792,512]{1,0:T(8,128)}, f32[2,512]{1,0:T(2,128)}) custom-call(f32[1,1]{1,0:T(1,128)} %bitcast.18.inv, f32[1792,512]{1,0:T(8,128)} %get-tuple-element.137.h1, f32[2,512]{1,0:T(2,128)} %slice.291.tot.tot1, f32[2,512]{1,0:T(2,128)} %get-tuple-element.278.gb.gb1, f32[1792,1]{1,0:T(8,128)} %bitcast.157, ...), custom_call_target="tpu_custom_call" | custom-call | flops 8455716864 | bytes 13893632 | tf_op jit(solution)/shard_map/spatial_conv/pallas_call | solution.py:211
  113.5 10.5 %all_to_all.55 = f32[32,8,128]{2,1,0:T(8,128)S(1)} all-to-all(f32[32,8,128]{2,1,0:T(8,128)S(1)} %broadcast_in_dim.82), channel_id=1, replica_groups=mesh['dp'=4,'fsdp'=8] {'dp','fsdp'}, dimensions={0} | all-to-all | bytes 262144 | tf_op jit(solution)/shard_map/all_to_all | solution.py:834
  124.7 9.1 %expand_conv.2 = (bf16[1792,512]{1,0:T(8,128)(2,1)}, bf16[1792,2048]{1,0:T(8,128)(2,1)}, f32[2,2048]{1,0:T(2,128)}) custom-call(f32[1,1]{1,0:T(1,128)} %bitcast.18.inv, f32[1792,512]{1,0:T(8,128)} %get-tuple-element.139.h2, f32[2,512]{1,0:T(2,128)} %reshape.567.tot.tot2, f32[2,512]{1,0:T(2,128)} %get-tuple-element.279.gb.gb2, f32[1792,1]{1,0:T(8,128)} %bitcast.159, ...), custom_call_target="tpu_custom_call" | custom-call | flops 3758096384 | bytes 12845056 | tf_op jit(solution)/shard_map/expand_conv/pallas_call | solution.py:254
  140.3 2.8 collective-permute-done.8
  149.9 13.5 %join.1 = (bf16[1792,2048]{1,0:T(8,128)(2,1)}, f32[1792,512]{1,0:T(8,128)}, f32[2,512]{1,0:T(2,128)}) custom-call(f32[1,1]{1,0:T(1,128)} %bitcast.18.inv, bf16[1792,2048]{1,0:T(8,128)(2,1)} %get-tuple-element.141.h3, bf16[1792,2048]{1,0:T(8,128)(2,1)} %prep.1.x, f32[2,2048]{1,0:T(2,128)} %reshape.569.tot.tot3, f32[2,2048]{1,0:T(2,128)} %get-tuple-element.270.gb.gb3, ...), custom_call_target="tpu_custom_call" | custom-call | flops 3758096384 | bytes 25690112 | tf_op jit(solution)/shard_map/join/pallas_call | solution.py:291
  164.1 13.6 %all_to_all.56 = f32[32,8,128]{2,1,0:T(8,128)S(1)} all-to-all(f32[32,8,128]{2,1,0:T(8,128)S(1)} %broadcast_in_dim.84), channel_id=1, replica_groups=mesh['dp'=4,'fsdp'=8] {'dp','fsdp'}, dimensions={0} | all-to-all | bytes 262144 | tf_op jit(solution)/shard_map/all_to_all | solution.py:834
  178.4 16.3 %spatial_conv.3 = (bf16[1792,512]{1,0:T(8,128)(2,1)}, f32[1792,512]{1,0:T(8,128)}, f32[2,512]{1,0:T(2,128)}) custom-call(f32[1,1]{1,0:T(1,128)} %bitcast.18.inv, f32[1792,512]{1,0:T(8,128)} %get-tuple-element.143.h1, f32[2,512]{1,0:T(2,128)} %reshape.570.tot.tot1, f32[2,512]{1,0:T(2,128)} %get-tuple-element.280.gb.gb1, f32[1792,1]{1,0:T(8,128)} %bitcast.161, ...), custom_call_target="tpu_custom_call" | custom-call | flops 8455716864 | bytes 13893632 | tf_op jit(solution)/shard_map/spatial_conv/pallas_call | solution.py:211
  199.5 7.3 %all-to-all-done.3 = f32[32,8,128]{2,1,0:T(8,128)S(1)} async-done(((f32[32,8,128]{2,1,0:T(8,128)}), f32[32,8,128]{2,1,0:T(8,128)S(1)}, u32[]{:S(2)}, u32[]{:S(2)}) %all-to-all-start.3) | async-done | bytes 131104 | tf_op jit(solution)/shard_map/all_to_all | solution.py:834
  207.4 9.4 %expand_conv.3 = (bf16[1792,512]{1,0:T(8,128)(2,1)}, bf16[1792,2048]{1,0:T(8,128)(2,1)}, f32[2,2048]{1,0:T(2,128)}) custom-call(f32[1,1]{1,0:T(1,128)} %bitcast.18.inv, f32[1792,512]{1,0:T(8,128)} %get-tuple-element.145.h2, f32[2,512]{1,0:T(2,128)} %reshape.571.tot.tot2, f32[2,512]{1,0:T(2,128)} %get-tuple-element.277.gb.gb2, f32[1792,1]{1,0:T(8,128)} %bitcast.163, ...), custom_call_target="tpu_custom_call" | custom-call | flops 3758096384 | bytes 12845056 | tf_op jit(solution)/shard_map/expand_conv/pallas_call | solution.py:254
  234.5 13.5 %last_join.1 = (bf16[49,36,2048]{2,1,0:T(8,128)(2,1)}, bf16[48,2048]{1,0:T(8,128)(2,1)}) custom-call(f32[1,1]{1,0:T(1,128)} %bitcast.18.inv, bf16[1792,2048]{1,0:T(8,128)(2,1)} %get-tuple-element.147.h3, bf16[1792,2048]{1,0:T(8,128)(2,1)} %get-tuple-element.148.x.left, f32[2,2048]{1,0:T(2,128)} %reshape.573.tot.tot3, f32[2,2048]{1,0:T(2,128)} %get-tuple-element.269.gb.gb3, ...), custom_call_target="tpu_custom_call" | custom-call | flops 352321536 | bytes 22020096 | tf_op jit(solution)/shard_map/last_join/pallas_call | solution.py:334
  248.0 14.3 %all-gather.13.cloned.1.call-done.w = bf16[1424,2048]{1,0:T(8,128)(2,1)} async-done(((bf16[1424,256]{1,0:T(8,128)(2,1)}), bf16[1424,2048]{1,0:T(8,128)(2,1)}) %all-gather.13.cloned.1.call-update) | async-done | bytes 5832720 | tf_op jit(solution)/shard_map/all_gather | solution.py:933
  262.3 7.9 %heads.1 = (f32[48,2048]{1,0:T(8,128)}, bf16[48,1536]{1,0:T(8,128)(2,1)}) custom-call(bf16[48,2048]{1,0:T(8,128)(2,1)} %get-tuple-element.151.pooled, s32[48,3]{1,0:T(8,128)} %pad.26.labels, f32[48,1]{1,0:T(8,128)} %copy.122.area, s32[48,2048]{1,0:T(8,128)} %pad.27.bits, bf16[1424,2048]{1,0:T(8,128)(2,1)} %all-gather.13.cloned.1.call-done.w), custom_call_target="tpu_custom_call" | custom-call | flops 603979776 | bytes 5832704 | tf_op jit(solution)/shard_map/heads/pallas_call | solution.py:390
  271.0 3.4 all-to-all-start.4
  274.4 15.3 %top_grad.1 = (bf16[1792,2048]{1,0:T(8,128)(2,1)}, f32[2,2048]{1,0:T(2,128)}) custom-call(f32[1,1]{1,0:T(1,128)} %bitcast.18.inv, f32[48,2048]{1,0:T(8,128)} %get-tuple-element.152.merged, bf16[1792,2048]{1,0:T(8,128)(2,1)} %get-tuple-element.147.h3, bf16[1792,2048]{1,0:T(8,128)(2,1)} %get-tuple-element.148.x.left, f32[2,2048]{1,0:T(2,128)} %reshape.573.tot.tot3, ...), custom_call_target="tpu_custom_call" | custom-call | flops 73400320 | bytes 22020096 | tf_op jit(solution)/shard_map/top_grad/pallas_call | solution.py:420
  307.5 13.2 %expand_back.2 = (bf16[1792,2048]{1,0:T(8,128)(2,1)}, f32[1792,512]{1,0:T(8,128)}, f32[2,512]{1,0:T(2,128)}) custom-call(f32[1,1]{1,0:T(1,128)} %bitcast.18.inv, bf16[1792,2048]{1,0:T(8,128)(2,1)} %get-tuple-element.153.e3, bf16[1792,2048]{1,0:T(8,128)(2,1)} %get-tuple-element.147.h3, f32[2,2048]{1,0:T(2,128)} %reshape.573.tot.tot3, ...), custom_call_target="tpu_custom_call" | custom-call | flops 3758096384 | bytes 29360128 | tf_op jit(solution)/shard_map/expand_back/pallas_call | solution.py:463
  322.0 5.5 all-to-all-start.5
  327.5 8.2 %wgrad.3 = bf16[512,2048]{1,0:T(8,128)(2,1)} custom-call(bf16[1792,512]{1,0:T(8,128)(2,1)} %get-tuple-element.158.left, bf16[1792,2048]{1,0:T(8,128)(2,1)} %get-tuple-element.159.right), custom_call_target="tpu_custom_call" | custom-call | flops 3758096384 | bytes 11272192 | tf_op jit(solution)/shard_map/wgrad/pallas_call | solution.py:656
  336.4 17.5 %spatial_back.2 = (bf16[1792,512]{1,0:T(8,128)(2,1)}, f32[1792,512]{1,0:T(8,128)}, f32[2,512]{1,0:T(2,128)}) custom-call(f32[1,1]{1,0:T(1,128)} %bitcast.18.inv, f32[1792,512]{1,0:T(8,128)} %get-tuple-element.156.e2, f32[1792,512]{1,0:T(8,128)} %get-tuple-element.145.h2, f32[2,512]{1,0:T(2,128)} %reshape.571.tot.tot2, f32[2,512]{1,0:T(2,128)} %get-tuple-element.277.gb.gb2, ...), custom_call_target="tpu_custom_call" | custom-call | flops 8455716864 | bytes 21233664 | tf_op jit(solution)/shard_map/spatial_back/pallas_call | solution.py:522
  355.2 6.3 all-to-all-start.6
  361.5 15.1 %spatial_wgrad.2 = (bf16[4,4,576,128]{3,2,1,0:T(8,128)(2,1)}, bf16[4,4,576,128]{3,2,1,0:T(8,128)(2,1)}) custom-call(s32[1,2]{1,0:T(1,128)} %copy-done.30, bf16[1792,512]{1,0:T(8,128)(2,1)} %get-tuple-element.163.act, bf16[1792,512]{1,0:T(8,128)(2,1)} %get-tuple-element.164.g), custom_call_target="tpu_custom_call" | custom-call | flops 8455716864 | bytes 8388608 | tf_op jit(solution)/shard_map/spatial_wgrad/pallas_call | solution.py:756
  377.7 19.2 %reduce_back.1 = (bf16[1792,512]{1,0:T(8,128)(2,1)}, bf16[1792,2048]{1,0:T(8,128)(2,1)}, f32[2,2048]{1,0:T(2,128)}) custom-call(f32[1,1]{1,0:T(1,128)} %bitcast.18.inv, f32[1792,512]{1,0:T(8,128)} %get-tuple-element.161.e1, f32[1792,512]{1,0:T(8,128)} %get-tuple-element.143.h1, f32[2,512]{1,0:T(2,128)} %reshape.570.tot.tot1, ...), custom_call_target="tpu_custom_call" | custom-call | flops 3758096384 | bytes 38535168 | tf_op jit(solution)/shard_map/reduce_back/pallas_call | solution.py:577
  398.5 5.7 all-to-all-start.7
  404.3 8.2 %wgrad.4 = bf16[2048,512]{1,0:T(8,128)(2,1)} custom-call(bf16[1792,2048]{1,0:T(8,128)(2,1)} %get-tuple-element.148.x.left, bf16[1792,512]{1,0:T(8,128)(2,1)} %get-tuple-element.172.right), custom_call_target="tpu_custom_call" | custom-call | flops 3758096384 | bytes 11272192 | tf_op jit(solution)/shard_map/wgrad/pallas_call | solution.py:656
  412.5 8.1 %all-to-all-done.7 = f32[32,8,512]{2,1,0:T(8,128)S(1)} async-done(((f32[32,8,512]{2,1,0:T(8,128)}), f32[32,8,512]{2,1,0:T(8,128)S(1)}, u32[]{:S(2)}, u32[]{:S(2)}) %all-to-all-start.7) | async-done | bytes 524320 | tf_op jit(solution)/shard_map/all_to_all | solution.py:834
  421.3 2.9 fusion.11
  430.2 13.1 %expand_back.3 = (bf16[1792,2048]{1,0:T(8,128)(2,1)}, f32[1792,512]{1,0:T(8,128)}, f32[2,512]{1,0:T(2,128)}) custom-call(f32[1,1]{1,0:T(1,128)} %bitcast.18.inv, bf16[1792,2048]{1,0:T(8,128)(2,1)} %get-tuple-element.209.e3, bf16[1792,2048]{1,0:T(8,128)(2,1)} %get-tuple-element.141.h3, f32[2,2048]{1,0:T(2,128)} %reshape.569.tot.tot3, ...), custom_call_target="tpu_custom_call" | custom-call | flops 3758096384 | bytes 29360128 | tf_op jit(solution)/shard_map/expand_back/pallas_call | solution.py:463
  443.3 9.4 %collective-permute-done.30 = bf16[4,576,128]{2,1,0:T(8,128)(2,1)} collective-permute-done((bf16[4,576,128]{2,1,0:T(8,128)(2,1)}, bf16[4,576,128]{2,1,0:T(8,128)(2,1)}, u32[]{:S(2)}, u32[]{:S(2)}) %collective-permute-start.30) | collective-permute-done | bytes 589856 | tf_op jit(solution)/shard_map/ppermute | solution.py:873
  464.6 8.1 %wgrad.5 = bf16[512,2048]{1,0:T(8,128)(2,1)} custom-call(bf16[1792,512]{1,0:T(8,128)(2,1)} %get-tuple-element.179.left, bf16[1792,2048]{1,0:T(8,128)(2,1)} %get-tuple-element.180.right), custom_call_target="tpu_custom_call" | custom-call | flops 3758096384 | bytes 11272192 | tf_op jit(solution)/shard_map/wgrad/pallas_call | solution.py:656
  477.3 17.4 %spatial_back.3 = (bf16[1792,512]{1,0:T(8,128)(2,1)}, f32[1792,512]{1,0:T(8,128)}, f32[2,512]{1,0:T(2,128)}) custom-call(f32[1,1]{1,0:T(1,128)} %bitcast.18.inv, f32[1792,512]{1,0:T(8,128)} %get-tuple-element.174.e2, f32[1792,512]{1,0:T(8,128)} %get-tuple-element.139.h2, f32[2,512]{1,0:T(2,128)} %reshape.567.tot.tot2, f32[2,512]{1,0:T(2,128)} %get-tuple-element.279.gb.gb2, ...), custom_call_target="tpu_custom_call" | custom-call | flops 8455716864 | bytes 21233664 | tf_op jit(solution)/shard_map/spatial_back/pallas_call | solution.py:522
  498.0 4.7 all-to-all-start.9
  502.8 15.4 %spatial_wgrad.3 = (bf16[4,4,576,128]{3,2,1,0:T(8,128)(2,1)}, bf16[4,4,576,128]{3,2,1,0:T(8,128)(2,1)}) custom-call(s32[1,2]{1,0:T(1,128)} %copy-done.30, bf16[1792,512]{1,0:T(8,128)(2,1)} %get-tuple-element.196.act, bf16[1792,512]{1,0:T(8,128)(2,1)} %get-tuple-element.197.g), custom_call_target="tpu_custom_call" | custom-call | flops 8455716864 | bytes 8388608 | tf_op jit(solution)/shard_map/spatial_wgrad/pallas_call | solution.py:756
  523.7 3.3 fusion.16
  532.3 10.7 %reduce_wgrad.1 = bf16[2048,512]{1,0:T(8,128)(2,1)} custom-call(f32[1,1]{1,0:T(1,128)} %bitcast.18.inv, f32[1792,512]{1,0:T(8,128)} %get-tuple-element.202.e1, f32[1792,512]{1,0:T(8,128)} %get-tuple-element.137.h1, f32[2,512]{1,0:T(2,128)} %slice.291.tot.tot1, f32[2,512]{1,0:T(2,128)} %get-tuple-element.278.gb.gb1, f32[2,512]{1,0:T(2,128)} %reshape.584.btot1, ...), custom_call_target="tpu_custom_call" | custom-call | flops 3758096384 | bytes 14680064 | tf_op jit(solution)/shard_map/reduce_wgrad/pallas_call | solution.py:684
  556.1 16.8 %features_back.1 = f32[49,36,2048]{2,1,0:T(8,128)} custom-call(f32[1,1]{1,0:T(1,128)} %bitcast.18.inv, f32[1792,512]{1,0:T(8,128)} %get-tuple-element.202.e1, f32[1792,512]{1,0:T(8,128)} %get-tuple-element.137.h1, f32[2,512]{1,0:T(2,128)} %slice.291.tot.tot1, f32[2,512]{1,0:T(2,128)} %get-tuple-element.278.gb.gb1, f32[2,512]{1,0:T(2,128)} %reshape.584.btot1, ...), custom_call_target="tpu_custom_call" | custom-call | flops 3758096384 | bytes 31195136 | tf_op jit(solution)/shard_map/features_back/pallas_call | solution.py:619
  580.9 3.0 reduce-scatter.11.cloned.1.call-done
  600.8 4.4 all-to-all-start.10
  615.9 4.3 collective-permute-done.50
  621.4 3.0 copy_bitcast_fusion
  (364 shorter events, 168.5 us)
Async XLA Ops:
  7.2 53.4 %all-gather.17.cloned.1.call-start = ((), (), s32[]{:S(2)}) async-start(), calls=%async_computation.21 | async-start | bytes 2359296 | tf_op jit(solution)/shard_map/all_gather | solution.py:916
  9.2 115.4 %all-gather.19.cloned.1.call-start = ((), (), s32[]{:S(2)}) async-start(), calls=%async_computation.22 | async-start | bytes 2359296 | tf_op jit(solution)/shard_map/all_gather | solution.py:918
  10.1 139.8 %all-gather.21.cloned.1.call-start = ((), (), s32[]{:S(2)}) async-start(), calls=%async_computation.23 | async-start | bytes 2359296 | tf_op jit(solution)/shard_map/all_gather | solution.py:916
  10.9 167.4 %all-gather.23.cloned.1.call-start = ((), (), s32[]{:S(2)}) async-start(), calls=%async_computation.24 | async-start | bytes 5308416 | tf_op jit(solution)/shard_map/all_gather | solution.py:917
  11.9 195.5 %all-gather.25.cloned.1.call-start = ((), (), s32[]{:S(2)}) async-start(), calls=%async_computation.25 | async-start | bytes 2359296 | tf_op jit(solution)/shard_map/all_gather | solution.py:918
  12.5 249.8 %all-gather.13.cloned.1.call-start = ((), (), s32[]{:S(2)}) async-start(), calls=%async_computation.15 | async-start | bytes 6561792 | tf_op jit(solution)/shard_map/all_gather | solution.py:933
  13.7 17.0 %collective-permute-start = (bf16[576,128]{1,0:T(8,128)(2,1)S(1)}, bf16[576,128]{1,0:T(8,128)(2,1)S(1)}, u32[]{:S(2)}, u32[]{:S(2)}) collective-permute-start(bf16[576,128]{1,0:T(8,128)(2,1)S(1)} %dynamic-slice_bitcast_fusion), channel_id=1, source_target_pairs={{0,2},{1,3},{2,0},{3,1},{4,6},{5,7},{6,4},{7,5},{8,10},{9,11},{10,... | collective-permute-start | bytes 442376 | tf_op jit(solution)/shard_map/ppermute | solution.py:812
  16.8 18.9 %collective-permute-start.1 = (bf16[576,128]{1,0:T(8,128)(2,1)S(1)}, bf16[576,128]{1,0:T(8,128)(2,1)S(1)}, u32[]{:S(2)}, u32[]{:S(2)}) collective-permute-start(bf16[576,128]{1,0:T(8,128)(2,1)S(1)} %dynamic-slice_bitcast_fusion), channel_id=1, source_target_pairs={{0,4},{1,5},{2,6},{3,7},{4,0},{5,1},{6,2},{7,3},{8,12},{9,13},{10,... | collective-permute-start | bytes 442376 | tf_op jit(solution)/shard_map/ppermute | solution.py:812
  19.4 16.3 %collective-permute-start.2 = (bf16[576,128]{1,0:T(8,128)(2,1)S(1)}, bf16[576,128]{1,0:T(8,128)(2,1)S(1)}, u32[]{:S(2)}, u32[]{:S(2)}) collective-permute-start(bf16[576,128]{1,0:T(8,128)(2,1)S(1)} %dynamic-slice_bitcast_fusion), channel_id=1, source_target_pairs={{0,6},{1,7},{2,4},{3,5},{4,2},{5,3},{6,0},{7,1},{8,14},{9,15},{10,... | collective-permute-start | bytes 442376 | tf_op jit(solution)/shard_map/ppermute | solution.py:812
  35.8 16.3 %collective-permute-start.3 = (bf16[4,576,128]{2,1,0:T(8,128)(2,1)S(1)}, bf16[4,576,128]{2,1,0:T(8,128)(2,1)S(1)}, u32[]{:S(2)}, u32[]{:S(2)}) collective-permute-start(bf16[4,576,128]{2,1,0:T(8,128)(2,1)S(1)} %get-tuple-element.258), channel_id=1, source_target_pairs={{0,8},{8,0},{16,24},{24,16},{1,9},{9,1},{17,25},{25,17},{2,10},{10... | collective-permute-start | bytes 1769480 | tf_op jit(solution)/shard_map/ppermute | solution.py:812
  37.3 23.0 %collective-permute-start.4 = (bf16[4,576,128]{2,1,0:T(8,128)(2,1)S(1)}, bf16[4,576,128]{2,1,0:T(8,128)(2,1)S(1)}, u32[]{:S(2)}, u32[]{:S(2)}) collective-permute-start(bf16[4,576,128]{2,1,0:T(8,128)(2,1)S(1)} %get-tuple-element.258), channel_id=1, source_target_pairs={{0,16},{8,24},{16,0},{24,8},{1,17},{9,25},{17,1},{25,9},{2,18},{10... | collective-permute-start | bytes 1769480 | tf_op jit(solution)/shard_map/ppermute | solution.py:812
  38.9 21.4 %collective-permute-start.5 = (bf16[4,576,128]{2,1,0:T(8,128)(2,1)S(1)}, bf16[4,576,128]{2,1,0:T(8,128)(2,1)S(1)}, u32[]{:S(2)}, u32[]{:S(2)}) collective-permute-start(bf16[4,576,128]{2,1,0:T(8,128)(2,1)S(1)} %get-tuple-element.258), channel_id=1, source_target_pairs={{0,24},{8,16},{16,8},{24,0},{1,25},{9,17},{17,9},{25,1},{2,26},{10... | collective-permute-start | bytes 1769480 | tf_op jit(solution)/shard_map/ppermute | solution.py:812
  73.5 21.1 %all-to-all-start = ((f32[32,8,256]{2,1,0:T(8,128)}), f32[32,8,256]{2,1,0:T(8,128)S(1)}, u32[]{:S(2)}, u32[]{:S(2)}) async-start(f32[32,8,256]{2,1,0:T(8,128)} %broadcast_in_dim.80), calls=%async_computation | async-start | bytes 524288 | tf_op jit(solution)/shard_map/all_to_all | solution.py:834
  196.0 10.8 %all-to-all-start.3 = ((f32[32,8,128]{2,1,0:T(8,128)}), f32[32,8,128]{2,1,0:T(8,128)S(1)}, u32[]{:S(2)}, u32[]{:S(2)}) async-start(f32[32,8,128]{2,1,0:T(8,128)} %broadcast_in_dim.86), calls=%async_computation.3 | async-start | bytes 262144 | tf_op jit(solution)/shard_map/all_to_all | solution.py:834
  198.6 229.1 %all-gather.15.cloned.1.call-start = ((), (), s32[]{:S(2)}) async-start(), calls=%async_computation.16 | async-start | bytes 1327104 | tf_op jit(solution)/shard_map/all_gather | solution.py:1006
  271.0 18.7 %all-to-all-start.4 = ((bf16[8,48,256]{2,1,0:T(8,128)(2,1)}), bf16[8,48,256]{2,1,0:T(8,128)(2,1)S(1)}, u32[]{:S(2)}, u32[]{:S(2)}) async-start(bf16[8,48,256]{2,1,0:T(8,128)(2,1)} %bitcast.153), calls=%async_computation.4 | async-start | bytes 393216 | tf_op jit(solution)/shard_map/all_to_all | solution.py:999
  322.0 13.7 %all-to-all-start.5 = ((f32[32,8,128]{2,1,0:T(8,128)}), f32[32,8,128]{2,1,0:T(8,128)S(1)}, u32[]{:S(2)}, u32[]{:S(2)}) async-start(f32[32,8,128]{2,1,0:T(8,128)} %broadcast_in_dim.89), calls=%async_computation.5 | async-start | bytes 262144 | tf_op jit(solution)/shard_map/all_to_all | solution.py:834
  327.5 146.0 %reduce-scatter.7.cloned.1.call-start = ((), (), s32[]{:S(2)}) async-start(), calls=%async_computation.18 | async-start | bytes 2359296 | tf_op jit(solution)/shard_map/reduce_scatter | solution.py:1031
  355.2 21.4 %all-to-all-start.6 = ((f32[32,8,128]{2,1,0:T(8,128)}), f32[32,8,128]{2,1,0:T(8,128)S(1)}, u32[]{:S(2)}, u32[]{:S(2)}) async-start(f32[32,8,128]{2,1,0:T(8,128)} %broadcast_in_dim.91), calls=%async_computation.6 | async-start | bytes 262144 | tf_op jit(solution)/shard_map/all_to_all | solution.py:834
  377.3 19.6 %collective-permute-start.28 = (bf16[4,4,576,128]{3,2,1,0:T(8,128)(2,1)}, bf16[4,4,576,128]{3,2,1,0:T(8,128)(2,1)}, u32[]{:S(2)}, u32[]{:S(2)}) collective-permute-start(bf16[4,4,576,128]{3,2,1,0:T(8,128)(2,1)} %get-tuple-element.170), channel_id=1, source_target_pairs={{0,1},{1,0},{2,3},{3,2},{4,5},{5,4},{6,7},{7,6},{8,9},{9,8},{10,11... | collective-permute-start | bytes 7077896 | tf_op jit(solution)/shard_map/ppermute | solution.py:868
  398.5 22.1 %all-to-all-start.7 = ((f32[32,8,512]{2,1,0:T(8,128)}), f32[32,8,512]{2,1,0:T(8,128)S(1)}, u32[]{:S(2)}, u32[]{:S(2)}) async-start(f32[32,8,512]{2,1,0:T(8,128)} %broadcast_in_dim.93), calls=%async_computation.7 | async-start | bytes 1048576 | tf_op jit(solution)/shard_map/all_to_all | solution.py:834
  404.2 70.4 %reduce-scatter.5.cloned.1.call-start = ((), (), s32[]{:S(2)}) async-start(), calls=%async_computation.17 | async-start | bytes 2359296 | tf_op jit(solution)/shard_map/reduce_scatter | solution.py:1068
  424.2 19.1 %collective-permute-start.29 = (bf16[4,576,128]{2,1,0:T(8,128)(2,1)}, bf16[4,576,128]{2,1,0:T(8,128)(2,1)}, u32[]{:S(2)}, u32[]{:S(2)}) collective-permute-start(bf16[4,576,128]{2,1,0:T(8,128)(2,1)} %get-tuple-element.246), channel_id=1, source_target_pairs={{0,8},{8,0},{16,24},{24,16},{1,9},{9,1},{17,25},{25,17},{2,10},{10... | collective-permute-start | bytes 1769480 | tf_op jit(solution)/shard_map/ppermute | solution.py:873
  424.2 28.4 %collective-permute-start.30 = (bf16[4,576,128]{2,1,0:T(8,128)(2,1)}, bf16[4,576,128]{2,1,0:T(8,128)(2,1)}, u32[]{:S(2)}, u32[]{:S(2)}) collective-permute-start(bf16[4,576,128]{2,1,0:T(8,128)(2,1)} %get-tuple-element.245), channel_id=1, source_target_pairs={{0,16},{8,24},{16,0},{24,8},{1,17},{9,25},{17,1},{25,9},{2,18},{10... | collective-permute-start | bytes 1769480 | tf_op jit(solution)/shard_map/ppermute | solution.py:873
  425.3 28.0 %collective-permute-start.31 = (bf16[4,576,128]{2,1,0:T(8,128)(2,1)}, bf16[4,576,128]{2,1,0:T(8,128)(2,1)}, u32[]{:S(2)}, u32[]{:S(2)}) collective-permute-start(bf16[4,576,128]{2,1,0:T(8,128)(2,1)} %get-tuple-element.244), channel_id=1, source_target_pairs={{0,24},{8,16},{16,8},{24,0},{1,25},{9,17},{17,9},{25,1},{2,26},{10... | collective-permute-start | bytes 1769480 | tf_op jit(solution)/shard_map/ppermute | solution.py:873
  430.1 64.6 %collective-permute-start.35 = (bf16[640,512]{1,0:T(8,128)(2,1)S(1)}, bf16[640,512]{1,0:T(8,128)(2,1)S(1)}, u32[]{:S(2)}, u32[]{:S(2)}) collective-permute-start(bf16[640,512]{1,0:T(8,128)(2,1)S(1)} %slice.314), channel_id=1, source_target_pairs={{0,8},{8,0},{16,24},{24,16},{1,9},{9,1},{17,25},{25,17},{2,10},{10... | collective-permute-start | bytes 1966088 | tf_op jit(solution)/shard_map/ppermute | solution.py:852
  454.7 18.1 %all-to-all-start.8 = ((f32[32,8,128]{2,1,0:T(8,128)}), f32[32,8,128]{2,1,0:T(8,128)S(1)}, u32[]{:S(2)}, u32[]{:S(2)}) async-start(f32[32,8,128]{2,1,0:T(8,128)} %broadcast_in_dim.95), calls=%async_computation.8 | async-start | bytes 262144 | tf_op jit(solution)/shard_map/all_to_all | solution.py:834
  457.3 72.9 %reduce-scatter.9.cloned.1.call-start = ((), (), s32[]{:S(2)}) async-start(), calls=%async_computation.19 | async-start | bytes 2359296 | tf_op jit(solution)/shard_map/reduce_scatter | solution.py:1031
  460.3 34.5 %collective-permute-start.32 = (bf16[576,128]{1,0:T(8,128)(2,1)}, bf16[576,128]{1,0:T(8,128)(2,1)}, u32[]{:S(2)}, u32[]{:S(2)}) collective-permute-start(bf16[576,128]{1,0:T(8,128)(2,1)} %get-tuple-element.256), channel_id=1, source_target_pairs={{0,2},{1,3},{2,0},{3,1},{4,6},{5,7},{6,4},{7,5},{8,10},{9,11},{10,... | collective-permute-start | bytes 442376 | tf_op jit(solution)/shard_map/ppermute | solution.py:873
  461.9 32.8 %collective-permute-start.33 = (bf16[576,128]{1,0:T(8,128)(2,1)}, bf16[576,128]{1,0:T(8,128)(2,1)}, u32[]{:S(2)}, u32[]{:S(2)}) collective-permute-start(bf16[576,128]{1,0:T(8,128)(2,1)} %get-tuple-element.255), channel_id=1, source_target_pairs={{0,4},{1,5},{2,6},{3,7},{4,0},{5,1},{6,2},{7,3},{8,12},{9,13},{10,... | collective-permute-start | bytes 442376 | tf_op jit(solution)/shard_map/ppermute | solution.py:873
  464.4 30.3 %collective-permute-start.34 = (bf16[576,128]{1,0:T(8,128)(2,1)S(1)}, bf16[576,128]{1,0:T(8,128)(2,1)}, u32[]{:S(2)}, u32[]{:S(2)}) collective-permute-start(bf16[576,128]{1,0:T(8,128)(2,1)S(1)} %get-tuple-element.254), channel_id=1, source_target_pairs={{0,6},{1,7},{2,4},{3,5},{4,2},{5,3},{6,0},{7,1},{8,14},{9,15},{10,... | collective-permute-start | bytes 442376 | tf_op jit(solution)/shard_map/ppermute | solution.py:873
  475.6 19.2 %collective-permute-start.36 = (bf16[640,512]{1,0:T(8,128)(2,1)S(1)}, bf16[640,512]{1,0:T(8,128)(2,1)S(1)}, u32[]{:S(2)}, u32[]{:S(2)}) collective-permute-start(bf16[640,512]{1,0:T(8,128)(2,1)S(1)} %pad_maximum_fusion.3), channel_id=1, source_target_pairs={{0,16},{8,24},{16,0},{24,8},{1,17},{9,25},{17,1},{25,9},{2,18},{10... | collective-permute-start | bytes 1966088 | tf_op jit(solution)/shard_map/ppermute | solution.py:852
  495.0 23.8 %collective-permute-start.38 = (bf16[640,512]{1,0:T(8,128)(2,1)S(1)}, bf16[640,512]{1,0:T(8,128)(2,1)}, u32[]{:S(2)}, u32[]{:S(2)}) collective-permute-start(bf16[640,512]{1,0:T(8,128)(2,1)S(1)} %add_convert_fusion.2), channel_id=1, source_target_pairs={{0,8},{8,0},{16,24},{24,16},{1,9},{9,1},{17,25},{25,17},{2,10},{10... | collective-permute-start | bytes 1966088 | tf_op jit(solution)/shard_map/ppermute | solution.py:852
  496.8 22.1 %collective-permute-start.37 = (bf16[640,512]{1,0:T(8,128)(2,1)S(1)}, bf16[640,512]{1,0:T(8,128)(2,1)S(1)}, u32[]{:S(2)}, u32[]{:S(2)}) collective-permute-start(bf16[640,512]{1,0:T(8,128)(2,1)S(1)} %add_convert_fusion.3), channel_id=1, source_target_pairs={{0,16},{8,24},{16,0},{24,8},{1,17},{9,25},{17,1},{25,9},{2,18},{10... | collective-permute-start | bytes 1966088 | tf_op jit(solution)/shard_map/ppermute | solution.py:852
  498.0 20.2 %all-to-all-start.9 = ((f32[32,8,128]{2,1,0:T(8,128)}), f32[32,8,128]{2,1,0:T(8,128)S(1)}, u32[]{:S(2)}, u32[]{:S(2)}) async-start(f32[32,8,128]{2,1,0:T(8,128)} %broadcast_in_dim.97), calls=%async_computation.11 | async-start | bytes 262144 | tf_op jit(solution)/shard_map/all_to_all | solution.py:834
  502.8 81.1 %reduce-scatter.11.cloned.1.call-start = ((), (), s32[]{:S(2)}) async-start(), calls=%async_computation.20 | async-start | bytes 2359296 | tf_op jit(solution)/shard_map/reduce_scatter | solution.py:1083
  526.9 16.5 %collective-permute-start.40 = (bf16[4,576,128]{2,1,0:T(8,128)(2,1)}, bf16[4,576,128]{2,1,0:T(8,128)(2,1)}, u32[]{:S(2)}, u32[]{:S(2)}) collective-permute-start(bf16[4,576,128]{2,1,0:T(8,128)(2,1)} %get-tuple-element.204), channel_id=1, source_target_pairs={{0,8},{8,0},{16,24},{24,16},{1,9},{9,1},{17,25},{25,17},{2,10},{10... | collective-permute-start | bytes 1769480 | tf_op jit(solution)/shard_map/ppermute | solution.py:873
  528.7 16.5 %collective-permute-start.41 = (bf16[4,576,128]{2,1,0:T(8,128)(2,1)}, bf16[4,576,128]{2,1,0:T(8,128)(2,1)}, u32[]{:S(2)}, u32[]{:S(2)}) collective-permute-start(bf16[4,576,128]{2,1,0:T(8,128)(2,1)} %get-tuple-element.205), channel_id=1, source_target_pairs={{0,16},{8,24},{16,0},{24,8},{1,17},{9,25},{17,1},{25,9},{2,18},{10... | collective-permute-start | bytes 1769480 | tf_op jit(solution)/shard_map/ppermute | solution.py:873
  531.3 14.3 %collective-permute-start.42 = (bf16[128,512]{1,0:T(8,128)(2,1)S(1)}, bf16[128,512]{1,0:T(8,128)(2,1)}, u32[]{:S(2)}, u32[]{:S(2)}) collective-permute-start(bf16[128,512]{1,0:T(8,128)(2,1)S(1)} %slice.325), channel_id=1, source_target_pairs={{0,8},{8,0},{16,24},{24,16},{1,9},{9,1},{17,25},{25,17},{2,10},{10... | collective-permute-start | bytes 393224 | tf_op jit(solution)/shard_map/ppermute | solution.py:852
  532.0 14.8 %collective-permute-start.43 = (bf16[128,512]{1,0:T(8,128)(2,1)S(1)}, bf16[128,512]{1,0:T(8,128)(2,1)S(1)}, u32[]{:S(2)}, u32[]{:S(2)}) collective-permute-start(bf16[128,512]{1,0:T(8,128)(2,1)S(1)} %slice.327), channel_id=1, source_target_pairs={{0,16},{8,24},{16,0},{24,8},{1,17},{9,25},{17,1},{25,9},{2,18},{10... | collective-permute-start | bytes 393224 | tf_op jit(solution)/shard_map/ppermute | solution.py:852
  551.6 21.4 %collective-permute-start.44 = (bf16[4,576,128]{2,1,0:T(8,128)(2,1)S(1)}, bf16[4,576,128]{2,1,0:T(8,128)(2,1)S(1)}, u32[]{:S(2)}, u32[]{:S(2)}) collective-permute-start(bf16[4,576,128]{2,1,0:T(8,128)(2,1)S(1)} %get-tuple-element.214), channel_id=1, source_target_pairs={{0,24},{8,16},{16,8},{24,0},{1,25},{9,17},{17,9},{25,1},{2,26},{10... | collective-permute-start | bytes 1769480 | tf_op jit(solution)/shard_map/ppermute | solution.py:873
  554.0 26.9 %collective-permute-start.52 = (bf16[128,512]{1,0:T(8,128)(2,1)S(1)}, bf16[128,512]{1,0:T(8,128)(2,1)S(1)}, u32[]{:S(2)}, u32[]{:S(2)}) collective-permute-start(bf16[128,512]{1,0:T(8,128)(2,1)S(1)} %add_convert_fusion.16), channel_id=1, source_target_pairs={{0,16},{8,24},{16,0},{24,8},{1,17},{9,25},{17,1},{25,9},{2,18},{10... | collective-permute-start | bytes 393224 | tf_op jit(solution)/shard_map/ppermute | solution.py:852
  554.4 33.0 %collective-permute-start.53 = (bf16[128,512]{1,0:T(8,128)(2,1)S(1)}, bf16[128,512]{1,0:T(8,128)(2,1)}, u32[]{:S(2)}, u32[]{:S(2)}) collective-permute-start(bf16[128,512]{1,0:T(8,128)(2,1)S(1)} %add_convert_fusion.14), channel_id=1, source_target_pairs={{0,8},{8,0},{16,24},{24,16},{1,9},{9,1},{17,25},{25,17},{2,10},{10... | collective-permute-start | bytes 393224 | tf_op jit(solution)/shard_map/ppermute | solution.py:852
  575.3 15.6 %collective-permute-start.45 = (bf16[576,128]{1,0:T(8,128)(2,1)}, bf16[576,128]{1,0:T(8,128)(2,1)}, u32[]{:S(2)}, u32[]{:S(2)}) collective-permute-start(bf16[576,128]{1,0:T(8,128)(2,1)} %get-tuple-element.253), channel_id=1, source_target_pairs={{0,2},{1,3},{2,0},{3,1},{4,6},{5,7},{6,4},{7,5},{8,10},{9,11},{10,... | collective-permute-start | bytes 442376 | tf_op jit(solution)/shard_map/ppermute | solution.py:873
  576.8 14.2 %collective-permute-start.46 = (bf16[576,128]{1,0:T(8,128)(2,1)}, bf16[576,128]{1,0:T(8,128)(2,1)}, u32[]{:S(2)}, u32[]{:S(2)}) collective-permute-start(bf16[576,128]{1,0:T(8,128)(2,1)} %get-tuple-element.252), channel_id=1, source_target_pairs={{0,4},{1,5},{2,6},{3,7},{4,0},{5,1},{6,2},{7,3},{8,12},{9,13},{10,... | collective-permute-start | bytes 442376 | tf_op jit(solution)/shard_map/ppermute | solution.py:873
  579.2 11.8 %collective-permute-start.47 = (bf16[576,128]{1,0:T(8,128)(2,1)}, bf16[576,128]{1,0:T(8,128)(2,1)}, u32[]{:S(2)}, u32[]{:S(2)}) collective-permute-start(bf16[576,128]{1,0:T(8,128)(2,1)} %get-tuple-element.251), channel_id=1, source_target_pairs={{0,6},{1,7},{2,4},{3,5},{4,2},{5,3},{6,0},{7,1},{8,14},{9,15},{10,... | collective-permute-start | bytes 442376 | tf_op jit(solution)/shard_map/ppermute | solution.py:873
  600.8 20.6 %all-to-all-start.10 = ((bf16[4,2,576,128]{3,2,1,0:T(8,128)(2,1)}), bf16[4,2,576,128]{3,2,1,0:T(8,128)(2,1)}, u32[]{:S(2)}, u32[]{:S(2)}) async-start(bf16[4,2,576,128]{3,2,1,0:T(8,128)(2,1)} %broadcast_in_dim.98), calls=%async_computation.14 | async-start | bytes 2359296 | tf_op jit(solution)/shard_map/all_to_all | solution.py:1104
  607.8 12.4 %collective-permute-start.50 = (bf16[128,512]{1,0:T(8,128)(2,1)S(1)}, bf16[128,512]{1,0:T(8,128)(2,1)S(1)}, u32[]{:S(2)}, u32[]{:S(2)}) collective-permute-start(bf16[128,512]{1,0:T(8,128)(2,1)S(1)} %get-tuple-element.263), channel_id=1, source_target_pairs={{0,16},{8,24},{16,0},{24,8},{1,17},{9,25},{17,1},{25,9},{2,18},{10... | collective-permute-start | bytes 393224 | tf_op jit(solution)/shard_map/ppermute | solution.py:852
  (64 other events, 448.2 us)
Sparse Core Ops, SparseCore 0:
  10.2 40.6 all-gather.16
  52.5 29.2 all-gather.18
  83.9 28.5 all-gather.20
  114.6 52.5 all-gather.22
  168.6 27.8 all-gather.24
  198.5 63.7 all-gather.12
  270.4 23.9 all-gather.14
  336.5 37.4 reduce-scatter.6
  421.4 33.2 reduce-scatter.4
  473.6 37.8 reduce-scatter.8
  547.0 36.8 reduce-scatter.10
